TPU v7x, 32 devices: a whole 2x2x4 slice. The times are simulated.
32 devices in a mesh: seq: 8 (over z, y), head: 4 (over x, core).
Axes of the slice: x: 2, y: 2, z: 4, core: 2. Of those that a mesh axis runs over, the one named last changes fastest.
Arguments:
- queries: bfloat16 [8192, 512], P('seq', 'head'), may hold values from -6 to 6
- keys: bfloat16 [8192, 512], P('seq', 'head'), may hold values from -6 to 6
- values: bfloat16 [8192, 512], P('seq', 'head'), may hold values from -6 to 6
- outputs: bfloat16 [8192, 512], P('seq', 'head'), may hold values from -6 to 6
- d_outputs: bfloat16 [8192, 512], P('seq', 'head'), may hold values from -6 to 6
- log_norm: float32 [8, 8192], P('head', 'seq'), may hold values from 4 to 5.5
- rand_owner: int32 [64, 3], P('seq'), may hold values from 0 to 7, all different within a row; in each aligned block of 8 rows (0 to 7, 8 to 15, ...) at most 3 rows name the same one
- rand_local: int32 [64, 3], P('seq'), may hold values from 0 to 7
- glob_blocks: int32 [2], replicated, may hold values from 0 to 63
Outputs:
- d_queries: bfloat16 [8192, 512], P('seq', 'head')
- d_keys: bfloat16 [8192, 512], P('seq', 'head')
- d_values: bfloat16 [8192, 512], P('seq', 'head')
Inputs may be any that keep to these rules, and one draw needn't show every extreme that they name: `rand_owner`: each row names 3 different seq indices; within the 8 rows of one seq index no value is named more than 3 times, a bound that some block reaches.
All inputs are finite; a program needn't handle non-finite values.
Results may differ from a plain program's by a relative error of at most 0.0085.
Values may be sent and summed in bfloat16 or wider, within the bound.
No kernel may reach another device: no remote copies, remote signals or barrier semaphores. Data moves between devices by JAX's collectives and lax.ppermute only.
A program may use at most 128 MiB of HBM per device.

v0:
```python
import math

import jax
import jax.numpy as jnp
from jax import lax
from jax.sharding import PartitionSpec as P

BLOCK = 128


def extended(array, sides, width):
    for axis, dim in sides:
        size, length = (lax.axis_size(axis), array.shape[dim])
        up = [(i, (i + 1) % size) for i in range(size - 1)]
        down = [(j, i) for i, j in up]
        last = lax.slice_in_dim(array, length - width, length, axis=dim)
        leading = lax.slice_in_dim(array, 0, width, axis=dim)
        before = lax.ppermute(last, axis, up)
        after = lax.ppermute(leading, axis, down)
        array = jnp.concatenate([before, array, after], axis=dim)
    return array


def pair_terms(query_rows, grad_rows, norm_rows, delta_rows, key_rows, value_rows, factor):
    scores = (
        jnp.einsum("nqhd,nkhd->nhqk", query_rows, key_rows, preferred_element_type=jnp.float32)
        * factor
    )
    weights = jnp.exp(scores - norm_rows[..., None])
    grad_weights = jnp.einsum(
        "nqhd,nkhd->nhqk", grad_rows, value_rows, preferred_element_type=jnp.float32
    )
    grad_scores = weights * (grad_weights - delta_rows[..., None])
    weights_low = weights.astype(jnp.bfloat16)
    scores_low = grad_scores.astype(jnp.bfloat16)
    grad_query = (
        jnp.einsum("nhqk,nkhd->nqhd", scores_low, key_rows, preferred_element_type=jnp.float32)
        * factor
    )
    grad_key = (
        jnp.einsum("nhqk,nqhd->nkhd", scores_low, query_rows, preferred_element_type=jnp.float32)
        * factor
    )
    grad_value = jnp.einsum(
        "nhqk,nqhd->nkhd", weights_low, grad_rows, preferred_element_type=jnp.float32
    )
    return (grad_query, grad_key, grad_value)


def add_by_block(targets, block_ids, blocks):
    selector = (block_ids[:, None] == jnp.arange(blocks, dtype=jnp.int32)[None, :]).astype(
        jnp.bfloat16
    )
    flat_terms = targets.reshape(targets.shape[0], -1)
    high_part = flat_terms.astype(jnp.bfloat16)
    low_part = (flat_terms - high_part.astype(jnp.float32)).astype(jnp.bfloat16)
    summed = jnp.einsum("sn,sf->nf", selector, high_part, preferred_element_type=jnp.float32)
    summed = summed + jnp.einsum(
        "sn,sf->nf", selector, low_part, preferred_element_type=jnp.float32
    )
    return summed.reshape((blocks,) + targets.shape[1:])


def shards(
    queries, keys, values, outputs, d_outputs, log_norm, rand_owner, rand_local, glob_blocks
):
    tokens_here, features = queries.shape
    heads_here = log_norm.shape[0]
    head_size = features // heads_here
    blocks = tokens_here // BLOCK
    per_block = rand_owner.shape[1]
    factor = 1.0 / math.sqrt(head_size)
    owners = lax.axis_size("seq")
    seq_index = lax.axis_index("seq")
    block_shape = (blocks, BLOCK, heads_here, head_size)
    query_blocks = queries.reshape(block_shape)
    grad_blocks = d_outputs.reshape(block_shape)
    split_out = outputs.reshape(tokens_here, heads_here, head_size).astype(jnp.float32)
    split_grad = d_outputs.reshape(tokens_here, heads_here, head_size).astype(jnp.float32)
    delta_flat = jnp.sum(split_out * split_grad, axis=-1).T
    delta_blocks = delta_flat.reshape(heads_here, blocks, BLOCK).transpose(1, 0, 2)
    norm_blocks = log_norm.reshape(heads_here, blocks, BLOCK).transpose(1, 0, 2)
    d_queries = jnp.zeros(block_shape, jnp.float32)
    pad_shape = (blocks + 2,) + block_shape[1:]
    keys_grad_pad = jnp.zeros(pad_shape, jnp.float32)
    values_grad_pad = jnp.zeros(pad_shape, jnp.float32)
    padded = extended(jnp.stack([keys, values]), (("seq", 1),), BLOCK)
    keys_pad = padded[0].reshape(pad_shape)
    values_pad = padded[1].reshape(pad_shape)
    for offset in range(3):
        grad_query, grad_key, grad_value = pair_terms(
            query_blocks,
            grad_blocks,
            norm_blocks,
            delta_blocks,
            keys_pad[offset : offset + blocks],
            values_pad[offset : offset + blocks],
            factor,
        )
        d_queries = d_queries + grad_query
        keys_grad_pad = keys_grad_pad.at[offset : offset + blocks].add(grad_key)
        values_grad_pad = values_grad_pad.at[offset : offset + blocks].add(grad_value)
    outgoing_edges = jnp.stack(
        [
            jnp.concatenate([keys_grad_pad[0], keys_grad_pad[blocks + 1]], axis=0).reshape(
                2 * BLOCK, features
            ),
            jnp.concatenate([values_grad_pad[0], values_grad_pad[blocks + 1]], axis=0).reshape(
                2 * BLOCK, features
            ),
        ]
    )
    arrived = extended(outgoing_edges.astype(jnp.bfloat16), (("seq", 1),), BLOCK).astype(
        outgoing_edges.dtype
    )
    from_before = arrived[:, :BLOCK].reshape((2,) + block_shape[1:])
    from_after = arrived[:, 3 * BLOCK :].reshape((2,) + block_shape[1:])
    d_keys = (
        keys_grad_pad[1 : blocks + 1].at[0].add(from_before[0]).at[blocks - 1].add(from_after[0])
    )
    d_values = (
        values_grad_pad[1 : blocks + 1].at[0].add(from_before[1]).at[blocks - 1].add(from_after[1])
    )
    global_owner = glob_blocks // blocks
    global_local = glob_blocks % blocks
    owned_here = (global_owner == seq_index).astype(jnp.float32)
    key_table = keys.reshape(blocks, BLOCK, features)
    value_table = values.reshape(blocks, BLOCK, features)
    own_part = jnp.stack([key_table[global_local], value_table[global_local]], axis=1).astype(
        jnp.float32
    )
    own_part = own_part * owned_here[:, None, None, None]
    shared = lax.psum(own_part, "seq").astype(jnp.bfloat16)
    global_pieces = []
    for number in range(shared.shape[0]):
        key_rows = jnp.broadcast_to(shared[number, 0].reshape(block_shape[1:]), block_shape)
        value_rows = jnp.broadcast_to(shared[number, 1].reshape(block_shape[1:]), block_shape)
        grad_query, grad_key, grad_value = pair_terms(
            query_blocks, grad_blocks, norm_blocks, delta_blocks, key_rows, value_rows, factor
        )
        d_queries = d_queries + grad_query
        global_pieces.append(
            jnp.stack(
                [
                    jnp.sum(grad_key, axis=0).reshape(BLOCK, features),
                    jnp.sum(grad_value, axis=0).reshape(BLOCK, features),
                ]
            )
        )
    totals = lax.psum(jnp.stack(global_pieces), "seq")
    for number in range(shared.shape[0]):
        d_keys = d_keys.at[global_local[number]].add(
            owned_here[number] * totals[number, 0].reshape(block_shape[1:])
        )
        d_values = d_values.at[global_local[number]].add(
            owned_here[number] * totals[number, 1].reshape(block_shape[1:])
        )
    references = blocks * per_block
    capacity = max(2, (references + owners - 1) // owners)
    owner_flat = rand_owner.reshape(-1)
    local_flat = rand_local.reshape(-1)
    matches = (owner_flat[:, None] == jnp.arange(owners, dtype=jnp.int32)[None, :]).astype(
        jnp.int32
    )
    within = jnp.sum((jnp.cumsum(matches, axis=0) - 1) * matches, axis=1)
    slot_index = owner_flat * capacity + within
    requested = jnp.zeros((owners * capacity,), jnp.int32).at[slot_index].set(local_flat)
    wanted = lax.all_to_all(
        requested.reshape(owners, capacity), "seq", split_axis=0, concat_axis=0, tiled=True
    )
    wanted_flat = wanted.reshape(-1)
    outgoing = jnp.stack([key_table[wanted_flat], value_table[wanted_flat]], axis=1)
    fetched = lax.all_to_all(
        outgoing.reshape(owners, capacity, 2, BLOCK, features),
        "seq",
        split_axis=0,
        concat_axis=0,
        tiled=True,
    )
    picked = fetched.reshape(owners * capacity, 2, BLOCK, features)[slot_index]
    picked = picked.reshape((blocks, per_block, 2) + block_shape[1:])
    pieces = []
    for column in range(per_block):
        grad_query, grad_key, grad_value = pair_terms(
            query_blocks,
            grad_blocks,
            norm_blocks,
            delta_blocks,
            picked[:, column, 0],
            picked[:, column, 1],
            factor,
        )
        d_queries = d_queries + grad_query
        pieces.append(jnp.stack([grad_key, grad_value], axis=1))
    partials = jnp.stack(pieces, axis=1).reshape(references, 2, BLOCK, features)
    returned = (
        jnp.zeros((owners * capacity, 2, BLOCK, features), jnp.float32).at[slot_index].set(partials)
    )
    received = lax.all_to_all(
        returned.reshape(owners, capacity, 2, BLOCK, features).astype(jnp.bfloat16),
        "seq",
        split_axis=0,
        concat_axis=0,
        tiled=True,
    ).astype(jnp.float32)
    summed = add_by_block(
        received.reshape(owners * capacity, 2, BLOCK, features), wanted_flat, blocks
    )
    d_keys = d_keys + summed[:, 0].reshape(block_shape)
    d_values = d_values + summed[:, 1].reshape(block_shape)
    return (
        d_queries.reshape(tokens_here, features).astype(jnp.bfloat16),
        d_keys.reshape(tokens_here, features).astype(jnp.bfloat16),
        d_values.reshape(tokens_here, features).astype(jnp.bfloat16),
    )


def solution(mesh):
    placed = (
        P("seq", "head"),
        P("seq", "head"),
        P("seq", "head"),
        P("seq", "head"),
        P("seq", "head"),
        P("head", "seq"),
        P("seq", None),
        P("seq", None),
        P(),
    )
    return jax.shard_map(
        shards,
        mesh=mesh,
        in_specs=placed,
        out_specs=(P("seq", "head"), P("seq", "head"), P("seq", "head")),
        check_vma=False,
    )
```

profile of v0, /device:TPU:0, one launch (start us, length us, event | category | flops | bytes accessed | tf_op | source)
XLA Modules:
  0.0 203.8 jit_solution(1023449087053819751)
XLA Ops:
  7.2 0.8 copy.251
  11.4 7.3 %all-to-all-start = ((s32[8,1,3]{2,1,0:T(1,128)}), s32[8,1,3]{2,1,0:T(1,128)}, u32[]{:S(2)}, u32[]{:S(2)}) async-start(s32[8,1,3]{2,1,0:T(1,128)} %bitcast.23), calls=%async_computation | async-start | bytes 8192 | tf_op jit(solution)/shard_map/all_to_all | solution.py:168
  18.7 1.5 pad_maximum_fusion.10
  20.2 4.5 %collective-permute-start = (bf16[2,128,128]{2,1,0:T(8,128)(2,1)}, bf16[2,128,128]{2,1,0:T(8,128)(2,1)}, u32[]{:S(2)}, u32[]{:S(2)}) collective-permute-start(bf16[2,128,128]{2,1,0:T(8,128)(2,1)} %get-tuple-element.192), channel_id=1, source_target_pairs={{0,4},{4,8},{8,12},{12,16},{16,20},{20,24},{24,28},{1,5},{5,9},{9,... | collective-permute-start | bytes 196616 | tf_op jit(solution)/shard_map/ppermute | solution.py:18
  24.7 1.3 collective-permute-start.1
  26.0 1.2 reshape.748
  30.0 41.2 %all-reduce.6 = bf16[2,2,128,128]{3,2,0,1:T(8,128)(2,1)S(1)} all-reduce(f32[2,2,128,128]{3,2,0,1:T(8,128)S(1)} %convert_multiply_fusion.1), channel_id=1, replica_groups=mesh['seq'=8,'head'=4] {'seq'}, use_global_device_ids=true, to_apply=%region_1.0 | all-reduce | flops 65536 | bytes 393216 | tf_op jit(solution)/shard_map/psum | solution.py:133
  75.8 1.1 reshape.742
  80.7 1.1 convolution_bitcast_fusion.10
  81.8 1.1 convolution_bitcast_fusion.9
  84.5 1.3 convolution_bitcast_fusion.12
  89.0 1.3 reduce.49
  91.1 1.6 gather_fusion.3
  92.7 2.5 %pad_maximum_fusion.1 = bf16[8,3,2,128,128]{4,3,1,2,0:T(8,128)(2,1)} fusion(bf16[8,3,1,128,128]{4,3,1,2,0:T(8,128)(2,1)} %bitcast.295, bf16[8,3,1,128,128]{4,3,1,2,0:T(8,128)(2,1)S(1)} %bitcast.294), kind=kLoop, calls=%fused_computation.10 | loop fusion | flops 786432 | bytes 3145728 | tf_op jit(solution)/shard_map/stack | solution.py:172
  95.2 4.3 %all-to-all-start.1 = ((bf16[8,3,2,128,128]{4,3,1,2,0:T(8,128)(2,1)}), bf16[8,3,2,128,128]{4,3,1,2,0:T(8,128)(2,1)}, u32[]{:S(2)}, u32[]{:S(2)}) async-start(bf16[8,3,2,128,128]{4,3,1,2,0:T(8,128)(2,1)} %pad_maximum_fusion.1), calls=%async_computation.1 | async-start | bytes 3145728 | tf_op jit(solution)/shard_map/all_to_all | solution.py:173
  99.5 1.3 eq.44
  100.8 1.7 pad_maximum_fusion.5
  103.5 1.2 reshape.741
  106.5 2.0 reshape.750
  108.5 1.9 copy.241
  110.4 2.0 reshape.743
  112.4 1.4 fusion.19
  116.1 3.8 %collective-permute-start.2 = (bf16[2,128,128]{1,2,0:T(8,128)(2,1)S(1)}, bf16[2,128,128]{1,2,0:T(8,128)(2,1)S(1)}, u32[]{:S(2)}, u32[]{:S(2)}) collective-permute-start(bf16[2,128,128]{1,2,0:T(8,128)(2,1)S(1)} %get-tuple-element.201), channel_id=1, source_target_pairs={{0,4},{4,8},{8,12},{12,16},{16,20},{20,24},{24,28},{1,5},{5,9},{9,... | collective-permute-start | bytes 196616 | tf_op jit(solution)/shard_map/ppermute | solution.py:18
  119.9 1.5 collective-permute-start.3
  121.4 1.1 convolution_bitcast_fusion.11
  122.6 0.8 slice.615
  123.4 2.7 %collective-permute-done.3 = bf16[2,128,128]{1,2,0:T(8,128)(2,1)S(1)} collective-permute-done((bf16[2,128,128]{1,2,0:T(8,128)(2,1)S(1)}, bf16[2,128,128]{1,2,0:T(8,128)(2,1)S(1)}, u32[]{:S(2)}, u32[]{:S(2)}) %collective-permute-start.3) | collective-permute-done | bytes 65568 | tf_op jit(solution)/shard_map/ppermute | solution.py:19
  127.6 3.9 %all-to-all-done.1 = bf16[8,3,2,128,128]{4,3,1,2,0:T(8,128)(2,1)} async-done(((bf16[8,3,2,128,128]{4,3,1,2,0:T(8,128)(2,1)}), bf16[8,3,2,128,128]{4,3,1,2,0:T(8,128)(2,1)}, u32[]{:S(2)}, u32[]{:S(2)}) %all-to-all-start.1) | async-done | bytes 1572896 | tf_op jit(solution)/shard_map/all_to_all | solution.py:173
  131.5 1.5 copy.256
  133.0 2.1 %gather_fusion.4 = bf16[24,2,128,128]{3,2,1,0:T(8,128)(2,1)} fusion(bf16[24,2,128,128]{3,2,1,0:T(8,128)(2,1)S(1)} %bitcast.292, s32[1024]{0:T(1024)} %pad_clamp_fusion), kind=kCustom, calls=%fused_computation.4 | custom fusion | bytes 3145824 | tf_op jit(solution)/shard_map/gather | solution.py:180
  135.1 1.9 copy.257
  142.9 2.3 %copy.290 = f32[24,2,128,128]{3,2,1,0:T(8,128)} copy(f32[24,2,128,128]{2,3,1,0:T(8,128)S(1)} %bitcast.273) | data formatting | bytes 6291456 | tf_op jit(solution)/shard_map/reshape | solution.py:195
  145.9 4.5 %scatter_fusion = f32[24,2,128,128]{3,2,1,0:T(8,128)S(1)} fusion(f32[24,2,128,128]{3,2,1,0:T(8,128)S(1)} %broadcast_in_dim.17, s32[24]{0:T(128)S(1)} %copy-done.42, f32[24,2,128,128]{3,2,1,0:T(8,128)} %copy.290), kind=kCustom, calls=%fused_computation.6 | custom fusion | bytes 9437280 | tf_op jit(solution)/shard_map/scatter | solution.py:197
  150.4 1.5 convert_element_type.120
  151.9 5.0 %all-to-all-start.2 = ((bf16[8,3,2,128,128]{4,3,2,1,0:T(8,128)(2,1)}), bf16[8,3,2,128,128]{4,3,2,1,0:T(8,128)(2,1)S(1)}, u32[]{:S(2)}, u32[]{:S(2)}) async-start(bf16[8,3,2,128,128]{4,3,2,1,0:T(8,128)(2,1)} %bitcast.291), calls=%async_computation.2 | async-start | bytes 3145728 | tf_op jit(solution)/shard_map/all_to_all | solution.py:199
  156.9 0.9 maximum_convert_fusion.2
  157.8 1.5 fusion.80
  159.3 1.5 fusion.83
  160.8 1.5 fusion.82
  162.3 2.3 %slice_multiply_fusion = (f32[1,1,128,128]{2,3,1,0:T(8,128)S(1)}, f32[1,1,128,128]{2,3,1,0:T(8,128)S(1)}, f32[1,1,128,128]{2,3,1,0:T(8,128)S(1)}, f32[1,1,128,128]{2,3,1,0:T(8,128)S(1)}) fusion(f32[2,2,128,128]{2,3,1,0:T(8,128)} %all-reduce.5.cloned.1.call-done, f32[]{:T(128)} %bitcast.72, f32[]{:T(128)} %bitcast.54), kind=kLoop, calls=%fused_computation.157 | loop fusion | flops 65536 | bytes 524296 | tf_op jit(solution)/shard_map/mul | solution.py:156
  164.6 2.2 %fusion.76 = (f32[8,128,2,64]{1,3,2,0:T(8,128)}, f32[8,128,2,64]{1,3,2,0:T(8,128)}) fusion(f32[8,128,2,64]{1,3,2,0:T(8,128)} %fusion.82, s32[]{:T(128)} %select_n.56, f32[1,128,2,64]{1,3,2,0:T(8,128)S(1)} %bitcast.332, pred[]{:T(512)} %get-tuple-element.181, f32[8,128,2,64]{1,3,2,0:T(8,128)} %fusion.80, f32[1,128,2,64]{1,3,2,0:T(8,128)S(1)} %bitcast.331), kind=kLoop, calls=%fused_computation.153 | loop fusion | flops 65536 | bytes 394240 | tf_op jit(solution)/shard_map/scatter-add | solution.py:152
  166.9 2.1 %fusion.79 = f32[8,128,2,64]{1,3,2,0:T(8,128)} fusion(f32[8,128,2,64]{1,3,2,0:T(8,128)} %get-tuple-element.212, s32[]{:T(128)} %select_n.58, f32[1,128,2,64]{1,3,2,0:T(8,128)S(1)} %bitcast.330, pred[]{:T(512)} %get-tuple-element.180), kind=kLoop, calls=%fused_computation.156 | loop fusion | flops 32768 | bytes 197632 | tf_op jit(solution)/shard_map/scatter-add | solution.py:155
  169.0 2.1 %fusion.77 = f32[8,128,2,64]{1,3,2,0:T(8,128)} fusion(f32[8,128,2,64]{1,3,2,0:T(8,128)} %get-tuple-element.211, s32[]{:T(128)} %select_n.58, f32[1,128,2,64]{1,3,2,0:T(8,128)S(1)} %bitcast.329, pred[]{:T(512)} %get-tuple-element.180), kind=kLoop, calls=%fused_computation.154 | loop fusion | flops 32768 | bytes 197632 | tf_op jit(solution)/shard_map/scatter-add | solution.py:152
  171.1 1.3 convolution_bitcast_fusion.8
  174.8 1.0 reshape.744
  175.8 15.1 %all-to-all-done.2 = bf16[8,3,2,128,128]{4,3,2,1,0:T(8,128)(2,1)S(1)} async-done(((bf16[8,3,2,128,128]{4,3,2,1,0:T(8,128)(2,1)}), bf16[8,3,2,128,128]{4,3,2,1,0:T(8,128)(2,1)S(1)}, u32[]{:S(2)}, u32[]{:S(2)}) %all-to-all-start.2) | async-done | bytes 1572896 | tf_op jit(solution)/shard_map/all_to_all | solution.py:199
  194.3 1.0 reshape.746
  196.0 1.0 reshape.745
  (208 shorter events, 35.4 us)
Async XLA Ops:
  7.2 20.5 %copy-start.35 = (bf16[1024,128]{1,0:T(8,128)(2,1)S(1)}, bf16[1024,128]{1,0:T(8,128)(2,1)}, u32[]{:S(2)}) copy-start(bf16[1024,128]{1,0:T(8,128)(2,1)} %param.41) | copy-start | bytes 786436
  10.1 16.0 %copy-start.40 = (s32[24]{0:T(128)}, s32[24]{0:T(128)S(1)}, u32[]{:S(2)}) copy-start(s32[24]{0:T(128)S(1)} %fusion.90) | copy-start | bytes 292
  11.4 77.1 %all-to-all-start = ((s32[8,1,3]{2,1,0:T(1,128)}), s32[8,1,3]{2,1,0:T(1,128)}, u32[]{:S(2)}, u32[]{:S(2)}) async-start(s32[8,1,3]{2,1,0:T(1,128)} %bitcast.23), calls=%async_computation | async-start | bytes 8192 | tf_op jit(solution)/shard_map/all_to_all | solution.py:168
  18.7 143.6 %all-reduce.5.cloned.1.call-start = ((), (), s32[]{:S(2)}) async-start(), calls=%async_computation.3 | async-start | bytes 524288 | tf_op jit(solution)/shard_map/psum | solution.py:150
  18.7 9.1 %copy-start.36 = (bf16[1024,128]{1,0:T(8,128)(2,1)S(1)}, bf16[1024,128]{1,0:T(8,128)(2,1)}, u32[]{:S(2)}) copy-start(bf16[1024,128]{1,0:T(8,128)(2,1)} %param.40) | copy-start | bytes 786436
  20.2 80.5 %collective-permute-start = (bf16[2,128,128]{2,1,0:T(8,128)(2,1)}, bf16[2,128,128]{2,1,0:T(8,128)(2,1)}, u32[]{:S(2)}, u32[]{:S(2)}) collective-permute-start(bf16[2,128,128]{2,1,0:T(8,128)(2,1)} %get-tuple-element.192), channel_id=1, source_target_pairs={{0,4},{4,8},{8,12},{12,16},{16,20},{20,24},{24,28},{1,5},{5,9},{9,... | collective-permute-start | bytes 196616 | tf_op jit(solution)/shard_map/ppermute | solution.py:18
  24.7 76.1 %collective-permute-start.1 = (bf16[2,128,128]{2,1,0:T(8,128)(2,1)}, bf16[2,128,128]{2,1,0:T(8,128)(2,1)}, u32[]{:S(2)}, u32[]{:S(2)}) collective-permute-start(bf16[2,128,128]{2,1,0:T(8,128)(2,1)} %get-tuple-element.193), channel_id=1, source_target_pairs={{4,0},{8,4},{12,8},{16,12},{20,16},{24,20},{28,24},{5,1},{9,5},{13... | collective-permute-start | bytes 196616 | tf_op jit(solution)/shard_map/ppermute | solution.py:19
  27.3 1.5 copy-start.1
  27.3 2.1 %copy-start = (bf16[1024,128]{1,0:T(8,128)(2,1)S(1)}, bf16[1024,128]{1,0:T(8,128)(2,1)}, u32[]{:S(2)}) copy-start(bf16[1024,128]{1,0:T(8,128)(2,1)} %param.39) | copy-start | bytes 786436
  27.8 43.7 %copy-start.24 = (f32[2,1024]{1,0:T(2,128)S(1)}, f32[2,1024]{1,0:T(2,128)}, u32[]{:S(2)}) copy-start(f32[2,1024]{1,0:T(2,128)} %param.42) | copy-start | bytes 24580
  29.9 42.2 %copy-start.37 = (f32[2]{0:T(128)}, f32[2]{0:T(128)S(1)}, u32[]{:S(2)}) copy-start(f32[2]{0:T(128)S(1)} %compare_convert_fusion) | copy-start | bytes 28
  74.7 2.1 %copy-start.38 = (f32[2]{0:T(128)S(1)}, f32[2]{0:T(128)}, u32[]{:S(2)}) copy-start(f32[2]{0:T(128)} %copy-done.37) | copy-start | bytes 28
  74.7 2.7 %copy-start.43 = (s32[2]{0:T(128)S(1)}, s32[2]{0:T(128)}, u32[]{:S(2)}) copy-start(s32[2]{0:T(128)} %get-tuple-element.183) | copy-start | bytes 28
  83.9 3.2 %copy-start.44 = (s32[4]{0:T(128)S(1)}, s32[4]{0:T(128)}, u32[]{:S(2)}) copy-start(s32[4]{0:T(128)} %constant.365.clone.1) | copy-start | bytes 52
  83.9 4.0 %copy-start.41 = (s32[24]{0:T(128)S(1)}, s32[24]{0:T(128)}, u32[]{:S(2)}) copy-start(s32[24]{0:T(128)} %copy-done.40) | copy-start | bytes 292
  84.5 8.2 %copy-start.7 = (bf16[8,2,128,128]{3,2,1,0:T(8,128)(2,1)}, bf16[8,2,128,128]{3,2,1,0:T(8,128)(2,1)S(1)}, u32[]{:S(2)}) copy-start(bf16[8,2,128,128]{3,2,1,0:T(8,128)(2,1)S(1)} %fusion.25) | copy-start | bytes 1572868
  95.2 36.3 %all-to-all-start.1 = ((bf16[8,3,2,128,128]{4,3,1,2,0:T(8,128)(2,1)}), bf16[8,3,2,128,128]{4,3,1,2,0:T(8,128)(2,1)}, u32[]{:S(2)}, u32[]{:S(2)}) async-start(bf16[8,3,2,128,128]{4,3,1,2,0:T(8,128)(2,1)} %pad_maximum_fusion.1), calls=%async_computation.1 | async-start | bytes 3145728 | tf_op jit(solution)/shard_map/all_to_all | solution.py:173
  105.0 1.5 copy-start.5
  105.0 1.2 copy-start.8
  112.4 1.4 copy-start.23
  114.6 11.5 %copy-start.25 = (bf16[1,128,2,64]{1,3,2,0:T(8,128)(2,1)}, bf16[1,128,2,64]{1,3,2,0:T(8,128)(2,1)S(1)}, u32[]{:S(2)}) copy-start(bf16[1,128,2,64]{1,3,2,0:T(8,128)(2,1)S(1)} %slice.675) | copy-start | bytes 98308
  114.6 7.9 %copy-start.4 = (f32[10,128,2,64]{1,3,2,0:T(8,128)}, f32[10,128,2,64]{1,3,2,0:T(8,128)S(1)}, u32[]{:S(2)}) copy-start(f32[10,128,2,64]{1,3,2,0:T(8,128)S(1)} %constant_dynamic-update-slice_fusion.1) | copy-start | bytes 1966084
  114.6 11.4 %copy-start.27 = (bf16[1,128,2,64]{1,3,2,0:T(8,128)(2,1)}, bf16[1,128,2,64]{1,3,2,0:T(8,128)(2,1)S(1)}, u32[]{:S(2)}) copy-start(bf16[1,128,2,64]{1,3,2,0:T(8,128)(2,1)S(1)} %slice.676) | copy-start | bytes 98308
  115.5 5.9 %copy-start.17 = (bf16[8,128,2,64]{1,3,2,0:T(8,128)(2,1)S(1)}, bf16[8,128,2,64]{1,3,2,0:T(8,128)(2,1)}, u32[]{:S(2)}) copy-start(bf16[8,128,2,64]{1,3,2,0:T(8,128)(2,1)} %copy.241) | copy-start | bytes 786436
  115.9 10.1 %copy-start.29 = (bf16[1,128,2,64]{1,3,2,0:T(8,128)(2,1)}, bf16[1,128,2,64]{1,3,2,0:T(8,128)(2,1)S(1)}, u32[]{:S(2)}) copy-start(bf16[1,128,2,64]{1,3,2,0:T(8,128)(2,1)S(1)} %slice.673) | copy-start | bytes 98308
  116.0 10.1 %copy-start.31 = (bf16[1,128,2,64]{1,3,2,0:T(8,128)(2,1)}, bf16[1,128,2,64]{1,3,2,0:T(8,128)(2,1)S(1)}, u32[]{:S(2)}) copy-start(bf16[1,128,2,64]{1,3,2,0:T(8,128)(2,1)S(1)} %slice.674) | copy-start | bytes 98308
  116.1 7.3 %collective-permute-start.2 = (bf16[2,128,128]{1,2,0:T(8,128)(2,1)S(1)}, bf16[2,128,128]{1,2,0:T(8,128)(2,1)S(1)}, u32[]{:S(2)}, u32[]{:S(2)}) collective-permute-start(bf16[2,128,128]{1,2,0:T(8,128)(2,1)S(1)} %get-tuple-element.201), channel_id=1, source_target_pairs={{0,4},{4,8},{8,12},{12,16},{16,20},{20,24},{24,28},{1,5},{5,9},{9,... | collective-permute-start | bytes 196616 | tf_op jit(solution)/shard_map/ppermute | solution.py:18
  119.9 6.2 %collective-permute-start.3 = (bf16[2,128,128]{1,2,0:T(8,128)(2,1)S(1)}, bf16[2,128,128]{1,2,0:T(8,128)(2,1)S(1)}, u32[]{:S(2)}, u32[]{:S(2)}) collective-permute-start(bf16[2,128,128]{1,2,0:T(8,128)(2,1)S(1)} %get-tuple-element.202), channel_id=1, source_target_pairs={{4,0},{8,4},{12,8},{16,12},{20,16},{24,20},{28,24},{5,1},{9,5},{13... | collective-permute-start | bytes 196616 | tf_op jit(solution)/shard_map/ppermute | solution.py:19
  123.4 3.4 %copy-start.33 = (bf16[2,128,128]{1,2,0:T(8,128)(2,1)}, bf16[2,128,128]{1,2,0:T(8,128)(2,1)S(1)}, u32[]{:S(2)}) copy-start(bf16[2,128,128]{1,2,0:T(8,128)(2,1)S(1)} %collective-permute-done.2) | copy-start | bytes 196612
  137.0 2.8 %copy-start.2 = (bf16[24,2,128,128]{2,3,1,0:T(8,128)(2,1)}, bf16[24,2,128,128]{2,3,1,0:T(8,128)(2,1)S(1)}, u32[]{:S(2)}) copy-start(bf16[24,2,128,128]{2,3,1,0:T(8,128)(2,1)S(1)} %copy.257) | copy-start | bytes 4718596
  138.1 3.0 %copy-start.9 = (bf16[8,2,128,128]{3,2,1,0:T(8,128)(2,1)}, bf16[8,2,128,128]{3,2,1,0:T(8,128)(2,1)S(1)}, u32[]{:S(2)}) copy-start(bf16[8,2,128,128]{3,2,1,0:T(8,128)(2,1)S(1)} %fusion.30) | copy-start | bytes 1572868
  139.0 1.7 copy-start.13
  140.2 1.4 copy-start.11
  151.9 5.0 %copy-start.26 = (bf16[1,128,2,64]{1,3,2,0:T(8,128)(2,1)S(1)}, bf16[1,128,2,64]{1,3,2,0:T(8,128)(2,1)}, u32[]{:S(2)}) copy-start(bf16[1,128,2,64]{1,3,2,0:T(8,128)(2,1)} %copy-done.25) | copy-start | bytes 98308
  151.9 5.0 %copy-start.28 = (bf16[1,128,2,64]{1,3,2,0:T(8,128)(2,1)S(1)}, bf16[1,128,2,64]{1,3,2,0:T(8,128)(2,1)}, u32[]{:S(2)}) copy-start(bf16[1,128,2,64]{1,3,2,0:T(8,128)(2,1)} %copy-done.27) | copy-start | bytes 98308
  151.9 5.0 %copy-start.30 = (bf16[1,128,2,64]{1,3,2,0:T(8,128)(2,1)S(1)}, bf16[1,128,2,64]{1,3,2,0:T(8,128)(2,1)}, u32[]{:S(2)}) copy-start(bf16[1,128,2,64]{1,3,2,0:T(8,128)(2,1)} %copy-done.29) | copy-start | bytes 98308
  151.9 5.0 %copy-start.32 = (bf16[1,128,2,64]{1,3,2,0:T(8,128)(2,1)S(1)}, bf16[1,128,2,64]{1,3,2,0:T(8,128)(2,1)}, u32[]{:S(2)}) copy-start(bf16[1,128,2,64]{1,3,2,0:T(8,128)(2,1)} %copy-done.31) | copy-start | bytes 98308
  151.9 39.0 %all-to-all-start.2 = ((bf16[8,3,2,128,128]{4,3,2,1,0:T(8,128)(2,1)}), bf16[8,3,2,128,128]{4,3,2,1,0:T(8,128)(2,1)S(1)}, u32[]{:S(2)}, u32[]{:S(2)}) async-start(bf16[8,3,2,128,128]{4,3,2,1,0:T(8,128)(2,1)} %bitcast.291), calls=%async_computation.2 | async-start | bytes 3145728 | tf_op jit(solution)/shard_map/all_to_all | solution.py:199
  156.9 14.2 %copy-start.3 = (bf16[24,2,128,128]{2,3,1,0:T(8,128)(2,1)S(1)}, bf16[24,2,128,128]{2,3,1,0:T(8,128)(2,1)}, u32[]{:S(2)}) copy-start(bf16[24,2,128,128]{2,3,1,0:T(8,128)(2,1)} %copy-done.2) | copy-start | bytes 4718596
  162.3 10.1 %copy-start.10 = (bf16[8,2,128,128]{3,2,1,0:T(8,128)(2,1)S(1)}, bf16[8,2,128,128]{3,2,1,0:T(8,128)(2,1)}, u32[]{:S(2)}) copy-start(bf16[8,2,128,128]{3,2,1,0:T(8,128)(2,1)} %copy-done.9) | copy-start | bytes 1572868
  166.9 5.9 %copy-start.12 = (bf16[8,2,128,128]{3,2,1,0:T(8,128)(2,1)S(1)}, bf16[8,2,128,128]{3,2,1,0:T(8,128)(2,1)}, u32[]{:S(2)}) copy-start(bf16[8,2,128,128]{3,2,1,0:T(8,128)(2,1)} %copy-done.11) | copy-start | bytes 1572868
  172.5 1.2 copy-start.18
  172.5 1.3 copy-start.19
  172.5 1.5 copy-start.20
  172.5 1.6 copy-start.21
  175.8 15.8 %copy-start.39 = (s32[24]{0:T(128)S(1)}, s32[24]{0:T(128)}, u32[]{:S(2)}) copy-start(s32[24]{0:T(128)} %eq.44) | copy-start | bytes 292
  192.8 1.0 copy-start.16
  193.9 1.6 copy-start.14
  (6 other events, 5.2 us)
Sparse Core Ops, SparseCore 0:
  75.6 77.2 all-reduce.4
where the time goes:
time: 205 us; the launch traced here: 204 us
  local copies, waits for them, and re-layouts  44.7 us (22%)
  blocking collectives  41.2 us (20%)
  other arithmetic  28 us (14%)
  starting transfers between devices  27.7 us (14%)
  waiting for transfers between devices  21.7 us (11%)
  matrix products  21.5 us (10%)
  between operations  19.1 us (9%)
    psum x1, blocking collectives, shards(): shared = lax.psum(own_part, 'seq').astype(jnp.bfloat16)  41.2 us
    all_to_all x1, waiting for transfers between devices, shards(): lax.all_to_all(returned.reshape(owners, capacity, 2, BLOCK, features).ast...  15.1 us
    unnamed x106, local copies, waits for them, and re-layouts  10.4 us
    ppermute x2, starting transfers between devices, extended(): before = lax.ppermute(last, axis, up)  8.29 us
    all_to_all x1, starting transfers between devices, shards(): lax.all_to_all(requested.reshape(owners, capacity), 'seq', split_axis=0,...  7.28 us
    dot_general x8, matrix products, pair_terms(): jnp.einsum('nhqk,nkhd->nqhd', scores_low, key_rows, preferred_element_typ...  6.67 us
    slice x6, local copies, waits for them, and re-layouts, shards(): keys_pad[offset:offset + blocks]  5.05 us
    all_to_all x1, starting transfers between devices, shards(): lax.all_to_all(returned.reshape(owners, capacity, 2, BLOCK, features).ast...  5.01 us
  transfers between devices with their start and end apart: 8, of which 3 were waited for; matrix products, arithmetic and copies ran while one was open for 40% of the time, Pallas kernels for 0%

commit v1 on v0

v1 whole, which is shorter than its diff:
```python
import functools
import math

import jax
import jax.numpy as jnp
from jax import lax
from jax.experimental import pallas as pl
from jax.experimental.pallas import tpu as pltpu
from jax.sharding import PartitionSpec as P

BLOCK = 128
STAT = 8
LOG2E = math.log2(math.e)
NT = (((1,), (1,)), ((), ()))
VMEM = pl.BlockSpec(memory_space=pltpu.VMEM)
SMEM = pl.BlockSpec(memory_space=pltpu.SMEM)
F32 = jnp.float32
BF16 = jnp.bfloat16


def call(body, out_shape, out_specs, in_specs, scratch, flops, moved, name):
    return pl.pallas_call(
        body,
        out_shape=out_shape,
        in_specs=in_specs,
        out_specs=out_specs,
        scratch_shapes=scratch,
        compiler_params=pltpu.CompilerParams(vmem_limit_bytes=48 * 1024 * 1024),
        cost_estimate=pl.CostEstimate(flops=flops, bytes_accessed=moved, transcendentals=0),
        name=name,
    )


def dot(a, b):
    return jnp.dot(a, b, preferred_element_type=F32)


def by_head(rows, heads):
    width = rows.shape[1] // heads
    lane = lax.broadcasted_iota(jnp.int32, (1, rows.shape[1]), 1)
    parts = []
    for h in range(heads):
        keep = ((lane >= h * width) & (lane < (h + 1) * width)).astype(F32).astype(BF16)
        parts.append(rows * keep)
    return jnp.concatenate(parts, axis=0)


def stat_rows(tile, heads):
    half = 2 * heads
    norm = [tile[h : h + 1] + tile[heads + h : heads + h + 1] for h in range(heads)]
    delta = [tile[half + h : half + h + 1] + tile[half + heads + h : half + heads + h + 1] for h in range(heads)]
    return jnp.concatenate(norm, axis=1), jnp.concatenate(delta, axis=1)


def weigh(key_rows, value_rows, q_bd, g_bd, norm, delta):
    scores = lax.dot_general(key_rows, q_bd, NT, preferred_element_type=F32)
    weights = jnp.exp2(scores * LOG2E - norm)
    grad = lax.dot_general(value_rows, g_bd, NT, preferred_element_type=F32)
    return weights.astype(BF16), (weights * (grad - delta)).astype(BF16)


def grad_query_t(keys_t, low, heads):
    width = keys_t.shape[0] // heads
    return jnp.concatenate(
        [dot(keys_t[h * width : (h + 1) * width], low[:, h * BLOCK : (h + 1) * BLOCK]) for h in range(heads)],
        axis=0,
    )


def pack_queries(heads, per_block, capacity, fold, refs):
    (q_ref, g_ref, o_ref, norm_ref, owner_ref, local_ref, scale_q_ref, stats_ref, src_ref) = refs[:9]
    out_refs, (count, source, place) = refs[9:-3], refs[-3:]
    blocks = q_ref.shape[0] // BLOCK
    owners = len(out_refs)
    width = q_ref.shape[1] // heads
    me = lax.axis_index("seq") if fold else 0
    for k in range(owners):
        count[k] = 0
        for s in range(capacity):
            source[k * capacity + s] = -1
    for b in range(blocks):
        for r in range(per_block):
            k = owner_ref[b, r] ^ me
            s = count[k]
            count[k] = s + 1
            source[k * capacity + s] = b
            place[k * capacity + s] = local_ref[b, r]
    for b in range(blocks):
        rows = pl.ds(b * BLOCK, BLOCK)
        prod = (o_ref[rows, :].astype(F32) * g_ref[rows, :].astype(F32)).T
        norm = [norm_ref[h : h + 1, rows] * LOG2E for h in range(heads)]
        delta = [jnp.sum(prod[h * width : (h + 1) * width], axis=0, keepdims=True) for h in range(heads)]
        exact = jnp.concatenate(norm + delta, axis=0)
        high = exact.astype(BF16).astype(F32)
        low = (exact - high).astype(BF16).astype(F32)
        stats_ref[b] = jnp.concatenate(
            [high[:heads], low[:heads], high[heads:], low[heads:]], axis=0
        )
        scale_q_ref[rows, :] = q_ref[rows, :] * jnp.asarray(1.0 / math.sqrt(width), BF16)
    full = blocks * per_block == owners * capacity
    for k in range(owners):
        out = out_refs[k]
        tiles, marks = [], []
        for s in range(capacity):
            b = source[k * capacity + s]
            src_ref[k * capacity + s] = b
            at = pl.ds(pl.multiple_of(jnp.maximum(b, 0) * BLOCK, BLOCK), BLOCK)
            query, grad, tile = scale_q_ref[at, :], g_ref[at, :], stats_ref[jnp.maximum(b, 0)]
            number = place[k * capacity + s]
            if not full:
                query = jnp.where(b >= 0, query, jnp.zeros_like(query))
                grad = jnp.where(b >= 0, grad, jnp.zeros_like(grad))
                tile = jnp.where(b >= 0, tile, jnp.zeros_like(tile))
                number = jnp.where(b >= 0, number, 0)
            out[2 * s * BLOCK : (2 * s + 1) * BLOCK, :] = query
            out[(2 * s + 1) * BLOCK : (2 * s + 2) * BLOCK, :] = grad
            tiles.append(tile)
            marks.append(jnp.full((1, BLOCK), number, jnp.int32).astype(F32))
        extra = out.shape[0] - (2 * BLOCK + STAT) * capacity - capacity
        marks.append(jnp.zeros((extra, BLOCK), F32))
        out[2 * capacity * BLOCK :, :] = jnp.concatenate(tiles + marks, axis=0).astype(BF16)


def pack_keys(head_size, k_ref, v_ref, q_ref, g_ref, stats_ref, glob_ref, up_ref, down_ref, own_ref, kt_ref):
    blocks = k_ref.shape[0] // BLOCK
    me = lax.axis_index("seq")
    for out, b in ((up_ref, blocks - 1), (down_ref, 0)):
        rows = pl.ds(b * BLOCK, BLOCK)
        for number, ref in enumerate((q_ref, g_ref, k_ref, v_ref)):
            out[number * BLOCK : (number + 1) * BLOCK, :] = ref[rows, :]
        out[4 * BLOCK :, :] = jnp.concatenate(
            [stats_ref[b], jnp.zeros((STAT, BLOCK), F32)], axis=0
        ).astype(BF16)
    for number in range(glob_ref.shape[0]):
        block = glob_ref[number]
        mine = block // blocks == me
        at = pl.ds(pl.multiple_of((block % blocks) * BLOCK, BLOCK), BLOCK)
        for turn, ref in enumerate((k_ref, v_ref)):
            first = (turn * glob_ref.shape[0] + number) * BLOCK
            rows = ref[at, :]
            own_ref[first : first + BLOCK, :] = jnp.where(mine, rows, jnp.zeros_like(rows))
    for b in range(blocks):
        rows = pl.ds(b * BLOCK, BLOCK)
        kt_ref[rows, :] = (k_ref[rows, :].astype(F32) * (1.0 / math.sqrt(head_size))).T.astype(BF16)


def window(
    heads, q_ref, g_ref, stats_ref, k_ref, v_ref, kt_ref, before_ref, after_ref, dqt_ref, dk_ref, dv_ref
):
    blocks = q_ref.shape[0] // BLOCK
    head_size = q_ref.shape[1] // heads

    def piece(ref, number):
        return ref[number * BLOCK : (number + 1) * BLOCK, :]

    def edge_t(ref):
        return (piece(ref, 2).astype(F32) * (1.0 / math.sqrt(head_size))).T.astype(BF16)

    def key_side(j):
        if j < 0:
            return piece(before_ref, 2), piece(before_ref, 3), edge_t(before_ref)
        if j == blocks:
            return piece(after_ref, 2), piece(after_ref, 3), edge_t(after_ref)
        return piece(k_ref, j), piece(v_ref, j), piece(kt_ref, j)

    for b in range(-1, blocks + 1):
        inside = 0 <= b < blocks
        if inside:
            query, grad, tile = piece(q_ref, b), piece(g_ref, b), stats_ref[b]
        else:
            ref = before_ref if b < 0 else after_ref
            query, grad, tile = piece(ref, 0), piece(ref, 1), ref[4 * BLOCK :, :].astype(F32)[:STAT]
        q_bd, g_bd = by_head(query, heads), by_head(grad, heads)
        norm, delta = stat_rows(tile, heads)
        near = range(b - 1, b + 2) if inside else [0 if b < 0 else blocks - 1]
        total = None
        for j in near:
            key_rows, value_rows, keys_t = key_side(j)
            weights_low, scores_low = weigh(key_rows, value_rows, q_bd, g_bd, norm, delta)
            if inside:
                term = grad_query_t(keys_t, scores_low, heads)
                total = term if total is None else total + term
            if 0 <= j < blocks:
                rows = pl.ds(j * BLOCK, BLOCK)
                grad_key, grad_value = dot(scores_low, q_bd), dot(weights_low, g_bd)
                if b == j - 1:
                    dk_ref[rows, :] = grad_key
                    dv_ref[rows, :] = grad_value
                else:
                    dk_ref[rows, :] += grad_key
                    dv_ref[rows, :] += grad_value
        if inside:
            dqt_ref[b * BLOCK : (b + 1) * BLOCK, :] = total


def globals_(heads, q_ref, g_ref, stats_ref, shared_ref, before_ref, dqt_ref, part_ref, total_k, total_v):
    blocks = q_ref.shape[0] // BLOCK
    head_size = q_ref.shape[1] // heads
    rows = shared_ref.shape[0] // 2
    key_rows, value_rows = shared_ref[:rows, :], shared_ref[rows:, :]
    keys_t = (key_rows.astype(F32) * (1.0 / math.sqrt(head_size))).T.astype(BF16)
    for b in range(blocks):
        at = pl.ds(b * BLOCK, BLOCK)
        q_bd, g_bd = by_head(q_ref[at, :], heads), by_head(g_ref[at, :], heads)
        norm, delta = stat_rows(stats_ref[b], heads)
        weights_low, scores_low = weigh(key_rows, value_rows, q_bd, g_bd, norm, delta)
        dqt_ref[at, :] = before_ref[at, :] + grad_query_t(keys_t, scores_low, heads)
        grad_key, grad_value = dot(scores_low, q_bd), dot(weights_low, g_bd)
        if b == 0:
            total_k[...] = grad_key
            total_v[...] = grad_value
        else:
            total_k[...] += grad_key
            total_v[...] += grad_value
    part_ref[:rows, :] = total_k[...].astype(BF16)
    part_ref[rows:, :] = total_v[...].astype(BF16)


def randoms(heads, capacity, in_ref, k_ref, v_ref, kt_ref, dk_in, dv_in, ret_ref, dk_ref, dv_ref):
    dk_ref[...] = dk_in[...]
    dv_ref[...] = dv_in[...]

    def partner(n):
        tail = in_ref[n, 2 * capacity * BLOCK :, :].astype(F32)
        for s in range(capacity):
            mark = STAT * capacity + s
            number = jnp.max(tail[mark : mark + 1]).astype(jnp.int32)
            at = pl.ds(pl.multiple_of(number * BLOCK, BLOCK), BLOCK)
            query = in_ref[n, 2 * s * BLOCK : (2 * s + 1) * BLOCK, :]
            grad = in_ref[n, (2 * s + 1) * BLOCK : (2 * s + 2) * BLOCK, :]
            q_bd, g_bd = by_head(query, heads), by_head(grad, heads)
            norm, delta = stat_rows(tail[s * STAT : (s + 1) * STAT], heads)
            weights_low, scores_low = weigh(k_ref[at, :], v_ref[at, :], q_bd, g_bd, norm, delta)
            ret_ref[n, s * BLOCK : (s + 1) * BLOCK, :] = grad_query_t(kt_ref[at, :], scores_low, heads).astype(BF16)
            dk_ref[at, :] += dot(scores_low, q_bd)
            dv_ref[at, :] += dot(weights_low, g_bd)

    if in_ref.shape[0] == 1:
        partner(0)
    else:
        pl.loop(0, in_ref.shape[0])(partner)


def finish_keys(dk_in, dv_in, total_ref, glob_ref, dk_ref, dv_ref, sum_k, sum_v):
    blocks = dk_in.shape[0] // BLOCK
    me = lax.axis_index("seq")
    many = glob_ref.shape[0]
    sum_k[...] = dk_in[...]
    sum_v[...] = dv_in[...]
    for number in range(many):
        block = glob_ref[number]

        @pl.when(block // blocks == me)
        def _():
            at = pl.ds(pl.multiple_of((block % blocks) * BLOCK, BLOCK), BLOCK)
            for turn, ref in enumerate((sum_k, sum_v)):
                first = (turn * many + number) * BLOCK
                ref[at, :] += total_ref[first : first + BLOCK, :].astype(F32)

    dk_ref[...] = sum_k[...].astype(BF16)
    dv_ref[...] = sum_v[...].astype(BF16)


def finish_queries(capacity, refs):
    dqt_ref, src_ref, ret_refs, (out_ref, total) = refs[0], refs[1], refs[2:-2], refs[-2:]
    blocks = dqt_ref.shape[0] // BLOCK
    total[...] = dqt_ref[...]
    at = 0
    for ref in ret_refs:
        for n in range(ref.shape[0]):
            for s in range(capacity):
                b = src_ref[at]
                at += 1

                @pl.when(b >= 0)
                def _():
                    rows = pl.ds(pl.multiple_of(b * BLOCK, BLOCK), BLOCK)
                    total[rows, :] += ref[n, s * BLOCK : (s + 1) * BLOCK, :].astype(F32)

    for b in range(blocks):
        rows = pl.ds(b * BLOCK, BLOCK)
        out_ref[rows, :] = total[rows, :].T.astype(BF16)


def shards(
    queries, keys, values, outputs, d_outputs, log_norm, rand_owner, rand_local, glob_blocks
):
    tokens, features = queries.shape
    heads = log_norm.shape[0]
    head_size = features // heads
    blocks = tokens // BLOCK
    per_block = rand_owner.shape[1]
    many = glob_blocks.shape[0]
    owners = lax.axis_size("seq")
    references = blocks * per_block
    capacity = max(2, (references + owners - 1) // owners)
    by_permute = owners <= 8
    rows = -(-((2 * BLOCK + STAT) * capacity + capacity) // 16) * 16
    whole = jax.ShapeDtypeStruct((tokens, features), BF16)
    wide = jax.ShapeDtypeStruct((tokens, features), F32)
    pair_flops = 10 * BLOCK * BLOCK * 256

    packed = call(
        lambda *refs: pack_queries(heads, per_block, capacity, by_permute, refs),
        [
            whole,
            jax.ShapeDtypeStruct((blocks, STAT, BLOCK), F32),
            jax.ShapeDtypeStruct((owners * capacity,), jnp.int32),
        ]
        + [jax.ShapeDtypeStruct((rows, features), BF16)] * owners,
        [VMEM, VMEM, SMEM] + [VMEM] * owners,
        [VMEM, VMEM, VMEM, VMEM, SMEM, SMEM],
        [
            pltpu.SMEM((owners,), jnp.int32),
            pltpu.SMEM((owners * capacity,), jnp.int32),
            pltpu.SMEM((owners * capacity,), jnp.int32),
        ],
        1 << 20,
        owners * rows * 256,
        "pack_queries",
    )(queries, d_outputs, outputs, log_norm, rand_owner, rand_local)
    scaled, stats, source = packed[:3]
    outgoing = packed[3:]

    def swap(array, k):
        return lax.ppermute(array, "seq", [(i, i ^ k) for i in range(owners)])

    if by_permute:
        order = sorted(range(1, owners), key=lambda k: (-(k & -2 & (owners // 2)), k))
        arrived = {k: swap(outgoing[k], k)[None] for k in order}
        arrived[0] = outgoing[0][None]
    else:
        everyone = lax.all_to_all(jnp.stack(outgoing), "seq", split_axis=0, concat_axis=0, tiled=True)

    edge = jax.ShapeDtypeStruct((4 * BLOCK + 16, features), BF16)
    up, down, own, keys_t = call(
        functools.partial(pack_keys, head_size),
        [edge, edge, jax.ShapeDtypeStruct((2 * many * BLOCK, features), BF16), whole],
        [VMEM] * 4,
        [VMEM] * 5 + [SMEM],
        [],
        1 << 20,
        tokens * features * 10,
        "pack_keys",
    )(keys, values, scaled, d_outputs, stats, glob_blocks)
    forward = [(i, i + 1) for i in range(owners - 1)]
    before = lax.ppermute(up, "seq", forward)
    after = lax.ppermute(down, "seq", [(j, i) for i, j in forward])

    shared = own
    step = 1
    while step < owners:
        shared = shared + swap(shared, step)
        step *= 2

    dqt, dk, dv = call(
        functools.partial(window, heads),
        [wide] * 3,
        [VMEM] * 3,
        [VMEM] * 8,
        [],
        3 * blocks * pair_flops,
        tokens * features * 24,
        "window",
    )(scaled, d_outputs, stats, keys, values, keys_t, before, after)

    def owned(taken, dk, dv):
        return call(
            functools.partial(randoms, heads, capacity),
            [jax.ShapeDtypeStruct((taken.shape[0], capacity * BLOCK, features), BF16), wide, wide],
            [VMEM] * 3,
            [VMEM] * 6,
            [],
            taken.shape[0] * capacity * pair_flops,
            tokens * features * 20,
            "randoms",
        )(taken, keys, values, keys_t, dk, dv)

    returned = {}
    if by_permute:
        returned[0], dk, dv = owned(arrived[0], dk, dv)
    dqt, part = call(
        functools.partial(globals_, heads),
        [wide, jax.ShapeDtypeStruct(own.shape, BF16)],
        [VMEM] * 2,
        [VMEM] * 5,
        [pltpu.VMEM((many * BLOCK, features), F32)] * 2,
        many * blocks * pair_flops,
        tokens * features * 16,
        "globals",
    )(scaled, d_outputs, stats, shared, dqt)
    step = 1
    while step < owners:
        part = (part.astype(F32) + swap(part, step).astype(F32)).astype(BF16)
        step *= 2

    if by_permute:
        for k in order:
            back, dk, dv = owned(arrived[k], dk, dv)
            returned[k] = swap(back, k)
        rets = [returned[k] for k in range(owners)]
    else:
        back, dk, dv = owned(everyone, dk, dv)
        rets = [lax.all_to_all(back, "seq", split_axis=0, concat_axis=0, tiled=True)]

    d_keys, d_values = call(
        finish_keys,
        [whole, whole],
        [VMEM] * 2,
        [VMEM] * 3 + [SMEM],
        [pltpu.VMEM((tokens, features), F32)] * 2,
        1 << 20,
        tokens * features * 12,
        "finish_keys",
    )(dk, dv, part, glob_blocks)
    d_queries = call(
        lambda *refs: finish_queries(capacity, refs),
        whole,
        VMEM,
        [VMEM, SMEM] + [VMEM] * len(rets),
        [pltpu.VMEM((tokens, features), F32)],
        1 << 20,
        tokens * features * 12,
        "finish_queries",
    )(dqt, source, *rets)
    return d_queries, d_keys, d_values


def solution(mesh):
    placed = (
        P("seq", "head"),
        P("seq", "head"),
        P("seq", "head"),
        P("seq", "head"),
        P("seq", "head"),
        P("head", "seq"),
        P("seq", None),
        P("seq", None),
        P(),
    )
    return jax.shard_map(
        shards,
        mesh=mesh,
        in_specs=placed,
        out_specs=(P("seq", "head"), P("seq", "head"), P("seq", "head")),
        check_vma=False,
    )
```

time: 205 us -> 114 us (0.56)
  blocking collectives: 41.2 us -> 0 us
  local copies, waits for them, and re-layouts: 44.7 us -> 4.34 us
  other arithmetic: 28 us -> 0.23 us
  Pallas kernels: 0 us -> 21.7 us
  matrix products: 21.5 us -> 0 us
  starting transfers between devices: 27.7 us -> 47.4 us
  between operations: 19.1 us -> 0.89 us
  waiting for transfers between devices: 21.7 us -> 39.4 us
    psum x1 -> x0, blocking collectives: 41.2 us -> none  [shards(): shared = lax.psum(own_part, 'seq').astype(jnp.bfloat16)]
    ppermute x4 -> x22, waiting for transfers between devices: 2.68 us -> 39.4 us  [the longest x20 38.5 us: swap(): return lax.ppermute(array, 'seq', [(i, i ^ k) for i in range(owners)])]
    ppermute x4 -> x22, starting transfers between devices: 11 us -> 47.4 us  [the longest x20 42.6 us: swap(): return lax.ppermute(array, 'seq', [(i, i ^ k) for i in range(owners)])]
    pallas_call x0 -> x14, Pallas kernels: none -> 21.7 us  [the longest x8 7.57 us: owned(): call(functools.partial(randoms, heads, capacity), [jax.ShapeDtypeStruct((...]
    dot_general x42 -> x0, matrix products: 21.5 us -> none  [the longest x8 6.67 us: pair_terms(): jnp.einsum('nhqk,nkhd->nqhd', scores_low, key_rows, preferred_element_typ...]
    all_to_all x3 -> x0, waiting for transfers between devices: 19 us -> none  [the longest x1 15.1 us: shards(): lax.all_to_all(returned.reshape(owners, capacity, 2, BLOCK, features).ast...]
    all_to_all x3 -> x0, starting transfers between devices: 16.6 us -> none  [the longest x1 7.28 us: shards(): lax.all_to_all(requested.reshape(owners, capacity), 'seq', split_axis=0,...]
    slice x24 -> x0, local copies, waits for them, and re-layouts: 12 us -> none  [the longest x6 5.05 us: shards(): keys_pad[offset:offset + blocks]]
  transfers between devices with their start and end apart: 8 -> 22, of which waited for: 3 -> 8; matrix products, arithmetic and copies ran while one was open for 40% -> 0% of each run, Pallas kernels for 0% -> 14%
where the time goes in v1:
time: 114 us
  starting transfers between devices  47.4 us (42%)
  waiting for transfers between devices  39.4 us (35%)
  Pallas kernels  21.7 us (19%)
  local copies, waits for them, and re-layouts  4.34 us (4%)
    ppermute x20, starting transfers between devices, swap(): return lax.ppermute(array, 'seq', [(i, i ^ k) for i in range(owners)])  42.6 us
    ppermute x20, waiting for transfers between devices, swap(): return lax.ppermute(array, 'seq', [(i, i ^ k) for i in range(owners)])  38.5 us
    pallas_call x8, Pallas kernels, owned(): call(functools.partial(randoms, heads, capacity), [jax.ShapeDtypeStruct((...  7.57 us
    pallas_call x1, Pallas kernels, shards(): call(functools.partial(window, heads), [wide] * 3, [VMEM] * 3, [VMEM] * 8...  6.12 us
    unnamed x20, local copies, waits for them, and re-layouts  4.34 us
    ppermute x1, starting transfers between devices, shards(): before = lax.ppermute(up, 'seq', forward)  3.42 us
    pallas_call x1, Pallas kernels, shards(): call(functools.partial(globals_, heads), [wide, jax.ShapeDtypeStruct(own....  2.56 us
  transfers between devices with their start and end apart: 22, of which 8 were waited for; matrix products, arithmetic and copies ran while one was open for 0% of the time, Pallas kernels for 14%

profile of v1, /device:TPU:0, one launch (start us, length us, event | category | flops | bytes accessed | tf_op | source)
XLA Modules:
  0.0 113.8 jit_solution(5398534448791884128)
XLA Ops:
  0.7 0.8 copy.12.refs_4_
  1.5 0.9 copy-done.2
  2.5 0.9 copy-done.4
  3.4 0.9 copy-done.5
  4.4 1.6 %pack_queries.1 = (bf16[1024,128]{1,0:T(8,128)(2,1)S(1)}, f32[8,8,128]{2,1,0:T(8,128)S(1)}, s32[24]{0:T(128)S(1)}, bf16[800,128]{1,0:T(8,128)(2,1)S(1)}, bf16[80...) custom-call(bf16[1024,128]{1,0:T(8,128)(2,1)S(1)} %copy-done.4, ...), custom_call_target="tpu_custom_call" | custom-call | flops 1048576 | bytes 1638400 | tf_op jit(solution)/shard_map/pack_queries/pallas_call | solution.py:303
  6.0 0.6 copy-done.7
  6.6 0.7 pack_keys.1
  7.3 3.0 %collective-permute-start = (bf16[512,128]{1,0:T(8,128)(2,1)S(1)}, bf16[512,128]{1,0:T(8,128)(2,1)S(1)}, u32[]{:S(2)}, u32[]{:S(2)}) collective-permute-start(bf16[512,128]{1,0:T(8,128)(2,1)S(1)} %get-tuple-element.51), channel_id=1, source_target_pairs={{0,4},{4,0},{8,12},{12,8},{16,20},{20,16},{24,28},{28,24},{1,5},{5... | collective-permute-start | bytes 393224 | tf_op jit(solution)/shard_map/ppermute | solution.py:326
  10.4 3.5 %collective-permute-done = bf16[512,128]{1,0:T(8,128)(2,1)S(1)} collective-permute-done((bf16[512,128]{1,0:T(8,128)(2,1)S(1)}, bf16[512,128]{1,0:T(8,128)(2,1)S(1)}, u32[]{:S(2)}, u32[]{:S(2)}) %collective-permute-start) | collective-permute-done | bytes 131104 | tf_op jit(solution)/shard_map/ppermute | solution.py:326
  13.9 1.9 %collective-permute-start.1 = (bf16[512,128]{1,0:T(8,128)(2,1)S(1)}, bf16[512,128]{1,0:T(8,128)(2,1)S(1)}, u32[]{:S(2)}, u32[]{:S(2)}) collective-permute-start(bf16[512,128]{1,0:T(8,128)(2,1)S(1)} %add.18), channel_id=1, source_target_pairs={{0,8},{4,12},{8,0},{12,4},{16,24},{20,28},{24,16},{28,20},{1,9},{5... | collective-permute-start | bytes 393224 | tf_op jit(solution)/shard_map/ppermute | solution.py:326
  15.8 3.4 %collective-permute-start.3 = (bf16[528,128]{1,0:T(8,128)(2,1)S(1)}, bf16[528,128]{1,0:T(8,128)(2,1)S(1)}, u32[]{:S(2)}, u32[]{:S(2)}) collective-permute-start(bf16[528,128]{1,0:T(8,128)(2,1)S(1)} %get-tuple-element.53), channel_id=1, source_target_pairs={{0,4},{4,8},{8,12},{12,16},{16,20},{20,24},{24,28},{1,5},{5,9},{9,... | collective-permute-start | bytes 405512 | tf_op jit(solution)/shard_map/ppermute | solution.py:347
  19.2 1.3 %collective-permute-start.4 = (bf16[528,128]{1,0:T(8,128)(2,1)S(1)}, bf16[528,128]{1,0:T(8,128)(2,1)S(1)}, u32[]{:S(2)}, u32[]{:S(2)}) collective-permute-start(bf16[528,128]{1,0:T(8,128)(2,1)S(1)} %get-tuple-element.54), channel_id=1, source_target_pairs={{4,0},{8,4},{12,8},{16,12},{20,16},{24,20},{28,24},{5,1},{9,5},{13... | collective-permute-start | bytes 405512 | tf_op jit(solution)/shard_map/ppermute | solution.py:348
  20.5 4.7 %collective-permute-start.2 = (bf16[512,128]{1,0:T(8,128)(2,1)S(1)}, bf16[512,128]{1,0:T(8,128)(2,1)S(1)}, u32[]{:S(2)}, u32[]{:S(2)}) collective-permute-start(bf16[512,128]{1,0:T(8,128)(2,1)S(1)} %add.19), channel_id=1, source_target_pairs={{0,16},{4,20},{8,24},{12,28},{16,0},{20,4},{24,8},{28,12},{1,17},{... | collective-permute-start | bytes 393224 | tf_op jit(solution)/shard_map/ppermute | solution.py:326
  25.2 0.9 collective-permute-done.4.after_ref
  26.1 6.1 %window.1 = (f32[1024,128]{1,0:T(8,128)S(1)}, f32[1024,128]{1,0:T(8,128)S(1)}, f32[1024,128]{1,0:T(8,128)S(1)}) custom-call(bf16[1024,128]{1,0:T(8,128)(2,1)S(1)} %get-tuple-element.49.q_ref, bf16[1024,128]{1,0:T(8,128)(2,1)S(1)} %copy-done.3, f32[8,8,128]{2,1,0:T(8,128)S(1)} %get-tuple-element.50.stats_ref, bf16[1024,128]{1,0:T(8,128)(2,1)S(1)} %copy-done, ...), custom_call_target="tpu_custom_call" | custom-call | flops 1006632960 | bytes 3145728 | tf_op jit(solution)/shard_map/window/pallas_call | solution.py:356
  32.2 0.3 collective-permute-done.2
  32.6 2.6 %globals.1 = (f32[1024,128]{1,0:T(8,128)S(1)}, bf16[512,128]{1,0:T(8,128)(2,1)S(1)}) custom-call(bf16[1024,128]{1,0:T(8,128)(2,1)S(1)} %get-tuple-element.49.q_ref, bf16[1024,128]{1,0:T(8,128)(2,1)S(1)} %copy-done.3, f32[8,8,128]{2,1,0:T(8,128)S(1)} %get-tuple-element.50.stats_ref, bf16[512,128]{1,0:T(8,128)(2,1)S(1)} %add.20.shared_ref, ...), custom_call_target="tpu_custom_call" | custom-call | flops 671088640 | bytes 2097152 | tf_op jit(solution)/shard_map/globals/pallas_call | solution.py:382
  35.2 0.9 collective-permute-start.19
  36.0 1.2 %collective-permute-start.5 = (bf16[800,128]{1,0:T(8,128)(2,1)S(1)}, bf16[800,128]{1,0:T(8,128)(2,1)S(1)}, u32[]{:S(2)}, u32[]{:S(2)}) collective-permute-start(bf16[800,128]{1,0:T(8,128)(2,1)S(1)} %get-tuple-element.62), channel_id=1, source_target_pairs={{0,4},{4,0},{8,12},{12,8},{16,20},{20,16},{24,28},{28,24},{1,5},{5... | collective-permute-start | bytes 614408 | tf_op jit(solution)/shard_map/ppermute | solution.py:326
  37.3 2.3 %collective-permute-start.6 = (bf16[800,128]{1,0:T(8,128)(2,1)S(1)}, bf16[800,128]{1,0:T(8,128)(2,1)S(1)}, u32[]{:S(2)}, u32[]{:S(2)}) collective-permute-start(bf16[800,128]{1,0:T(8,128)(2,1)S(1)} %get-tuple-element.63), channel_id=1, source_target_pairs={{0,28},{4,24},{8,20},{12,16},{16,12},{20,8},{24,4},{28,0},{1,29},{... | collective-permute-start | bytes 614408 | tf_op jit(solution)/shard_map/ppermute | solution.py:326
  39.6 1.7 %collective-permute-start.7 = (bf16[800,128]{1,0:T(8,128)(2,1)S(1)}, bf16[800,128]{1,0:T(8,128)(2,1)S(1)}, u32[]{:S(2)}, u32[]{:S(2)}) collective-permute-start(bf16[800,128]{1,0:T(8,128)(2,1)S(1)} %get-tuple-element.64), channel_id=1, source_target_pairs={{0,24},{4,28},{8,16},{12,20},{16,8},{20,12},{24,0},{28,4},{1,25},{... | collective-permute-start | bytes 614408 | tf_op jit(solution)/shard_map/ppermute | solution.py:326
  41.3 3.6 %collective-permute-start.8 = (bf16[800,128]{1,0:T(8,128)(2,1)S(1)}, bf16[800,128]{1,0:T(8,128)(2,1)S(1)}, u32[]{:S(2)}, u32[]{:S(2)}) collective-permute-start(bf16[800,128]{1,0:T(8,128)(2,1)S(1)} %get-tuple-element.65), channel_id=1, source_target_pairs={{0,20},{4,16},{8,28},{12,24},{16,4},{20,0},{24,12},{28,8},{1,21},{... | collective-permute-start | bytes 614408 | tf_op jit(solution)/shard_map/ppermute | solution.py:326
  44.9 0.9 collective-permute-start.9
  45.9 28.3 %collective-permute-done.9 = bf16[800,128]{1,0:T(8,128)(2,1)S(1)} collective-permute-done((bf16[800,128]{1,0:T(8,128)(2,1)S(1)}, bf16[800,128]{1,0:T(8,128)(2,1)S(1)}, u32[]{:S(2)}, u32[]{:S(2)}) %collective-permute-start.9) | collective-permute-done | bytes 204832 | tf_op jit(solution)/shard_map/ppermute | solution.py:326
  74.2 0.9 randoms.8
  75.2 0.9 randoms.9
  76.1 2.1 %collective-permute-start.11 = (bf16[800,128]{1,0:T(8,128)(2,1)S(1)}, bf16[800,128]{1,0:T(8,128)(2,1)S(1)}, u32[]{:S(2)}, u32[]{:S(2)}) collective-permute-start(bf16[800,128]{1,0:T(8,128)(2,1)S(1)} %get-tuple-element.78), channel_id=1, source_target_pairs={{0,8},{4,12},{8,0},{12,4},{16,24},{20,28},{24,16},{28,20},{1,9},{5... | collective-permute-start | bytes 614408 | tf_op jit(solution)/shard_map/ppermute | solution.py:326
  78.2 0.9 randoms.10
  79.2 0.8 collective-permute-start.13
  80.0 0.9 randoms.11
  81.0 0.9 randoms.12
  81.9 1.0 randoms.13
  82.9 0.8 collective-permute-start.10
  83.7 3.6 %collective-permute-start.18 = (bf16[1,384,128]{2,1,0:T(8,128)(2,1)S(1)}, bf16[1,384,128]{2,1,0:T(8,128)(2,1)S(1)}, u32[]{:S(2)}, u32[]{:S(2)}) collective-permute-start(bf16[1,384,128]{2,1,0:T(8,128)(2,1)S(1)} %get-tuple-element.89), channel_id=1, source_target_pairs={{0,28},{4,24},{8,20},{12,16},{16,12},{20,8},{24,4},{28,0},{1,29},{... | collective-permute-start | bytes 294920 | tf_op jit(solution)/shard_map/ppermute | solution.py:326
  87.2 1.0 collective-permute-start.17
  88.3 1.6 %collective-permute-start.21 = (bf16[512,128]{1,0:T(8,128)(2,1)S(1)}, bf16[512,128]{1,0:T(8,128)(2,1)S(1)}, u32[]{:S(2)}, u32[]{:S(2)}) collective-permute-start(bf16[512,128]{1,0:T(8,128)(2,1)S(1)} %add_convert_fusion.1), channel_id=1, source_target_pairs={{0,16},{4,20},{8,24},{12,28},{16,0},{20,4},{24,8},{28,12},{1,17},{... | collective-permute-start | bytes 393224 | tf_op jit(solution)/shard_map/ppermute | solution.py:326
  89.9 0.9 randoms.14
  90.9 1.6 %collective-permute-start.16 = (bf16[1,384,128]{2,1,0:T(8,128)(2,1)S(1)}, bf16[1,384,128]{2,1,0:T(8,128)(2,1)S(1)}, u32[]{:S(2)}, u32[]{:S(2)}) collective-permute-start(bf16[1,384,128]{2,1,0:T(8,128)(2,1)S(1)} %get-tuple-element.87), channel_id=1, source_target_pairs={{0,20},{4,16},{8,28},{12,24},{16,4},{20,0},{24,12},{28,8},{1,21},{... | collective-permute-start | bytes 294920 | tf_op jit(solution)/shard_map/ppermute | solution.py:326
  92.5 0.9 randoms.15
  93.4 1.3 %collective-permute-start.15 = (bf16[1,384,128]{2,1,0:T(8,128)(2,1)S(1)}, bf16[1,384,128]{2,1,0:T(8,128)(2,1)S(1)}, u32[]{:S(2)}, u32[]{:S(2)}) collective-permute-start(bf16[1,384,128]{2,1,0:T(8,128)(2,1)S(1)} %get-tuple-element.86), channel_id=1, source_target_pairs={{0,16},{4,20},{8,24},{12,28},{16,0},{20,4},{24,8},{28,12},{1,17},{... | collective-permute-start | bytes 294920 | tf_op jit(solution)/shard_map/ppermute | solution.py:326
  94.7 6.1 %collective-permute-start.12 = (bf16[1,384,128]{2,1,0:T(8,128)(2,1)S(1)}, bf16[1,384,128]{2,1,0:T(8,128)(2,1)S(1)}, u32[]{:S(2)}, u32[]{:S(2)}) collective-permute-start(bf16[1,384,128]{2,1,0:T(8,128)(2,1)S(1)} %get-tuple-element.81), channel_id=1, source_target_pairs={{0,8},{4,12},{8,0},{12,4},{16,24},{20,28},{24,16},{28,20},{1,9},{5... | collective-permute-start | bytes 294920 | tf_op jit(solution)/shard_map/ppermute | solution.py:326
  100.8 3.6 %collective-permute-start.14 = (bf16[1,384,128]{2,1,0:T(8,128)(2,1)S(1)}, bf16[1,384,128]{2,1,0:T(8,128)(2,1)S(1)}, u32[]{:S(2)}, u32[]{:S(2)}) collective-permute-start(bf16[1,384,128]{2,1,0:T(8,128)(2,1)S(1)} %get-tuple-element.85), channel_id=1, source_target_pairs={{0,12},{4,8},{8,4},{12,0},{16,28},{20,24},{24,20},{28,16},{1,13},{... | collective-permute-start | bytes 294920 | tf_op jit(solution)/shard_map/ppermute | solution.py:326
  104.4 3.2 %collective-permute-done.16.refs_7_ = bf16[1,384,128]{2,1,0:T(8,128)(2,1)S(1)} collective-permute-done((bf16[1,384,128]{2,1,0:T(8,128)(2,1)S(1)}, bf16[1,384,128]{2,1,0:T(8,128)(2,1)S(1)}, u32[]{:S(2)}, u32[]{:S(2)}) %collective-permute-start.16) | collective-permute-done | bytes 98336 | tf_op jit(solution)/shard_map/ppermute | solution.py:326
  107.6 0.9 collective-permute-done.15.refs_6_
  108.5 0.3 collective-permute-done.12.refs_4_
  108.8 1.9 %collective-permute-done.14.refs_5_ = bf16[1,384,128]{2,1,0:T(8,128)(2,1)S(1)} collective-permute-done((bf16[1,384,128]{2,1,0:T(8,128)(2,1)S(1)}, bf16[1,384,128]{2,1,0:T(8,128)(2,1)S(1)}, u32[]{:S(2)}, u32[]{:S(2)}) %collective-permute-start.14) | collective-permute-done | bytes 98336 | tf_op jit(solution)/shard_map/ppermute | solution.py:326
  110.7 1.7 %finish_queries.1 = bf16[1024,128]{1,0:T(8,128)(2,1)} custom-call(f32[1024,128]{1,0:T(8,128)S(1)} %get-tuple-element.56.refs_0_, s32[24]{0:T(128)S(1)} %get-tuple-element.57.refs_1_, bf16[1,384,128]{2,1,0:T(8,128)(2,1)S(1)} %get-tuple-element.61.refs_2_, bf16[1,384,128]{2,1,0:T(8,128)(2,1)S(1)} %collective-permute-done.10.refs_3_, ...), custom_call_target="tpu_custom_call" | custom-call | flops 1048576 | bytes 1572864 | tf_op jit(solution)/shard_map/finish_queries/pallas_call | solution.py:416
  112.4 1.4 %finish_keys.1 = (bf16[1024,128]{1,0:T(8,128)(2,1)}, bf16[1024,128]{1,0:T(8,128)(2,1)}) custom-call(f32[1024,128]{1,0:T(8,128)S(1)} %get-tuple-element.90.dk_in, f32[1024,128]{1,0:T(8,128)S(1)} %get-tuple-element.91.dv_in, bf16[512,128]{1,0:T(8,128)(2,1)S(1)} %add_convert_fusion.total_ref, s32[2]{0:T(128)S(1)} %copy-done.7), custom_call_target="tpu_custom_call" | custom-call | flops 1048576 | bytes 1572864 | tf_op jit(solution)/shard_map/finish_keys/pallas_call | solution.py:406
  (36 shorter events, 0.4 us)
Async XLA Ops:
  0.6 0.8 copy-start.8
  0.6 0.9 copy-start.6
  1.5 1.0 copy-start.2
  2.5 0.9 copy-start.4
  3.4 0.9 copy-start.5
  4.4 1.6 %copy-start = (bf16[1024,128]{1,0:T(8,128)(2,1)S(1)}, bf16[1024,128]{1,0:T(8,128)(2,1)}, u32[]{:S(2)}) copy-start(bf16[1024,128]{1,0:T(8,128)(2,1)} %k_ref.19) | copy-start | bytes 786436
  4.4 1.6 %copy-start.1 = (bf16[1024,128]{1,0:T(8,128)(2,1)S(1)}, bf16[1024,128]{1,0:T(8,128)(2,1)}, u32[]{:S(2)}) copy-start(bf16[1024,128]{1,0:T(8,128)(2,1)} %v_ref.19) | copy-start | bytes 786436
  4.4 1.6 %copy-start.3 = (bf16[1024,128]{1,0:T(8,128)(2,1)S(1)}, bf16[1024,128]{1,0:T(8,128)(2,1)}, u32[]{:S(2)}) copy-start(bf16[1024,128]{1,0:T(8,128)(2,1)} %g_ref.5) | copy-start | bytes 786436
  6.0 0.7 copy-start.7
  7.3 6.5 %collective-permute-start = (bf16[512,128]{1,0:T(8,128)(2,1)S(1)}, bf16[512,128]{1,0:T(8,128)(2,1)S(1)}, u32[]{:S(2)}, u32[]{:S(2)}) collective-permute-start(bf16[512,128]{1,0:T(8,128)(2,1)S(1)} %get-tuple-element.51), channel_id=1, source_target_pairs={{0,4},{4,0},{8,12},{12,8},{16,20},{20,16},{24,28},{28,24},{1,5},{5... | collective-permute-start | bytes 393224 | tf_op jit(solution)/shard_map/ppermute | solution.py:326
  13.9 6.6 %collective-permute-start.1 = (bf16[512,128]{1,0:T(8,128)(2,1)S(1)}, bf16[512,128]{1,0:T(8,128)(2,1)S(1)}, u32[]{:S(2)}, u32[]{:S(2)}) collective-permute-start(bf16[512,128]{1,0:T(8,128)(2,1)S(1)} %add.18), channel_id=1, source_target_pairs={{0,8},{4,12},{8,0},{12,4},{16,24},{20,28},{24,16},{28,20},{1,9},{5... | collective-permute-start | bytes 393224 | tf_op jit(solution)/shard_map/ppermute | solution.py:326
  15.8 9.5 %collective-permute-start.3 = (bf16[528,128]{1,0:T(8,128)(2,1)S(1)}, bf16[528,128]{1,0:T(8,128)(2,1)S(1)}, u32[]{:S(2)}, u32[]{:S(2)}) collective-permute-start(bf16[528,128]{1,0:T(8,128)(2,1)S(1)} %get-tuple-element.53), channel_id=1, source_target_pairs={{0,4},{4,8},{8,12},{12,16},{16,20},{20,24},{24,28},{1,5},{5,9},{9,... | collective-permute-start | bytes 405512 | tf_op jit(solution)/shard_map/ppermute | solution.py:347
  19.2 6.9 %collective-permute-start.4 = (bf16[528,128]{1,0:T(8,128)(2,1)S(1)}, bf16[528,128]{1,0:T(8,128)(2,1)S(1)}, u32[]{:S(2)}, u32[]{:S(2)}) collective-permute-start(bf16[528,128]{1,0:T(8,128)(2,1)S(1)} %get-tuple-element.54), channel_id=1, source_target_pairs={{4,0},{8,4},{12,8},{16,12},{20,16},{24,20},{28,24},{5,1},{9,5},{13... | collective-permute-start | bytes 405512 | tf_op jit(solution)/shard_map/ppermute | solution.py:348
  20.5 12.0 %collective-permute-start.2 = (bf16[512,128]{1,0:T(8,128)(2,1)S(1)}, bf16[512,128]{1,0:T(8,128)(2,1)S(1)}, u32[]{:S(2)}, u32[]{:S(2)}) collective-permute-start(bf16[512,128]{1,0:T(8,128)(2,1)S(1)} %add.19), channel_id=1, source_target_pairs={{0,16},{4,20},{8,24},{12,28},{16,0},{20,4},{24,8},{28,12},{1,17},{... | collective-permute-start | bytes 393224 | tf_op jit(solution)/shard_map/ppermute | solution.py:326
  35.2 9.8 %collective-permute-start.19 = (bf16[512,128]{1,0:T(8,128)(2,1)S(1)}, bf16[512,128]{1,0:T(8,128)(2,1)S(1)}, u32[]{:S(2)}, u32[]{:S(2)}) collective-permute-start(bf16[512,128]{1,0:T(8,128)(2,1)S(1)} %get-tuple-element.92), channel_id=1, source_target_pairs={{0,4},{4,0},{8,12},{12,8},{16,20},{20,16},{24,28},{28,24},{1,5},{5... | collective-permute-start | bytes 393224 | tf_op jit(solution)/shard_map/ppermute | solution.py:326
  36.0 45.9 %collective-permute-start.5 = (bf16[800,128]{1,0:T(8,128)(2,1)S(1)}, bf16[800,128]{1,0:T(8,128)(2,1)S(1)}, u32[]{:S(2)}, u32[]{:S(2)}) collective-permute-start(bf16[800,128]{1,0:T(8,128)(2,1)S(1)} %get-tuple-element.62), channel_id=1, source_target_pairs={{0,4},{4,0},{8,12},{12,8},{16,20},{20,16},{24,28},{28,24},{1,5},{5... | collective-permute-start | bytes 614408 | tf_op jit(solution)/shard_map/ppermute | solution.py:326
  37.3 43.7 %collective-permute-start.6 = (bf16[800,128]{1,0:T(8,128)(2,1)S(1)}, bf16[800,128]{1,0:T(8,128)(2,1)S(1)}, u32[]{:S(2)}, u32[]{:S(2)}) collective-permute-start(bf16[800,128]{1,0:T(8,128)(2,1)S(1)} %get-tuple-element.63), channel_id=1, source_target_pairs={{0,28},{4,24},{8,20},{12,16},{16,12},{20,8},{24,4},{28,0},{1,29},{... | collective-permute-start | bytes 614408 | tf_op jit(solution)/shard_map/ppermute | solution.py:326
  39.6 39.6 %collective-permute-start.7 = (bf16[800,128]{1,0:T(8,128)(2,1)S(1)}, bf16[800,128]{1,0:T(8,128)(2,1)S(1)}, u32[]{:S(2)}, u32[]{:S(2)}) collective-permute-start(bf16[800,128]{1,0:T(8,128)(2,1)S(1)} %get-tuple-element.64), channel_id=1, source_target_pairs={{0,24},{4,28},{8,16},{12,20},{16,8},{20,12},{24,0},{28,4},{1,25},{... | collective-permute-start | bytes 614408 | tf_op jit(solution)/shard_map/ppermute | solution.py:326
  41.3 34.8 %collective-permute-start.8 = (bf16[800,128]{1,0:T(8,128)(2,1)S(1)}, bf16[800,128]{1,0:T(8,128)(2,1)S(1)}, u32[]{:S(2)}, u32[]{:S(2)}) collective-permute-start(bf16[800,128]{1,0:T(8,128)(2,1)S(1)} %get-tuple-element.65), channel_id=1, source_target_pairs={{0,20},{4,16},{8,28},{12,24},{16,4},{20,0},{24,12},{28,8},{1,21},{... | collective-permute-start | bytes 614408 | tf_op jit(solution)/shard_map/ppermute | solution.py:326
  44.9 29.3 %collective-permute-start.9 = (bf16[800,128]{1,0:T(8,128)(2,1)S(1)}, bf16[800,128]{1,0:T(8,128)(2,1)S(1)}, u32[]{:S(2)}, u32[]{:S(2)}) collective-permute-start(bf16[800,128]{1,0:T(8,128)(2,1)S(1)} %get-tuple-element.66), channel_id=1, source_target_pairs={{0,16},{4,20},{8,24},{12,28},{16,0},{20,4},{24,8},{28,12},{1,17},{... | collective-permute-start | bytes 614408 | tf_op jit(solution)/shard_map/ppermute | solution.py:326
  74.2 13.0 %collective-permute-start.20 = (bf16[512,128]{1,0:T(8,128)(2,1)S(1)}, bf16[512,128]{1,0:T(8,128)(2,1)S(1)}, u32[]{:S(2)}, u32[]{:S(2)}) collective-permute-start(bf16[512,128]{1,0:T(8,128)(2,1)S(1)} %add_convert_fusion.2), channel_id=1, source_target_pairs={{0,8},{4,12},{8,0},{12,4},{16,24},{20,28},{24,16},{28,20},{1,9},{5... | collective-permute-start | bytes 393224 | tf_op jit(solution)/shard_map/ppermute | solution.py:326
  76.1 12.1 %collective-permute-start.11 = (bf16[800,128]{1,0:T(8,128)(2,1)S(1)}, bf16[800,128]{1,0:T(8,128)(2,1)S(1)}, u32[]{:S(2)}, u32[]{:S(2)}) collective-permute-start(bf16[800,128]{1,0:T(8,128)(2,1)S(1)} %get-tuple-element.78), channel_id=1, source_target_pairs={{0,8},{4,12},{8,0},{12,4},{16,24},{20,28},{24,16},{28,20},{1,9},{5... | collective-permute-start | bytes 614408 | tf_op jit(solution)/shard_map/ppermute | solution.py:326
  79.2 11.7 %collective-permute-start.13 = (bf16[800,128]{1,0:T(8,128)(2,1)S(1)}, bf16[800,128]{1,0:T(8,128)(2,1)S(1)}, u32[]{:S(2)}, u32[]{:S(2)}) collective-permute-start(bf16[800,128]{1,0:T(8,128)(2,1)S(1)} %get-tuple-element.82), channel_id=1, source_target_pairs={{0,12},{4,8},{8,4},{12,0},{16,28},{20,24},{24,20},{28,16},{1,13},{... | collective-permute-start | bytes 614408 | tf_op jit(solution)/shard_map/ppermute | solution.py:326
  82.9 10.6 %collective-permute-start.10 = (bf16[1,384,128]{2,1,0:T(8,128)(2,1)S(1)}, bf16[1,384,128]{2,1,0:T(8,128)(2,1)S(1)}, u32[]{:S(2)}, u32[]{:S(2)}) collective-permute-start(bf16[1,384,128]{2,1,0:T(8,128)(2,1)S(1)} %get-tuple-element.77), channel_id=1, source_target_pairs={{0,4},{4,0},{8,12},{12,8},{16,20},{20,16},{24,28},{28,24},{1,5},{5... | collective-permute-start | bytes 294920 | tf_op jit(solution)/shard_map/ppermute | solution.py:326
  83.7 11.0 %collective-permute-start.18 = (bf16[1,384,128]{2,1,0:T(8,128)(2,1)S(1)}, bf16[1,384,128]{2,1,0:T(8,128)(2,1)S(1)}, u32[]{:S(2)}, u32[]{:S(2)}) collective-permute-start(bf16[1,384,128]{2,1,0:T(8,128)(2,1)S(1)} %get-tuple-element.89), channel_id=1, source_target_pairs={{0,28},{4,24},{8,20},{12,16},{16,12},{20,8},{24,4},{28,0},{1,29},{... | collective-permute-start | bytes 294920 | tf_op jit(solution)/shard_map/ppermute | solution.py:326
  87.2 13.5 %collective-permute-start.17 = (bf16[1,384,128]{2,1,0:T(8,128)(2,1)S(1)}, bf16[1,384,128]{2,1,0:T(8,128)(2,1)S(1)}, u32[]{:S(2)}, u32[]{:S(2)}) collective-permute-start(bf16[1,384,128]{2,1,0:T(8,128)(2,1)S(1)} %get-tuple-element.88), channel_id=1, source_target_pairs={{0,24},{4,28},{8,16},{12,20},{16,8},{20,12},{24,0},{28,4},{1,25},{... | collective-permute-start | bytes 294920 | tf_op jit(solution)/shard_map/ppermute | solution.py:326
  88.3 24.1 %collective-permute-start.21 = (bf16[512,128]{1,0:T(8,128)(2,1)S(1)}, bf16[512,128]{1,0:T(8,128)(2,1)S(1)}, u32[]{:S(2)}, u32[]{:S(2)}) collective-permute-start(bf16[512,128]{1,0:T(8,128)(2,1)S(1)} %add_convert_fusion.1), channel_id=1, source_target_pairs={{0,16},{4,20},{8,24},{12,28},{16,0},{20,4},{24,8},{28,12},{1,17},{... | collective-permute-start | bytes 393224 | tf_op jit(solution)/shard_map/ppermute | solution.py:326
  90.9 16.7 %collective-permute-start.16 = (bf16[1,384,128]{2,1,0:T(8,128)(2,1)S(1)}, bf16[1,384,128]{2,1,0:T(8,128)(2,1)S(1)}, u32[]{:S(2)}, u32[]{:S(2)}) collective-permute-start(bf16[1,384,128]{2,1,0:T(8,128)(2,1)S(1)} %get-tuple-element.87), channel_id=1, source_target_pairs={{0,20},{4,16},{8,28},{12,24},{16,4},{20,0},{24,12},{28,8},{1,21},{... | collective-permute-start | bytes 294920 | tf_op jit(solution)/shard_map/ppermute | solution.py:326
  93.4 15.0 %collective-permute-start.15 = (bf16[1,384,128]{2,1,0:T(8,128)(2,1)S(1)}, bf16[1,384,128]{2,1,0:T(8,128)(2,1)S(1)}, u32[]{:S(2)}, u32[]{:S(2)}) collective-permute-start(bf16[1,384,128]{2,1,0:T(8,128)(2,1)S(1)} %get-tuple-element.86), channel_id=1, source_target_pairs={{0,16},{4,20},{8,24},{12,28},{16,0},{20,4},{24,8},{28,12},{1,17},{... | collective-permute-start | bytes 294920 | tf_op jit(solution)/shard_map/ppermute | solution.py:326
  94.7 14.0 %collective-permute-start.12 = (bf16[1,384,128]{2,1,0:T(8,128)(2,1)S(1)}, bf16[1,384,128]{2,1,0:T(8,128)(2,1)S(1)}, u32[]{:S(2)}, u32[]{:S(2)}) collective-permute-start(bf16[1,384,128]{2,1,0:T(8,128)(2,1)S(1)} %get-tuple-element.81), channel_id=1, source_target_pairs={{0,8},{4,12},{8,0},{12,4},{16,24},{20,28},{24,16},{28,20},{1,9},{5... | collective-permute-start | bytes 294920 | tf_op jit(solution)/shard_map/ppermute | solution.py:326
  100.8 9.9 %collective-permute-start.14 = (bf16[1,384,128]{2,1,0:T(8,128)(2,1)S(1)}, bf16[1,384,128]{2,1,0:T(8,128)(2,1)S(1)}, u32[]{:S(2)}, u32[]{:S(2)}) collective-permute-start(bf16[1,384,128]{2,1,0:T(8,128)(2,1)S(1)} %get-tuple-element.85), channel_id=1, source_target_pairs={{0,12},{4,8},{8,4},{12,0},{16,28},{20,24},{24,20},{28,16},{1,13},{... | collective-permute-start | bytes 294920 | tf_op jit(solution)/shard_map/ppermute | solution.py:326

commit v2 on v1

v2 whole, which is shorter than its diff:
```python
import functools
import math

import jax
import jax.numpy as jnp
from jax import lax
from jax.experimental import pallas as pl
from jax.experimental.pallas import tpu as pltpu
from jax.sharding import PartitionSpec as P

BLOCK = 128
STAT = 8
LOG2E = math.log2(math.e)
NT = (((1,), (1,)), ((), ()))
VMEM = pl.BlockSpec(memory_space=pltpu.VMEM)
SMEM = pl.BlockSpec(memory_space=pltpu.SMEM)
HBM = pl.BlockSpec(memory_space=pltpu.HBM)
F32 = jnp.float32
BF16 = jnp.bfloat16
LIMIT = 24
PIECES = 4
COSTS = {'window': 3, 'randoms': 3, 'finish_keys': 3, 'finish_queries': 3}
GATES = {'W': ['G1'], 'F5': ['G1'], 'F6': ['G2', 'R0'], 'F7': ['F4'], 'F2': ['F5'], 'F3': ['F5'], 'R1': ['G2'], 'R3': ['R1'], 'r6': ['r4'], 'r7': ['r5'], 'P2': ['F6', 'F7', 'r4'], 'P3': ['r5', 'F5'], 'r1': ['r6']}
GROUPS = [[4], [0], [5], [1], [2], [6], [7], [3]]
HOPS = {'G': [4, 2, 1], 'P': [1, 2, 4]}


def call(body, out_shape, out_specs, in_specs, scratch, name, aliases={}, limit=24):
    return pl.pallas_call(
        body,
        out_shape=out_shape,
        in_specs=in_specs,
        out_specs=out_specs,
        scratch_shapes=scratch,
        input_output_aliases=aliases,
        compiler_params=pltpu.CompilerParams(vmem_limit_bytes=int(limit * 1024 * 1024)),
        cost_estimate=pl.CostEstimate(
            flops=int(COSTS.get(name, 0) * 1.15e9), bytes_accessed=0, transcendentals=0
        ),
        name=name,
    )


def after(array, *others):
    return lax.optimization_barrier((array, *others))[0] if others else array


def dot(a, b):
    return jnp.dot(a, b, preferred_element_type=F32)


def by_head(rows, heads):
    width = rows.shape[1] // heads
    lane = lax.broadcasted_iota(jnp.int32, (1, rows.shape[1]), 1)
    parts = []
    for h in range(heads):
        keep = ((lane >= h * width) & (lane < (h + 1) * width)).astype(F32).astype(BF16)
        parts.append(rows * keep)
    return jnp.concatenate(parts, axis=0)


def stat_rows(tile, heads):
    half = 2 * heads
    norm = [tile[h : h + 1] + tile[heads + h : heads + h + 1] for h in range(heads)]
    delta = [tile[half + h : half + h + 1] + tile[half + heads + h : half + heads + h + 1] for h in range(heads)]
    return jnp.concatenate(norm, axis=1), jnp.concatenate(delta, axis=1)


def weigh(key_rows, value_rows, q_bd, g_bd, norm, delta):
    scores = lax.dot_general(key_rows, q_bd, NT, preferred_element_type=F32)
    weights = jnp.exp2(scores * LOG2E - norm)
    grad = lax.dot_general(value_rows, g_bd, NT, preferred_element_type=F32)
    return weights.astype(BF16), (weights * (grad - delta)).astype(BF16)


def grad_query_t(keys_t, low, heads):
    width = keys_t.shape[0] // heads
    return jnp.concatenate(
        [dot(keys_t[h * width : (h + 1) * width], low[:, h * BLOCK : (h + 1) * BLOCK]) for h in range(heads)],
        axis=0,
    )


def message_rows(slots):
    return -(-((2 * BLOCK + STAT + 1) * slots) // 16) * 16


def pack(heads, plan, refs):
    q_hbm, g_hbm, o_hbm, k_hbm, v_hbm, norm_hbm, owner_ref, local_ref, glob_ref = refs[:9]
    scaled_ref, stats_ref, own_ref, kt_ref, src_ref = refs[9:14]
    out_refs = refs[14 : 14 + len(plan)]
    q_ref, g_ref, o_ref, k_ref, v_ref, norm_ref, sems, count, source, place = refs[14 + len(plan) :]
    copies = [
        pltpu.make_async_copy(a, b, sems.at[n])
        for n, (a, b) in enumerate(
            (
                (g_hbm, g_ref),
                (o_hbm, o_ref),
                (norm_hbm, norm_ref),
                (q_hbm, q_ref),
                (k_hbm, k_ref),
                (v_hbm, v_ref),
            )
        )
    ]
    for copy in copies:
        copy.start()
    blocks = q_ref.shape[0] // BLOCK
    per_block = owner_ref.shape[0]
    width = q_ref.shape[1] // heads
    me = lax.axis_index("seq")
    fold = any(entry[1] == "xor" for entry in plan)
    most = max(entry[0] for entry in plan)
    randoms = sum(1 for entry in plan if entry[0])
    for k in range(randoms):
        count[k] = 0
        for s in range(most):
            source[k * most + s] = -1
    for b in range(blocks):
        for r in range(per_block):
            k = owner_ref[r, b]
            if fold:
                k = k ^ me
            s = count[k]
            count[k] = s + 1
            source[k * most + s] = b
            place[k * most + s] = local_ref[r, b]
    for copy in copies[:3]:
        copy.wait()
    for b in range(blocks):
        rows = pl.ds(b * BLOCK, BLOCK)
        prod = (o_ref[rows, :].astype(F32) * g_ref[rows, :].astype(F32)).T
        norm = [norm_ref[h : h + 1, rows] * LOG2E for h in range(heads)]
        delta = [jnp.sum(prod[h * width : (h + 1) * width], axis=0, keepdims=True) for h in range(heads)]
        exact = jnp.concatenate(norm + delta, axis=0)
        high = exact.astype(BF16).astype(F32)
        low = (exact - high).astype(BF16).astype(F32)
        stats_ref[b] = jnp.concatenate([high[:heads], low[:heads], high[heads:], low[heads:]], axis=0)
    copies[3].wait()
    scaled_ref[...] = q_ref[...] * jnp.asarray(1.0 / math.sqrt(width), BF16)
    full = blocks * per_block == randoms * most
    done = 0
    for k, (slots, edge) in enumerate(plan):
        out = out_refs[k]
        tiles, marks = [], []
        total = slots + (edge not in (None, "xor"))
        for s in range(total):
            if s < slots:
                b, number, sure = source[k * most + s], place[k * most + s], full
            else:
                up, down = edge(me)
                b = jnp.where(up, blocks - 1, jnp.where(down, 0, -1))
                number, sure = jnp.where(up, 0, blocks - 1), False
            src_ref[done + s] = b
            safe = jnp.maximum(b, 0)
            at = pl.ds(pl.multiple_of(safe * BLOCK, BLOCK), BLOCK)
            query, grad, tile = scaled_ref[at, :], g_ref[at, :], stats_ref[safe]
            if not sure:
                query = jnp.where(b >= 0, query, jnp.zeros_like(query))
                grad = jnp.where(b >= 0, grad, jnp.zeros_like(grad))
                tile = jnp.where(b >= 0, tile, jnp.zeros_like(tile))
                number = jnp.where(b >= 0, number, 0)
            out[2 * s * BLOCK : (2 * s + 1) * BLOCK, :] = query
            out[(2 * s + 1) * BLOCK : (2 * s + 2) * BLOCK, :] = grad
            tiles.append(tile)
            marks.append(jnp.full((1, BLOCK), number, jnp.int32).astype(F32))
        done += total
        extra = out.shape[0] - (2 * BLOCK + STAT + 1) * total
        if extra:
            marks.append(jnp.zeros((extra, BLOCK), F32))
        out[2 * total * BLOCK :, :] = jnp.concatenate(tiles + marks, axis=0).astype(BF16)
    for copy in copies[4:]:
        copy.wait()
    for number in range(glob_ref.shape[0]):
        block = glob_ref[number]
        mine = block // blocks == me
        at = pl.ds(pl.multiple_of((block % blocks) * BLOCK, BLOCK), BLOCK)
        for turn, ref in enumerate((k_ref, v_ref)):
            first = (turn * glob_ref.shape[0] + number) * BLOCK
            rows = ref[at, :]
            own_ref[first : first + BLOCK, :] = jnp.where(mine, rows, jnp.zeros_like(rows))
    for b in range(blocks):
        rows = pl.ds(b * BLOCK, BLOCK)
        kt_ref[rows, :] = (k_ref[rows, :].astype(F32) * (1.0 / math.sqrt(width))).T.astype(BF16)


def window(heads, first, last, q_ref, g_ref, stats_ref, k_ref, v_ref, kt_ref, *rest):
    dqt_ref, dk_ref, dv_ref = rest[-3:]
    blocks = q_ref.shape[0] // BLOCK
    if first == 0:
        dk_ref[...] = jnp.zeros_like(dk_ref)
        dv_ref[...] = jnp.zeros_like(dv_ref)
    for b in range(first, last):
        rows = pl.ds(b * BLOCK, BLOCK)
        q_bd, g_bd = by_head(q_ref[rows, :], heads), by_head(g_ref[rows, :], heads)
        norm, delta = stat_rows(stats_ref[b], heads)
        total = None
        for j in range(max(b - 1, 0), min(b + 2, blocks)):
            at = pl.ds(j * BLOCK, BLOCK)
            weights_low, scores_low = weigh(k_ref[at, :], v_ref[at, :], q_bd, g_bd, norm, delta)
            term = grad_query_t(kt_ref[at, :], scores_low, heads)
            total = term if total is None else total + term
            dk_ref[at, :] += dot(scores_low, q_bd)
            dv_ref[at, :] += dot(weights_low, g_bd)
        dqt_ref[rows, :] = total


def globals_(heads, q_ref, g_ref, stats_ref, shared_ref, _, dqt_ref, part_ref, total_k, total_v):
    blocks = q_ref.shape[0] // BLOCK
    head_size = q_ref.shape[1] // heads
    rows = shared_ref.shape[0] // 2
    key_rows, value_rows = shared_ref[:rows, :], shared_ref[rows:, :]
    keys_t = (key_rows.astype(F32) * (1.0 / math.sqrt(head_size))).T.astype(BF16)
    for b in range(blocks):
        at = pl.ds(b * BLOCK, BLOCK)
        q_bd, g_bd = by_head(q_ref[at, :], heads), by_head(g_ref[at, :], heads)
        norm, delta = stat_rows(stats_ref[b], heads)
        weights_low, scores_low = weigh(key_rows, value_rows, q_bd, g_bd, norm, delta)
        dqt_ref[at, :] += grad_query_t(keys_t, scores_low, heads)
        grad_key, grad_value = dot(scores_low, q_bd), dot(weights_low, g_bd)
        if b == 0:
            total_k[...] = grad_key
            total_v[...] = grad_value
        else:
            total_k[...] += grad_key
            total_v[...] += grad_value
    part_ref[:rows, :] = total_k[...].astype(BF16)
    part_ref[rows:, :] = total_v[...].astype(BF16)


def randoms(heads, slots, refs):
    many = len(slots)
    in_refs, (k_ref, v_ref, kt_ref) = refs[:many], refs[many : many + 3]
    ret_refs, (dk_ref, dv_ref) = refs[many + 5 : 2 * many + 5], refs[2 * many + 5 :]

    def partner(in_ref, ret_ref, total):
        tail = in_ref[2 * total * BLOCK :, :].astype(F32)
        for s in range(total):
            mark = STAT * total + s
            number = jnp.max(tail[mark : mark + 1]).astype(jnp.int32)
            at = pl.ds(pl.multiple_of(number * BLOCK, BLOCK), BLOCK)
            query = in_ref[2 * s * BLOCK : (2 * s + 1) * BLOCK, :]
            grad = in_ref[(2 * s + 1) * BLOCK : (2 * s + 2) * BLOCK, :]
            q_bd, g_bd = by_head(query, heads), by_head(grad, heads)
            norm, delta = stat_rows(tail[s * STAT : (s + 1) * STAT], heads)
            weights_low, scores_low = weigh(k_ref[at, :], v_ref[at, :], q_bd, g_bd, norm, delta)
            ret_ref[s * BLOCK : (s + 1) * BLOCK, :] = grad_query_t(kt_ref[at, :], scores_low, heads).astype(BF16)
            dk_ref[at, :] += dot(scores_low, q_bd)
            dv_ref[at, :] += dot(weights_low, g_bd)

    for in_ref, ret_ref, total in zip(in_refs, ret_refs, slots):
        if len(in_ref.shape) == 2:
            partner(in_ref, ret_ref, total)
        else:
            pl.loop(0, in_ref.shape[0])(lambda n, a=in_ref, b=ret_ref, c=total: partner(a.at[n], b.at[n], c))


def finish_keys(dk_in, dv_in, total_ref, glob_ref, dk_ref, dv_ref, sum_k, sum_v):
    blocks = dk_in.shape[0] // BLOCK
    me = lax.axis_index("seq")
    many = glob_ref.shape[0]
    sum_k[...] = dk_in[...]
    sum_v[...] = dv_in[...]
    for number in range(many):
        block = glob_ref[number]

        @pl.when(block // blocks == me)
        def _():
            at = pl.ds(pl.multiple_of((block % blocks) * BLOCK, BLOCK), BLOCK)
            for turn, ref in enumerate((sum_k, sum_v)):
                first = (turn * many + number) * BLOCK
                ref[at, :] += total_ref[first : first + BLOCK, :].astype(F32)

    dk_ref[...] = sum_k[...].astype(BF16)
    dv_ref[...] = sum_v[...].astype(BF16)


def finish_queries(slots, refs):
    many = len(slots)
    dqt_ref, src_ref, ret_refs, (out_ref, total) = refs[0], refs[1], refs[2 : 2 + many], refs[-2:]
    blocks = dqt_ref.shape[0] // BLOCK
    total[...] = dqt_ref[...]
    done = 0
    for ref, many_slots in zip(ret_refs, slots):
        parts = [ref] if len(ref.shape) == 2 else [ref.at[n] for n in range(ref.shape[0])]
        for part in parts:
            for s in range(many_slots):
                b = src_ref[done]
                done += 1

                @pl.when(b >= 0)
                def _():
                    rows = pl.ds(pl.multiple_of(b * BLOCK, BLOCK), BLOCK)
                    total[rows, :] += part[s * BLOCK : (s + 1) * BLOCK, :].astype(F32)

    for b in range(blocks):
        rows = pl.ds(b * BLOCK, BLOCK)
        out_ref[rows, :] = total[rows, :].T.astype(BF16)


def shards(
    queries, keys, values, outputs, d_outputs, log_norm, rand_owner, rand_local, glob_blocks
):
    tokens, features = queries.shape
    heads = log_norm.shape[0]
    blocks = tokens // BLOCK
    many = glob_blocks.shape[0]
    owners = lax.axis_size("seq")
    references = blocks * rand_owner.shape[1]
    capacity = max(2, (references + owners - 1) // owners)
    by_permute = owners == 8
    whole = jax.ShapeDtypeStruct((tokens, features), BF16)
    wide = jax.ShapeDtypeStruct((tokens, features), F32)

    if by_permute:
        plan = [
            (capacity, (lambda me, k=k: ((me ^ k) == me + 1, (me ^ k) == me - 1)) if k in (1, 3, 7) else "xor")
            for k in range(owners)
        ]
    else:
        plan = [(capacity, None)] * owners
        plan.append((0, lambda me: (me < owners - 1, me < 0)))
        plan.append((0, lambda me: (me < 0, me > 0)))
    slots = [n + (edge not in (None, "xor")) for n, edge in plan]

    packed = call(
        lambda *refs: pack(heads, plan, refs),
        [
            whole,
            jax.ShapeDtypeStruct((blocks, STAT, BLOCK), F32),
            jax.ShapeDtypeStruct((2 * many * BLOCK, features), BF16),
            whole,
            jax.ShapeDtypeStruct((sum(slots),), jnp.int32),
        ]
        + [jax.ShapeDtypeStruct((message_rows(n), features), BF16) for n in slots],
        [VMEM] * 4 + [SMEM] + [VMEM] * len(plan),
        [HBM] * 6 + [SMEM] * 3,
        [pltpu.VMEM((tokens, features), BF16)] * 5
        + [
            pltpu.VMEM(log_norm.shape, F32),
            pltpu.SemaphoreType.DMA((6,)),
            pltpu.SMEM((owners,), jnp.int32),
            pltpu.SMEM((owners * capacity,), jnp.int32),
            pltpu.SMEM((owners * capacity,), jnp.int32),
        ],
        "pack",
        limit=LIMIT,
    )(*(pltpu.with_memory_space_constraint(x, pltpu.HBM) for x in (queries, d_outputs, outputs, keys, values, log_norm)), rand_owner.T, rand_local.T, glob_blocks)
    scaled, stats, own, keys_t, source = packed[:5]
    outgoing = packed[5:]

    def swap(array, k):
        return lax.ppermute(array, "seq", [(i, i ^ k) for i in range(owners)])

    def add_globals(shared, dqt):
        return call(
            functools.partial(globals_, heads),
            [wide, jax.ShapeDtypeStruct(own.shape, BF16)],
            [VMEM] * 2,
            [VMEM] * 5,
            [pltpu.VMEM((many * BLOCK, features), F32)] * 2,
            "globals",
            {4: 0},
        )(scaled, d_outputs, stats, shared, dqt)

    def owned(taken, counts, dk, dv):
        shapes = [
            jax.ShapeDtypeStruct(a.shape[:-2] + (n * BLOCK, features), BF16) for a, n in zip(taken, counts)
        ]
        size = len(taken)
        outs = call(
            lambda *refs: randoms(heads, counts, refs),
            shapes + [wide, wide],
            [VMEM] * (size + 2),
            [VMEM] * (size + 5),
            [],
            "randoms",
            {size + 3: size, size + 4: size + 1},
        )(*taken, keys, values, keys_t, dk, dv)
        return outs[:size], outs[size], outs[size + 1]

    def add_window(stats):
        running = ()
        cuts = [blocks * n // PIECES for n in range(PIECES + 1)]
        for first, last in zip(cuts[:-1], cuts[1:]):
            running = call(
                functools.partial(window, heads, first, last),
                [wide] * 3,
                [VMEM] * 3,
                [VMEM] * (6 + len(running)),
                [],
                "window",
                {6 + n: n for n in range(len(running))},
            )(scaled, d_outputs, stats, keys, values, keys_t, *running)
        return running

    if by_permute:
        made = {}

        def gated(name, array):
            return after(array, *[get(other) for other in GATES.get(name, ())])

        def get(name):
            if name not in made:
                made[name] = None
                made[name] = make(name)
            if made[name] is None:
                raise ValueError("cycle")
            return made[name]

        def make(name):
            kind, number = name[0], int(name[1:] or 0)
            if kind == "F":
                return swap(gated(name, outgoing[number]), number) if number else outgoing[0]
            if kind == "G":
                if number == 0:
                    return own
                base = get(f"G{number - 1}")
                return base + swap(gated(name, base), HOPS["G"][number - 1])
            if kind == "P":
                if number == 0:
                    return get("g")[1]
                base = get(f"P{number - 1}")
                other = swap(gated(name, base), HOPS["P"][number - 1])
                return (base.astype(F32) + other.astype(F32)).astype(BF16)
            if kind == "W":
                return add_window(gated(name, stats))
            if kind == "g":
                return add_globals(gated(name, get("G3")), get("W")[0])
            if kind == "R":
                before = get(f"R{number - 1}")[1:] if number else get("W")[1:]
                group = GROUPS[number]
                before = (gated(name, before[0]), before[1])
                return owned([get(f"F{k}") for k in group], [slots[k] for k in group], *before)
            if kind == "r":
                at = [n for n, group in enumerate(GROUPS) if number in group][0]
                back = get(f"R{at}")[0][GROUPS[at].index(number)]
                return swap(gated(name, back), number) if number else back

        rets = [get(f"r{k}") for k in range(owners)]
        _, dk, dv = get(f"R{len(GROUPS) - 1}")
        dqt = get("g")[0]
        part = get("P3")
        ret_slots = slots
    else:
        forward = [(i, i + 1) for i in range(owners - 1)]
        backward = [(j, i) for i, j in forward]
        everyone = lax.all_to_all(
            jnp.stack(outgoing[:owners]), "seq", split_axis=0, concat_axis=0, tiled=True
        )
        from_before = lax.ppermute(outgoing[owners], "seq", forward)
        from_after = lax.ppermute(outgoing[owners + 1], "seq", backward)
        shared = own
        step = 1
        while step < owners:
            shared = shared + swap(shared, step)
            step *= 2
        dqt, dk, dv = add_window(stats)
        dqt, part = add_globals(shared, dqt)
        step = 1
        while step < owners:
            part = (part.astype(F32) + swap(part, step).astype(F32)).astype(BF16)
            step *= 2
        backs, dk, dv = owned([everyone, from_before, from_after], [capacity, 1, 1], dk, dv)
        rets = [
            lax.all_to_all(backs[0], "seq", split_axis=0, concat_axis=0, tiled=True),
            lax.ppermute(backs[1], "seq", backward),
            lax.ppermute(backs[2], "seq", forward),
        ]
        ret_slots = [capacity, 1, 1]

    d_keys, d_values = call(
        finish_keys,
        [whole, whole],
        [VMEM] * 2,
        [VMEM] * 3 + [SMEM],
        [pltpu.VMEM((tokens, features), F32)] * 2,
        "finish_keys",
    )(dk, dv, part, glob_blocks)
    d_queries = call(
        lambda *refs: finish_queries(ret_slots, refs),
        whole,
        VMEM,
        [VMEM, SMEM] + [VMEM] * len(rets),
        [pltpu.VMEM((tokens, features), F32)],
        "finish_queries",
    )(after(dqt, d_keys), source, *rets)
    return d_queries, d_keys, d_values


def solution(mesh):
    placed = (
        P("seq", "head"),
        P("seq", "head"),
        P("seq", "head"),
        P("seq", "head"),
        P("seq", "head"),
        P("head", "seq"),
        P("seq", None),
        P("seq", None),
        P(),
    )
    return jax.shard_map(
        shards,
        mesh=mesh,
        in_specs=placed,
        out_specs=(P("seq", "head"), P("seq", "head"), P("seq", "head")),
        check_vma=False,
    )
```

time: 114 us -> 84.1 us (0.74)
  waiting for transfers between devices: 39.4 us -> 22.6 us
  starting transfers between devices: 47.4 us -> 36.1 us
  local copies, waits for them, and re-layouts: 4.34 us -> 1.44 us
    ppermute x20, waiting for transfers between devices: 38.5 us -> 22.6 us  [swap(): return lax.ppermute(array, 'seq', [(i, i ^ k) for i in range(owners)])]
    ppermute x20, starting transfers between devices: 42.6 us -> 36.1 us  [swap(): return lax.ppermute(array, 'seq', [(i, i ^ k) for i in range(owners)])]
    ppermute x2 -> x0, starting transfers between devices: 4.71 us -> none  [the longest x1 3.42 us: shards(): before = lax.ppermute(up, 'seq', forward)]
    unnamed x20 -> x14, local copies, waits for them, and re-layouts: 4.34 us -> 1.44 us
    pallas_call x13 -> x15, Pallas kernels: 20.2 us -> 21.1 us  [the longest x8 8.28 us: owned(): call(lambda *refs: randoms(heads, counts, refs), shapes + [wide, wide], [...]
  transfers between devices with their start and end apart: 22 -> 20, of which waited for: 8 -> 5; matrix products, arithmetic and copies ran while one was open for 0% -> 0% of each run, Pallas kernels for 14% -> 22%
where the time goes in v2:
time: 84.1 us; the launch traced here: 83.9 us
  starting transfers between devices  36.1 us (43%)
  Pallas kernels  22.6 us (27%)
  waiting for transfers between devices  22.6 us (27%)
  local copies, waits for them, and re-layouts  1.44 us (2%)
  between operations  0.94 us (1%)
    ppermute x20, starting transfers between devices, swap(): return lax.ppermute(array, 'seq', [(i, i ^ k) for i in range(owners)])  36.1 us
    ppermute x20, waiting for transfers between devices, swap(): return lax.ppermute(array, 'seq', [(i, i ^ k) for i in range(owners)])  22.6 us
    pallas_call x8, Pallas kernels, owned(): call(lambda *refs: randoms(heads, counts, refs), shapes + [wide, wide], [...  8.28 us
    pallas_call x4, Pallas kernels, add_window(): call(functools.partial(window, heads, first, last), [wide] * 3, [VMEM] *...  5.82 us
    pallas_call x1, Pallas kernels, shards(): call(lambda *refs: pack(heads, plan, refs), [whole, jax.ShapeDtypeStruct(...  2.76 us
    pallas_call x1, Pallas kernels, add_globals(): call(functools.partial(globals_, heads), [wide, jax.ShapeDtypeStruct(own....  2.54 us
    pallas_call x1, Pallas kernels, shards(): call(lambda *refs: finish_queries(ret_slots, refs), whole, VMEM, [VMEM, S...  1.72 us
  transfers between devices with their start and end apart: 20, of which 5 were waited for; matrix products, arithmetic and copies ran while one was open for 0% of the time, Pallas kernels for 22%

profile of v2, /device:TPU:0, one launch (start us, length us, event | category | flops | bytes accessed | tf_op | source)
XLA Modules:
  0.0 83.9 jit_solution(16731579965580815288)
XLA Ops:
  0.7 0.7 copy-done.3
  1.3 0.7 copy-done.4
  2.0 2.8 %pack.1 = (bf16[1024,128]{1,0:T(8,128)(2,1)S(1)}, f32[8,8,128]{2,1,0:T(8,128)S(1)}, bf16[512,128]{1,0:T(8,128)(2,1)S(1)}, bf16[1024,128]{1,0:T(8,128)(2,1)S(1)},...) custom-call(bf16[1024,128]{1,0:T(8,128)(2,1)} %refs_0_.1, ...), custom_call_target="tpu_custom_call" | custom-call | tf_op jit(solution)/shard_map/pack/pallas_call | solution.py:326
  4.8 0.0 copy-start
  4.8 4.1 %collective-permute-start = (bf16[512,128]{1,0:T(8,128)(2,1)S(1)}, bf16[512,128]{1,0:T(8,128)(2,1)S(1)}, u32[]{:S(2)}, u32[]{:S(2)}) collective-permute-start(bf16[512,128]{1,0:T(8,128)(2,1)S(1)} %get-tuple-element.72), channel_id=1, source_target_pairs={{0,16},{4,20},{8,24},{12,28},{16,0},{20,4},{24,8},{28,12},{1,17},{... | collective-permute-start | bytes 393224 | tf_op jit(solution)/shard_map/ppermute | solution.py:353
  8.9 0.1 collective-permute-start.5
  9.0 1.8 %collective-permute-start.9 = (bf16[1072,128]{1,0:T(8,128)(2,1)S(1)}, bf16[1072,128]{1,0:T(8,128)(2,1)S(1)}, u32[]{:S(2)}, u32[]{:S(2)}) collective-permute-start(bf16[1072,128]{1,0:T(8,128)(2,1)S(1)} %get-tuple-element.102), channel_id=1, source_target_pairs={{0,4},{4,0},{8,12},{12,8},{16,20},{20,16},{24,28},{28,24},{1,5},{5... | collective-permute-start | bytes 823304 | tf_op jit(solution)/shard_map/ppermute | solution.py:353
  10.7 9.7 %collective-permute-done = bf16[512,128]{1,0:T(8,128)(2,1)S(1)} collective-permute-done((bf16[512,128]{1,0:T(8,128)(2,1)S(1)}, bf16[512,128]{1,0:T(8,128)(2,1)S(1)}, u32[]{:S(2)}, u32[]{:S(2)}) %collective-permute-start) | collective-permute-done | bytes 131104 | tf_op jit(solution)/shard_map/ppermute | solution.py:353
  20.5 0.1 collective-permute-start.1
  20.5 4.3 %collective-permute-start.3 = (bf16[800,128]{1,0:T(8,128)(2,1)S(1)}, bf16[800,128]{1,0:T(8,128)(2,1)S(1)}, u32[]{:S(2)}, u32[]{:S(2)}) collective-permute-start(bf16[800,128]{1,0:T(8,128)(2,1)S(1)} %get-tuple-element.88), channel_id=1, source_target_pairs={{0,20},{4,16},{8,28},{12,24},{16,4},{20,0},{24,12},{28,8},{1,21},{... | collective-permute-start | bytes 614408 | tf_op jit(solution)/shard_map/ppermute | solution.py:353
  24.8 1.3 %window.4 = (f32[1024,128]{1,0:T(8,128)S(1)}, f32[1024,128]{1,0:T(8,128)S(1)}, f32[1024,128]{1,0:T(8,128)S(1)}) custom-call(bf16[1024,128]{1,0:T(8,128)(2,1)S(1)} %get-tuple-element.70.q_ref, bf16[1024,128]{1,0:T(8,128)(2,1)S(1)} %copy-done, f32[8,8,128]{2,1,0:T(8,128)S(1)} %get-tuple-element.73.stats_ref, bf16[1024,128]{1,0:T(8,128)(2,1)S(1)} %copy-done.1, ...), custom_call_target="tpu_custom_call" | custom-call | flops 3449999872 | tf_op jit(solution)/shard_map/window/pallas_call | solution.py:386
  26.2 1.6 %window.5 = (f32[1024,128]{1,0:T(8,128)S(1)}, f32[1024,128]{1,0:T(8,128)S(1)}, f32[1024,128]{1,0:T(8,128)S(1)}) custom-call(bf16[1024,128]{1,0:T(8,128)(2,1)S(1)} %get-tuple-element.70.q_ref, bf16[1024,128]{1,0:T(8,128)(2,1)S(1)} %copy-done, ...), custom_call_target="tpu_custom_call", output_to_operand_aliasing={{0}: (6, {}), {1}: (7, {}), {2}: (8, {})} | custom-call | flops 3449999872 | tf_op jit(solution)/shard_map/window/pallas_call | solution.py:386
  27.8 1.6 %window.6 = (f32[1024,128]{1,0:T(8,128)S(1)}, f32[1024,128]{1,0:T(8,128)S(1)}, f32[1024,128]{1,0:T(8,128)S(1)}) custom-call(bf16[1024,128]{1,0:T(8,128)(2,1)S(1)} %get-tuple-element.70.q_ref, bf16[1024,128]{1,0:T(8,128)(2,1)S(1)} %copy-done, ...), custom_call_target="tpu_custom_call", output_to_operand_aliasing={{0}: (6, {}), {1}: (7, {}), {2}: (8, {})} | custom-call | flops 3449999872 | tf_op jit(solution)/shard_map/window/pallas_call | solution.py:386
  29.4 1.3 %window.7 = (f32[1024,128]{1,0:T(8,128)S(1)}, f32[1024,128]{1,0:T(8,128)S(1)}, f32[1024,128]{1,0:T(8,128)S(1)}) custom-call(bf16[1024,128]{1,0:T(8,128)(2,1)S(1)} %get-tuple-element.70.q_ref, bf16[1024,128]{1,0:T(8,128)(2,1)S(1)} %copy-done, ...), custom_call_target="tpu_custom_call", output_to_operand_aliasing={{0}: (6, {}), {1}: (7, {}), {2}: (8, {})} | custom-call | flops 3449999872 | tf_op jit(solution)/shard_map/window/pallas_call | solution.py:386
  30.7 0.0 collective-permute-done.5.refs_0_
  30.7 1.0 %collective-permute-start.6 = (bf16[1072,128]{1,0:T(8,128)(2,1)S(1)}, bf16[1072,128]{1,0:T(8,128)(2,1)S(1)}, u32[]{:S(2)}, u32[]{:S(2)}) collective-permute-start(bf16[1072,128]{1,0:T(8,128)(2,1)S(1)} %get-tuple-element.92), channel_id=1, source_target_pairs={{0,28},{4,24},{8,20},{12,16},{16,12},{20,8},{24,4},{28,0},{1,29},{... | collective-permute-start | bytes 823304 | tf_op jit(solution)/shard_map/ppermute | solution.py:353
  31.7 0.9 %randoms.8 = (bf16[384,128]{1,0:T(8,128)(2,1)S(1)}, f32[1024,128]{1,0:T(8,128)S(1)}, f32[1024,128]{1,0:T(8,128)S(1)}) custom-call(bf16[800,128]{1,0:T(8,128)(2,1)S(1)} %collective-permute-done.5.refs_0_, bf16[1024,128]{1,0:T(8,128)(2,1)S(1)} %copy-done.1, bf16[1024,128]{1,0:T(8,128)(2,1)S(1)} %copy-done.2, ...), custom_call_target="tpu_custom_call", output_to_operand_aliasing={{1}: (4, {}), {2}: (5, {})} | custom-call | flops 3449999872 | tf_op jit(solution)/shard_map/randoms/pallas_call | solution.py:371
  32.7 0.6 collective-permute-start.11
  33.3 0.0 collective-permute-done.1
  33.3 1.6 %collective-permute-start.2 = (bf16[512,128]{1,0:T(8,128)(2,1)S(1)}, bf16[512,128]{1,0:T(8,128)(2,1)S(1)}, u32[]{:S(2)}, u32[]{:S(2)}) collective-permute-start(bf16[512,128]{1,0:T(8,128)(2,1)S(1)} %add.19), channel_id=1, source_target_pairs={{0,4},{4,0},{8,12},{12,8},{16,20},{20,16},{24,28},{28,24},{1,5},{5... | collective-permute-start | bytes 393224 | tf_op jit(solution)/shard_map/ppermute | solution.py:353
  34.9 0.9 %randoms.9 = (bf16[384,128]{1,0:T(8,128)(2,1)S(1)}, f32[1024,128]{1,0:T(8,128)S(1)}, f32[1024,128]{1,0:T(8,128)S(1)}) custom-call(bf16[800,128]{1,0:T(8,128)(2,1)S(1)} %get-tuple-element.103.refs_0_, bf16[1024,128]{1,0:T(8,128)(2,1)S(1)} %copy-done.1, bf16[1024,128]{1,0:T(8,128)(2,1)S(1)} %copy-done.2, ...), custom_call_target="tpu_custom_call", output_to_operand_aliasing={{1}: (4, {}), {2}: (5, {})} | custom-call | flops 3449999872 | tf_op jit(solution)/shard_map/randoms/pallas_call | solution.py:371
  36.0 9.6 %collective-permute-start.7 = (bf16[800,128]{1,0:T(8,128)(2,1)S(1)}, bf16[800,128]{1,0:T(8,128)(2,1)S(1)}, u32[]{:S(2)}, u32[]{:S(2)}) collective-permute-start(bf16[800,128]{1,0:T(8,128)(2,1)S(1)} %get-tuple-element.99), channel_id=1, source_target_pairs={{0,24},{4,28},{8,16},{12,20},{16,8},{20,12},{24,0},{28,4},{1,25},{... | collective-permute-start | bytes 614408 | tf_op jit(solution)/shard_map/ppermute | solution.py:353
  45.6 0.9 %randoms.10 = (bf16[384,128]{1,0:T(8,128)(2,1)S(1)}, f32[1024,128]{1,0:T(8,128)S(1)}, f32[1024,128]{1,0:T(8,128)S(1)}) custom-call(bf16[800,128]{1,0:T(8,128)(2,1)S(1)} %collective-permute-done.3.refs_0_, bf16[1024,128]{1,0:T(8,128)(2,1)S(1)} %copy-done.1, bf16[1024,128]{1,0:T(8,128)(2,1)S(1)} %copy-done.2, ...), custom_call_target="tpu_custom_call", output_to_operand_aliasing={{1}: (4, {}), {2}: (5, {})} | custom-call | flops 3449999872 | tf_op jit(solution)/shard_map/randoms/pallas_call | solution.py:371
  46.5 0.0 collective-permute-done.2
  46.6 0.1 collective-permute-start.8
  46.7 2.5 %globals.1 = (f32[1024,128]{1,0:T(8,128)S(1)}, bf16[512,128]{1,0:T(8,128)(2,1)S(1)}) custom-call(bf16[1024,128]{1,0:T(8,128)(2,1)S(1)} %get-tuple-element.70.q_ref, bf16[1024,128]{1,0:T(8,128)(2,1)S(1)} %copy-done, f32[8,8,128]{2,1,0:T(8,128)S(1)} %get-tuple-element.73.stats_ref, ...), custom_call_target="tpu_custom_call", output_to_operand_aliasing={{0}: (4, {})} | custom-call | tf_op jit(solution)/shard_map/globals/pallas_call | solution.py:356
  49.2 0.0 collective-permute-done.9.refs_0_
  49.2 1.5 %collective-permute-start.10 = (bf16[512,128]{1,0:T(8,128)(2,1)S(1)}, bf16[512,128]{1,0:T(8,128)(2,1)S(1)}, u32[]{:S(2)}, u32[]{:S(2)}) collective-permute-start(bf16[512,128]{1,0:T(8,128)(2,1)S(1)} %get-tuple-element.121), channel_id=1, source_target_pairs={{0,4},{4,0},{8,12},{12,8},{16,20},{20,16},{24,28},{28,24},{1,5},{5... | collective-permute-start | bytes 393224 | tf_op jit(solution)/shard_map/ppermute | solution.py:353
  50.8 1.2 %randoms.11 = (bf16[512,128]{1,0:T(8,128)(2,1)S(1)}, f32[1024,128]{1,0:T(8,128)S(1)}, f32[1024,128]{1,0:T(8,128)S(1)}) custom-call(bf16[1072,128]{1,0:T(8,128)(2,1)S(1)} %collective-permute-done.9.refs_0_, bf16[1024,128]{1,0:T(8,128)(2,1)S(1)} %copy-done.1, bf16[1024,128]{1,0:T(8,128)(2,1)S(1)} %copy-done.2, ...), custom_call_target="tpu_custom_call", output_to_operand_aliasing={{1}: (4, {}), {2}: (5, {})} | custom-call | flops 3449999872 | tf_op jit(solution)/shard_map/randoms/pallas_call | solution.py:371
  52.0 2.3 %collective-permute-done.10 = bf16[512,128]{1,0:T(8,128)(2,1)S(1)} collective-permute-done((bf16[512,128]{1,0:T(8,128)(2,1)S(1)}, bf16[512,128]{1,0:T(8,128)(2,1)S(1)}, u32[]{:S(2)}, u32[]{:S(2)}) %collective-permute-start.10) | collective-permute-done | bytes 131104 | tf_op jit(solution)/shard_map/ppermute | solution.py:353
  54.3 2.9 %collective-permute-start.4 = (bf16[1072,128]{1,0:T(8,128)(2,1)S(1)}, bf16[1072,128]{1,0:T(8,128)(2,1)S(1)}, u32[]{:S(2)}, u32[]{:S(2)}) collective-permute-start(bf16[1072,128]{1,0:T(8,128)(2,1)S(1)} %get-tuple-element.89), channel_id=1, source_target_pairs={{0,12},{4,8},{8,4},{12,0},{16,28},{20,24},{24,20},{28,16},{1,13},{... | collective-permute-start | bytes 823304 | tf_op jit(solution)/shard_map/ppermute | solution.py:353
  57.2 0.0 collective-permute-done.11.refs_6_
  57.2 0.1 collective-permute-start.13
  57.3 1.5 %collective-permute-start.12 = (bf16[512,128]{1,0:T(8,128)(2,1)S(1)}, bf16[512,128]{1,0:T(8,128)(2,1)S(1)}, u32[]{:S(2)}, u32[]{:S(2)}) collective-permute-start(bf16[512,128]{1,0:T(8,128)(2,1)S(1)} %add_convert_fusion.2), channel_id=1, source_target_pairs={{0,8},{4,12},{8,0},{12,4},{16,24},{20,28},{24,16},{28,20},{1,9},{5... | collective-permute-start | bytes 393224 | tf_op jit(solution)/shard_map/ppermute | solution.py:353
  58.8 0.9 %randoms.12 = (bf16[384,128]{1,0:T(8,128)(2,1)S(1)}, f32[1024,128]{1,0:T(8,128)S(1)}, f32[1024,128]{1,0:T(8,128)S(1)}) custom-call(bf16[800,128]{1,0:T(8,128)(2,1)S(1)} %collective-permute-done.8.refs_0_, bf16[1024,128]{1,0:T(8,128)(2,1)S(1)} %copy-done.1, bf16[1024,128]{1,0:T(8,128)(2,1)S(1)} %copy-done.2, ...), custom_call_target="tpu_custom_call", output_to_operand_aliasing={{1}: (4, {}), {2}: (5, {})} | custom-call | flops 3449999872 | tf_op jit(solution)/shard_map/randoms/pallas_call | solution.py:371
  59.7 0.9 %randoms.13 = (bf16[384,128]{1,0:T(8,128)(2,1)S(1)}, f32[1024,128]{1,0:T(8,128)S(1)}, f32[1024,128]{1,0:T(8,128)S(1)}) custom-call(bf16[800,128]{1,0:T(8,128)(2,1)S(1)} %collective-permute-done.7.refs_0_, bf16[1024,128]{1,0:T(8,128)(2,1)S(1)} %copy-done.1, bf16[1024,128]{1,0:T(8,128)(2,1)S(1)} %copy-done.2, ...), custom_call_target="tpu_custom_call", output_to_operand_aliasing={{1}: (4, {}), {2}: (5, {})} | custom-call | flops 3449999872 | tf_op jit(solution)/shard_map/randoms/pallas_call | solution.py:371
  60.7 3.5 %collective-permute-start.15 = (bf16[384,128]{1,0:T(8,128)(2,1)S(1)}, bf16[384,128]{1,0:T(8,128)(2,1)S(1)}, u32[]{:S(2)}, u32[]{:S(2)}) collective-permute-start(bf16[384,128]{1,0:T(8,128)(2,1)S(1)} %get-tuple-element.130), channel_id=1, source_target_pairs={{0,24},{4,28},{8,16},{12,20},{16,8},{20,12},{24,0},{28,4},{1,25},{... | collective-permute-start | bytes 294920 | tf_op jit(solution)/shard_map/ppermute | solution.py:353
  64.2 1.2 %randoms.14 = (bf16[512,128]{1,0:T(8,128)(2,1)S(1)}, f32[1024,128]{1,0:T(8,128)S(1)}, f32[1024,128]{1,0:T(8,128)S(1)}) custom-call(bf16[1072,128]{1,0:T(8,128)(2,1)S(1)} %collective-permute-done.6.refs_0_, bf16[1024,128]{1,0:T(8,128)(2,1)S(1)} %copy-done.1, bf16[1024,128]{1,0:T(8,128)(2,1)S(1)} %copy-done.2, ...), custom_call_target="tpu_custom_call", output_to_operand_aliasing={{1}: (4, {}), {2}: (5, {})} | custom-call | flops 3449999872 | tf_op jit(solution)/shard_map/randoms/pallas_call | solution.py:371
  65.3 0.8 collective-permute-done.13.refs_7_
  66.1 1.0 %collective-permute-start.19 = (bf16[512,128]{1,0:T(8,128)(2,1)S(1)}, bf16[512,128]{1,0:T(8,128)(2,1)S(1)}, u32[]{:S(2)}, u32[]{:S(2)}) collective-permute-start(bf16[512,128]{1,0:T(8,128)(2,1)S(1)} %get-tuple-element.135), channel_id=1, source_target_pairs={{0,28},{4,24},{8,20},{12,16},{16,12},{20,8},{24,4},{28,0},{1,29},{... | collective-permute-start | bytes 393224 | tf_op jit(solution)/shard_map/ppermute | solution.py:353
  67.1 5.8 %collective-permute-done.12 = bf16[512,128]{1,0:T(8,128)(2,1)S(1)} collective-permute-done((bf16[512,128]{1,0:T(8,128)(2,1)S(1)}, bf16[512,128]{1,0:T(8,128)(2,1)S(1)}, u32[]{:S(2)}, u32[]{:S(2)}) %collective-permute-start.12) | collective-permute-done | bytes 131104 | tf_op jit(solution)/shard_map/ppermute | solution.py:353
  73.0 0.1 collective-permute-start.14
  73.0 1.2 %randoms.15 = (bf16[512,128]{1,0:T(8,128)(2,1)S(1)}, f32[1024,128]{1,0:T(8,128)S(1)}, f32[1024,128]{1,0:T(8,128)S(1)}) custom-call(bf16[1072,128]{1,0:T(8,128)(2,1)S(1)} %collective-permute-done.4.refs_0_, bf16[1024,128]{1,0:T(8,128)(2,1)S(1)} %copy-done.1, bf16[1024,128]{1,0:T(8,128)(2,1)S(1)} %copy-done.2, ...), custom_call_target="tpu_custom_call", output_to_operand_aliasing={{1}: (4, {}), {2}: (5, {})} | custom-call | flops 3449999872 | tf_op jit(solution)/shard_map/randoms/pallas_call | solution.py:371
  74.2 0.1 collective-permute-start.18
  74.3 2.3 %collective-permute-start.16 = (bf16[512,128]{1,0:T(8,128)(2,1)S(1)}, bf16[512,128]{1,0:T(8,128)(2,1)S(1)}, u32[]{:S(2)}, u32[]{:S(2)}) collective-permute-start(bf16[512,128]{1,0:T(8,128)(2,1)S(1)} %get-tuple-element.131), channel_id=1, source_target_pairs={{0,4},{4,0},{8,12},{12,8},{16,20},{20,16},{24,28},{28,24},{1,5},{5... | collective-permute-start | bytes 393224 | tf_op jit(solution)/shard_map/ppermute | solution.py:353
  76.7 4.0 %collective-permute-done.14 = bf16[512,128]{1,0:T(8,128)(2,1)S(1)} collective-permute-done((bf16[512,128]{1,0:T(8,128)(2,1)S(1)}, bf16[512,128]{1,0:T(8,128)(2,1)S(1)}, u32[]{:S(2)}, u32[]{:S(2)}) %collective-permute-start.14) | collective-permute-done | bytes 131104 | tf_op jit(solution)/shard_map/ppermute | solution.py:353
  80.7 1.4 %finish_keys.1 = (bf16[1024,128]{1,0:T(8,128)(2,1)}, bf16[1024,128]{1,0:T(8,128)(2,1)}) custom-call(f32[1024,128]{1,0:T(8,128)S(1)} %get-tuple-element.119.dk_in, f32[1024,128]{1,0:T(8,128)S(1)} %get-tuple-element.120.dv_in, bf16[512,128]{1,0:T(8,128)(2,1)S(1)} %add_convert_fusion.total_ref, s32[2]{0:T(128)S(1)} %copy-done.5), custom_call_target="tpu_custom_call" | custom-call | flops 3449999872 | tf_op jit(solution)/shard_map/finish_keys/pallas_call | solution.py:472
  82.1 1.7 %finish_queries.1 = bf16[1024,128]{1,0:T(8,128)(2,1)} custom-call(f32[1024,128]{1,0:T(8,128)S(1)} %get-tuple-element.126.refs_0_, s32[27]{0:T(128)S(1)} %get-tuple-element.127.refs_1_, bf16[384,128]{1,0:T(8,128)(2,1)S(1)} %get-tuple-element.108.refs_2_, bf16[512,128]{1,0:T(8,128)(2,1)S(1)} %collective-permute-done.16.refs_3_, ...), custom_call_target="tpu_custom_call" | custom-call | flops 3449999872 | tf_op jit(solution)/shard_map/finish_queries/pallas_call | solution.py:480
  (28 shorter events, 0.3 us)
Async XLA Ops:
  0.6 0.7 copy-start.3
  0.6 0.7 copy-start.5
  1.3 0.7 copy-start.4
  2.0 22.8 %copy-start.1 = (bf16[1024,128]{1,0:T(8,128)(2,1)S(1)}, bf16[1024,128]{1,0:T(8,128)(2,1)}, u32[]{:S(2)}) copy-start(bf16[1024,128]{1,0:T(8,128)(2,1)} %refs_1_.17) | copy-start | bytes 786436
  2.0 22.8 %copy-start.2 = (bf16[1024,128]{1,0:T(8,128)(2,1)S(1)}, bf16[1024,128]{1,0:T(8,128)(2,1)}, u32[]{:S(2)}) copy-start(bf16[1024,128]{1,0:T(8,128)(2,1)} %refs_2_.17) | copy-start | bytes 786436
  4.8 20.1 %copy-start = (bf16[1024,128]{1,0:T(8,128)(2,1)S(1)}, bf16[1024,128]{1,0:T(8,128)(2,1)}, u32[]{:S(2)}) copy-start(bf16[1024,128]{1,0:T(8,128)(2,1)} %g_ref.9) | copy-start | bytes 786436
  4.8 15.6 %collective-permute-start = (bf16[512,128]{1,0:T(8,128)(2,1)S(1)}, bf16[512,128]{1,0:T(8,128)(2,1)S(1)}, u32[]{:S(2)}, u32[]{:S(2)}) collective-permute-start(bf16[512,128]{1,0:T(8,128)(2,1)S(1)} %get-tuple-element.72), channel_id=1, source_target_pairs={{0,16},{4,20},{8,24},{12,28},{16,0},{20,4},{24,8},{28,12},{1,17},{... | collective-permute-start | bytes 393224 | tf_op jit(solution)/shard_map/ppermute | solution.py:353
  8.9 21.8 %collective-permute-start.5 = (bf16[800,128]{1,0:T(8,128)(2,1)S(1)}, bf16[800,128]{1,0:T(8,128)(2,1)S(1)}, u32[]{:S(2)}, u32[]{:S(2)}) collective-permute-start(bf16[800,128]{1,0:T(8,128)(2,1)S(1)} %get-tuple-element.91), channel_id=1, source_target_pairs={{0,16},{4,20},{8,24},{12,28},{16,0},{20,4},{24,8},{28,12},{1,17},{... | collective-permute-start | bytes 614408 | tf_op jit(solution)/shard_map/ppermute | solution.py:353
  9.0 40.3 %collective-permute-start.9 = (bf16[1072,128]{1,0:T(8,128)(2,1)S(1)}, bf16[1072,128]{1,0:T(8,128)(2,1)S(1)}, u32[]{:S(2)}, u32[]{:S(2)}) collective-permute-start(bf16[1072,128]{1,0:T(8,128)(2,1)S(1)} %get-tuple-element.102), channel_id=1, source_target_pairs={{0,4},{4,0},{8,12},{12,8},{16,20},{20,16},{24,28},{28,24},{1,5},{5... | collective-permute-start | bytes 823304 | tf_op jit(solution)/shard_map/ppermute | solution.py:353
  20.5 12.8 %collective-permute-start.1 = (bf16[512,128]{1,0:T(8,128)(2,1)S(1)}, bf16[512,128]{1,0:T(8,128)(2,1)S(1)}, u32[]{:S(2)}, u32[]{:S(2)}) collective-permute-start(bf16[512,128]{1,0:T(8,128)(2,1)S(1)} %add.18), channel_id=1, source_target_pairs={{0,8},{4,12},{8,0},{12,4},{16,24},{20,28},{24,16},{28,20},{1,9},{5... | collective-permute-start | bytes 393224 | tf_op jit(solution)/shard_map/ppermute | solution.py:353
  20.5 15.4 %collective-permute-start.3 = (bf16[800,128]{1,0:T(8,128)(2,1)S(1)}, bf16[800,128]{1,0:T(8,128)(2,1)S(1)}, u32[]{:S(2)}, u32[]{:S(2)}) collective-permute-start(bf16[800,128]{1,0:T(8,128)(2,1)S(1)} %get-tuple-element.88), channel_id=1, source_target_pairs={{0,20},{4,16},{8,28},{12,24},{16,4},{20,0},{24,12},{28,8},{1,21},{... | collective-permute-start | bytes 614408 | tf_op jit(solution)/shard_map/ppermute | solution.py:353
  30.7 26.6 %collective-permute-start.6 = (bf16[1072,128]{1,0:T(8,128)(2,1)S(1)}, bf16[1072,128]{1,0:T(8,128)(2,1)S(1)}, u32[]{:S(2)}, u32[]{:S(2)}) collective-permute-start(bf16[1072,128]{1,0:T(8,128)(2,1)S(1)} %get-tuple-element.92), channel_id=1, source_target_pairs={{0,28},{4,24},{8,20},{12,16},{16,12},{20,8},{24,4},{28,0},{1,29},{... | collective-permute-start | bytes 823304 | tf_op jit(solution)/shard_map/ppermute | solution.py:353
  32.7 24.5 %collective-permute-start.11 = (bf16[384,128]{1,0:T(8,128)(2,1)S(1)}, bf16[384,128]{1,0:T(8,128)(2,1)S(1)}, u32[]{:S(2)}, u32[]{:S(2)}) collective-permute-start(bf16[384,128]{1,0:T(8,128)(2,1)S(1)} %get-tuple-element.96), channel_id=1, source_target_pairs={{0,16},{4,20},{8,24},{12,28},{16,0},{20,4},{24,8},{28,12},{1,17},{... | collective-permute-start | bytes 294920 | tf_op jit(solution)/shard_map/ppermute | solution.py:353
  33.3 13.2 %collective-permute-start.2 = (bf16[512,128]{1,0:T(8,128)(2,1)S(1)}, bf16[512,128]{1,0:T(8,128)(2,1)S(1)}, u32[]{:S(2)}, u32[]{:S(2)}) collective-permute-start(bf16[512,128]{1,0:T(8,128)(2,1)S(1)} %add.19), channel_id=1, source_target_pairs={{0,4},{4,0},{8,12},{12,8},{16,20},{20,16},{24,28},{28,24},{1,5},{5... | collective-permute-start | bytes 393224 | tf_op jit(solution)/shard_map/ppermute | solution.py:353
  36.0 21.3 %collective-permute-start.7 = (bf16[800,128]{1,0:T(8,128)(2,1)S(1)}, bf16[800,128]{1,0:T(8,128)(2,1)S(1)}, u32[]{:S(2)}, u32[]{:S(2)}) collective-permute-start(bf16[800,128]{1,0:T(8,128)(2,1)S(1)} %get-tuple-element.99), channel_id=1, source_target_pairs={{0,24},{4,28},{8,16},{12,20},{16,8},{20,12},{24,0},{28,4},{1,25},{... | collective-permute-start | bytes 614408 | tf_op jit(solution)/shard_map/ppermute | solution.py:353
  46.6 12.2 %collective-permute-start.8 = (bf16[800,128]{1,0:T(8,128)(2,1)S(1)}, bf16[800,128]{1,0:T(8,128)(2,1)S(1)}, u32[]{:S(2)}, u32[]{:S(2)}) collective-permute-start(bf16[800,128]{1,0:T(8,128)(2,1)S(1)} %get-tuple-element.101), channel_id=1, source_target_pairs={{0,8},{4,12},{8,0},{12,4},{16,24},{20,28},{24,16},{28,20},{1,9},{5... | collective-permute-start | bytes 614408 | tf_op jit(solution)/shard_map/ppermute | solution.py:353
  49.2 5.0 %collective-permute-start.10 = (bf16[512,128]{1,0:T(8,128)(2,1)S(1)}, bf16[512,128]{1,0:T(8,128)(2,1)S(1)}, u32[]{:S(2)}, u32[]{:S(2)}) collective-permute-start(bf16[512,128]{1,0:T(8,128)(2,1)S(1)} %get-tuple-element.121), channel_id=1, source_target_pairs={{0,4},{4,0},{8,12},{12,8},{16,20},{20,16},{24,28},{28,24},{1,5},{5... | collective-permute-start | bytes 393224 | tf_op jit(solution)/shard_map/ppermute | solution.py:353
  54.3 18.8 %collective-permute-start.4 = (bf16[1072,128]{1,0:T(8,128)(2,1)S(1)}, bf16[1072,128]{1,0:T(8,128)(2,1)S(1)}, u32[]{:S(2)}, u32[]{:S(2)}) collective-permute-start(bf16[1072,128]{1,0:T(8,128)(2,1)S(1)} %get-tuple-element.89), channel_id=1, source_target_pairs={{0,12},{4,8},{8,4},{12,0},{16,28},{20,24},{24,20},{28,16},{1,13},{... | collective-permute-start | bytes 823304 | tf_op jit(solution)/shard_map/ppermute | solution.py:353
  57.2 8.9 %collective-permute-start.13 = (bf16[384,128]{1,0:T(8,128)(2,1)S(1)}, bf16[384,128]{1,0:T(8,128)(2,1)S(1)}, u32[]{:S(2)}, u32[]{:S(2)}) collective-permute-start(bf16[384,128]{1,0:T(8,128)(2,1)S(1)} %get-tuple-element.123), channel_id=1, source_target_pairs={{0,20},{4,16},{8,28},{12,24},{16,4},{20,0},{24,12},{28,8},{1,21},{... | collective-permute-start | bytes 294920 | tf_op jit(solution)/shard_map/ppermute | solution.py:353
  57.3 15.6 %collective-permute-start.12 = (bf16[512,128]{1,0:T(8,128)(2,1)S(1)}, bf16[512,128]{1,0:T(8,128)(2,1)S(1)}, u32[]{:S(2)}, u32[]{:S(2)}) collective-permute-start(bf16[512,128]{1,0:T(8,128)(2,1)S(1)} %add_convert_fusion.2), channel_id=1, source_target_pairs={{0,8},{4,12},{8,0},{12,4},{16,24},{20,28},{24,16},{28,20},{1,9},{5... | collective-permute-start | bytes 393224 | tf_op jit(solution)/shard_map/ppermute | solution.py:353
  60.7 13.6 %collective-permute-start.15 = (bf16[384,128]{1,0:T(8,128)(2,1)S(1)}, bf16[384,128]{1,0:T(8,128)(2,1)S(1)}, u32[]{:S(2)}, u32[]{:S(2)}) collective-permute-start(bf16[384,128]{1,0:T(8,128)(2,1)S(1)} %get-tuple-element.130), channel_id=1, source_target_pairs={{0,24},{4,28},{8,16},{12,20},{16,8},{20,12},{24,0},{28,4},{1,25},{... | collective-permute-start | bytes 294920 | tf_op jit(solution)/shard_map/ppermute | solution.py:353
  64.1 18.0 %collective-permute-start.17 = (bf16[384,128]{1,0:T(8,128)(2,1)S(1)}, bf16[384,128]{1,0:T(8,128)(2,1)S(1)}, u32[]{:S(2)}, u32[]{:S(2)}) collective-permute-start(bf16[384,128]{1,0:T(8,128)(2,1)S(1)} %get-tuple-element.132), channel_id=1, source_target_pairs={{0,8},{4,12},{8,0},{12,4},{16,24},{20,28},{24,16},{28,20},{1,9},{5... | collective-permute-start | bytes 294920 | tf_op jit(solution)/shard_map/ppermute | solution.py:353
  66.1 16.0 %collective-permute-start.19 = (bf16[512,128]{1,0:T(8,128)(2,1)S(1)}, bf16[512,128]{1,0:T(8,128)(2,1)S(1)}, u32[]{:S(2)}, u32[]{:S(2)}) collective-permute-start(bf16[512,128]{1,0:T(8,128)(2,1)S(1)} %get-tuple-element.135), channel_id=1, source_target_pairs={{0,28},{4,24},{8,20},{12,16},{16,12},{20,8},{24,4},{28,0},{1,29},{... | collective-permute-start | bytes 393224 | tf_op jit(solution)/shard_map/ppermute | solution.py:353
  73.0 7.7 %collective-permute-start.14 = (bf16[512,128]{1,0:T(8,128)(2,1)S(1)}, bf16[512,128]{1,0:T(8,128)(2,1)S(1)}, u32[]{:S(2)}, u32[]{:S(2)}) collective-permute-start(bf16[512,128]{1,0:T(8,128)(2,1)S(1)} %add_convert_fusion.1), channel_id=1, source_target_pairs={{0,16},{4,20},{8,24},{12,28},{16,0},{20,4},{24,8},{28,12},{1,17},{... | collective-permute-start | bytes 393224 | tf_op jit(solution)/shard_map/ppermute | solution.py:353
  74.2 7.9 %collective-permute-start.18 = (bf16[512,128]{1,0:T(8,128)(2,1)S(1)}, bf16[512,128]{1,0:T(8,128)(2,1)S(1)}, u32[]{:S(2)}, u32[]{:S(2)}) collective-permute-start(bf16[512,128]{1,0:T(8,128)(2,1)S(1)} %get-tuple-element.133), channel_id=1, source_target_pairs={{0,12},{4,8},{8,4},{12,0},{16,28},{20,24},{24,20},{28,16},{1,13},{... | collective-permute-start | bytes 393224 | tf_op jit(solution)/shard_map/ppermute | solution.py:353
  74.3 7.8 %collective-permute-start.16 = (bf16[512,128]{1,0:T(8,128)(2,1)S(1)}, bf16[512,128]{1,0:T(8,128)(2,1)S(1)}, u32[]{:S(2)}, u32[]{:S(2)}) collective-permute-start(bf16[512,128]{1,0:T(8,128)(2,1)S(1)} %get-tuple-element.131), channel_id=1, source_target_pairs={{0,4},{4,0},{8,12},{12,8},{16,20},{20,16},{24,28},{28,24},{1,5},{5... | collective-permute-start | bytes 393224 | tf_op jit(solution)/shard_map/ppermute | solution.py:353

commit v3 on v2

--- a/solution.py
+++ b/solution.py
@@ -19,8 +19,8 @@
 BF16 = jnp.bfloat16
 LIMIT = 24
 PIECES = 4
-COSTS = {'window': 3, 'randoms': 3, 'finish_keys': 3, 'finish_queries': 3}
-GATES = {'W': ['G1'], 'F5': ['G1'], 'F6': ['G2', 'R0'], 'F7': ['F4'], 'F2': ['F5'], 'F3': ['F5'], 'R1': ['G2'], 'R3': ['R1'], 'r6': ['r4'], 'r7': ['r5'], 'P2': ['F6', 'F7', 'r4'], 'P3': ['r5', 'F5'], 'r1': ['r6']}
+COSTS = {'window': 3, 'randoms': 3, 'finish': 3}
+GATES = {'W': ['G1'], 'F5': ['G1'], 'F6': ['R0'], 'F7': ['F4'], 'F2': ['F5'], 'F3': ['F5'], 'R1': ['G2'], 'R3': ['R1'], 'r6': ['r4'], 'r7': ['r5', 'F1', 'F6'], 'P2': ['F6', 'F7', 'r4'], 'P3': ['r5', 'F5'], 'r1': ['r6'], 'R0': ['G2']}
 GROUPS = [[4], [0], [5], [1], [2], [6], [7], [3]]
 HOPS = {'G': [4, 2, 1], 'P': [1, 2, 4]}
 
@@ -85,21 +85,41 @@
     return -(-((2 * BLOCK + STAT + 1) * slots) // 16) * 16
 
 
+def pick_globals(blocks, k_hbm, v_hbm, glob_ref, own_ref, sems):
+    many = glob_ref.shape[0]
+    me = lax.axis_index("seq")
+    own_ref[...] = jnp.zeros_like(own_ref)
+    for waiting in (False, True):
+        for number in range(many):
+            block = glob_ref[number]
+
+            @pl.when(block // blocks == me)
+            def _():
+                at = pl.ds(pl.multiple_of((block % blocks) * BLOCK, BLOCK), BLOCK)
+                for turn, ref in enumerate((k_hbm, v_hbm)):
+                    place = turn * many + number
+                    copy = pltpu.make_async_copy(
+                        ref.at[at, :], own_ref.at[pl.ds(place * BLOCK, BLOCK), :], sems.at[place]
+                    )
+                    copy.wait() if waiting else copy.start()
+
+
 def pack(heads, plan, refs):
-    q_hbm, g_hbm, o_hbm, k_hbm, v_hbm, norm_hbm, owner_ref, local_ref, glob_ref = refs[:9]
-    scaled_ref, stats_ref, own_ref, kt_ref, src_ref = refs[9:14]
-    out_refs = refs[14 : 14 + len(plan)]
-    q_ref, g_ref, o_ref, k_ref, v_ref, norm_ref, sems, count, source, place = refs[14 + len(plan) :]
+    q_hbm, g_hbm, o_hbm, k_hbm, norm_hbm, owner_hbm, local_hbm = refs[:7]
+    scaled_ref, stats_ref, kt_ref, src_ref = refs[7:11]
+    out_refs = refs[11 : 11 + len(plan)]
+    q_ref, g_ref, o_ref, k_ref, norm_ref, owner_ref, local_ref, sems, count, source, place = refs[11 + len(plan) :]
     copies = [
         pltpu.make_async_copy(a, b, sems.at[n])
         for n, (a, b) in enumerate(
             (
+                (owner_hbm, owner_ref),
+                (local_hbm, local_ref),
                 (g_hbm, g_ref),
                 (o_hbm, o_ref),
                 (norm_hbm, norm_ref),
                 (q_hbm, q_ref),
                 (k_hbm, k_ref),
-                (v_hbm, v_ref),
             )
         )
     ]
@@ -112,6 +132,8 @@
     fold = any(entry[1] == "xor" for entry in plan)
     most = max(entry[0] for entry in plan)
     randoms = sum(1 for entry in plan if entry[0])
+    for copy in copies[:2]:
+        copy.wait()
     for k in range(randoms):
         count[k] = 0
         for s in range(most):
@@ -125,7 +147,7 @@
             count[k] = s + 1
             source[k * most + s] = b
             place[k * most + s] = local_ref[r, b]
-    for copy in copies[:3]:
+    for copy in copies[2:5]:
         copy.wait()
     for b in range(blocks):
         rows = pl.ds(b * BLOCK, BLOCK)
@@ -136,7 +158,7 @@
         high = exact.astype(BF16).astype(F32)
         low = (exact - high).astype(BF16).astype(F32)
         stats_ref[b] = jnp.concatenate([high[:heads], low[:heads], high[heads:], low[heads:]], axis=0)
-    copies[3].wait()
+    copies[5].wait()
     scaled_ref[...] = q_ref[...] * jnp.asarray(1.0 / math.sqrt(width), BF16)
     full = blocks * per_block == randoms * most
     done = 0
@@ -169,16 +191,7 @@
         if extra:
             marks.append(jnp.zeros((extra, BLOCK), F32))
         out[2 * total * BLOCK :, :] = jnp.concatenate(tiles + marks, axis=0).astype(BF16)
-    for copy in copies[4:]:
-        copy.wait()
-    for number in range(glob_ref.shape[0]):
-        block = glob_ref[number]
-        mine = block // blocks == me
-        at = pl.ds(pl.multiple_of((block % blocks) * BLOCK, BLOCK), BLOCK)
-        for turn, ref in enumerate((k_ref, v_ref)):
-            first = (turn * glob_ref.shape[0] + number) * BLOCK
-            rows = ref[at, :]
-            own_ref[first : first + BLOCK, :] = jnp.where(mine, rows, jnp.zeros_like(rows))
+    copies[6].wait()
     for b in range(blocks):
         rows = pl.ds(b * BLOCK, BLOCK)
         kt_ref[rows, :] = (k_ref[rows, :].astype(F32) * (1.0 / math.sqrt(width))).T.astype(BF16)
@@ -255,12 +268,23 @@
             pl.loop(0, in_ref.shape[0])(lambda n, a=in_ref, b=ret_ref, c=total: partner(a.at[n], b.at[n], c))
 
 
-def finish_keys(dk_in, dv_in, total_ref, glob_ref, dk_ref, dv_ref, sum_k, sum_v):
+def finish(slots, refs):
+    dqt_ref, dk_in, dv_in, total_ref, glob_hbm, src_hbm = refs[:6]
+    ret_refs = refs[6 : 6 + len(slots)]
+    q_hbm, k_hbm, v_hbm, sum_q, sum_k, sum_v, q_out, k_out, v_out, glob_ref, src_ref, sems = refs[6 + len(slots) :]
     blocks = dk_in.shape[0] // BLOCK
+    many = glob_ref.shape[0]
     me = lax.axis_index("seq")
-    many = glob_ref.shape[0]
+    names = [
+        pltpu.make_async_copy(a, b, sems.at[n]) for n, (a, b) in enumerate(((glob_hbm, glob_ref), (src_hbm, src_ref)))
+    ]
+    for copy in names:
+        copy.start()
     sum_k[...] = dk_in[...]
     sum_v[...] = dv_in[...]
+    sum_q[...] = dqt_ref[...]
+    for copy in names:
+        copy.wait()
     for number in range(many):
         block = glob_ref[number]
 
@@ -271,15 +295,14 @@
                 first = (turn * many + number) * BLOCK
                 ref[at, :] += total_ref[first : first + BLOCK, :].astype(F32)
 
-    dk_ref[...] = sum_k[...].astype(BF16)
-    dv_ref[...] = sum_v[...].astype(BF16)
-
-
-def finish_queries(slots, refs):
-    many = len(slots)
-    dqt_ref, src_ref, ret_refs, (out_ref, total) = refs[0], refs[1], refs[2 : 2 + many], refs[-2:]
-    blocks = dqt_ref.shape[0] // BLOCK
-    total[...] = dqt_ref[...]
+    k_out[...] = sum_k[...].astype(BF16)
+    v_out[...] = sum_v[...].astype(BF16)
+    copies = [
+        pltpu.make_async_copy(a, b, sems.at[2 + n])
+        for n, (a, b) in enumerate(((k_out, k_hbm), (v_out, v_hbm), (q_out, q_hbm)))
+    ]
+    copies[0].start()
+    copies[1].start()
     done = 0
     for ref, many_slots in zip(ret_refs, slots):
         parts = [ref] if len(ref.shape) == 2 else [ref.at[n] for n in range(ref.shape[0])]
@@ -291,11 +314,14 @@
                 @pl.when(b >= 0)
                 def _():
                     rows = pl.ds(pl.multiple_of(b * BLOCK, BLOCK), BLOCK)
-                    total[rows, :] += part[s * BLOCK : (s + 1) * BLOCK, :].astype(F32)
+                    sum_q[rows, :] += part[s * BLOCK : (s + 1) * BLOCK, :].astype(F32)
 
     for b in range(blocks):
         rows = pl.ds(b * BLOCK, BLOCK)
-        out_ref[rows, :] = total[rows, :].T.astype(BF16)
+        q_out[rows, :] = sum_q[rows, :].T.astype(BF16)
+    copies[2].start()
+    for copy in copies:
+        copy.wait()
 
 
 def shards(
@@ -323,31 +349,42 @@
         plan.append((0, lambda me: (me < 0, me > 0)))
     slots = [n + (edge not in (None, "xor")) for n, edge in plan]
 
+    def in_hbm(*arrays):
+        return [pltpu.with_memory_space_constraint(array, pltpu.HBM) for array in arrays]
+
+    own = call(
+        functools.partial(pick_globals, blocks),
+        jax.ShapeDtypeStruct((2 * many * BLOCK, features), BF16),
+        VMEM,
+        [HBM] * 2 + [SMEM],
+        [pltpu.SemaphoreType.DMA((2 * many,))],
+        "pick_globals",
+    )(*in_hbm(keys, values), glob_blocks)
     packed = call(
         lambda *refs: pack(heads, plan, refs),
         [
             whole,
             jax.ShapeDtypeStruct((blocks, STAT, BLOCK), F32),
-            jax.ShapeDtypeStruct((2 * many * BLOCK, features), BF16),
             whole,
             jax.ShapeDtypeStruct((sum(slots),), jnp.int32),
         ]
         + [jax.ShapeDtypeStruct((message_rows(n), features), BF16) for n in slots],
-        [VMEM] * 4 + [SMEM] + [VMEM] * len(plan),
-        [HBM] * 6 + [SMEM] * 3,
-        [pltpu.VMEM((tokens, features), BF16)] * 5
+        [VMEM] * 3 + [SMEM] + [VMEM] * len(plan),
+        [HBM] * 7,
+        [pltpu.VMEM((tokens, features), BF16)] * 4
         + [
             pltpu.VMEM(log_norm.shape, F32),
-            pltpu.SemaphoreType.DMA((6,)),
+            pltpu.SMEM(rand_owner.shape[::-1], jnp.int32),
+            pltpu.SMEM(rand_local.shape[::-1], jnp.int32),
+            pltpu.SemaphoreType.DMA((7,)),
             pltpu.SMEM((owners,), jnp.int32),
             pltpu.SMEM((owners * capacity,), jnp.int32),
             pltpu.SMEM((owners * capacity,), jnp.int32),
         ],
         "pack",
-        limit=LIMIT,
-    )(*(pltpu.with_memory_space_constraint(x, pltpu.HBM) for x in (queries, d_outputs, outputs, keys, values, log_norm)), rand_owner.T, rand_local.T, glob_blocks)
-    scaled, stats, own, keys_t, source = packed[:5]
-    outgoing = packed[5:]
+    )(*in_hbm(queries, d_outputs, outputs, keys, log_norm, rand_owner.T, rand_local.T))
+    scaled, stats, keys_t, source = packed[:4]
+    outgoing = packed[4:]
 
     def swap(array, k):
         return lax.ppermute(array, "seq", [(i, i ^ k) for i in range(owners)])
@@ -398,7 +435,8 @@
         made = {}
 
         def gated(name, array):
-            return after(array, *[get(other) for other in GATES.get(name, ())])
+            others = [get(other) for other in GATES.get(name, ())]
+            return after(array, *[x if isinstance(x, jax.Array) else x[0] for x in others])
 
         def get(name):
             if name not in made:
@@ -419,14 +457,14 @@
                 return base + swap(gated(name, base), HOPS["G"][number - 1])
             if kind == "P":
                 if number == 0:
-                    return get("g")[1]
+                    return get("g")[0]
                 base = get(f"P{number - 1}")
                 other = swap(gated(name, base), HOPS["P"][number - 1])
                 return (base.astype(F32) + other.astype(F32)).astype(BF16)
             if kind == "W":
                 return add_window(gated(name, stats))
             if kind == "g":
-                return add_globals(gated(name, get("G3")), get("W")[0])
+                return add_globals(gated(name, get("G3")), get("W")[0])[::-1]
             if kind == "R":
                 before = get(f"R{number - 1}")[1:] if number else get("W")[1:]
                 group = GROUPS[number]
@@ -439,7 +477,7 @@
 
         rets = [get(f"r{k}") for k in range(owners)]
         _, dk, dv = get(f"R{len(GROUPS) - 1}")
-        dqt = get("g")[0]
+        dqt = get("g")[1]
         part = get("P3")
         ret_slots = slots
     else:
@@ -469,23 +507,20 @@
         ]
         ret_slots = [capacity, 1, 1]
 
-    d_keys, d_values = call(
-        finish_keys,
-        [whole, whole],
-        [VMEM] * 2,
-        [VMEM] * 3 + [SMEM],
-        [pltpu.VMEM((tokens, features), F32)] * 2,
-        "finish_keys",
-    )(dk, dv, part, glob_blocks)
-    d_queries = call(
-        lambda *refs: finish_queries(ret_slots, refs),
-        whole,
-        VMEM,
-        [VMEM, SMEM] + [VMEM] * len(rets),
-        [pltpu.VMEM((tokens, features), F32)],
-        "finish_queries",
-    )(after(dqt, d_keys), source, *rets)
-    return d_queries, d_keys, d_values
+    return call(
+        lambda *refs: finish(ret_slots, refs),
+        [whole] * 3,
+        [HBM] * 3,
+        [VMEM] * 4 + [HBM] * 2 + [VMEM] * len(rets),
+        [pltpu.VMEM((tokens, features), F32)] * 3
+        + [pltpu.VMEM((tokens, features), BF16)] * 3
+        + [
+            pltpu.SMEM(glob_blocks.shape, jnp.int32),
+            pltpu.SMEM(source.shape, jnp.int32),
+            pltpu.SemaphoreType.DMA((5,)),
+        ],
+        "finish",
+    )(dqt, dk, dv, part, *in_hbm(glob_blocks, source), *rets)
 
 
 def solution(mesh):

time: 84.1 us -> 82.4 us (0.980); the launches traced: 83.9 us -> 81.3 us
  waiting for transfers between devices: 22.6 us -> 19.7 us
  starting transfers between devices: 36.1 us -> 37.9 us
  Pallas kernels: 22.6 us -> 21.4 us
    ppermute x20, waiting for transfers between devices: 22.6 us -> 19.7 us  [swap(): return lax.ppermute(array, 'seq', [(i, i ^ k) for i in range(owners)])]
    ppermute x20, starting transfers between devices: 36.1 us -> 37.9 us  [swap(): return lax.ppermute(array, 'seq', [(i, i ^ k) for i in range(owners)])]
  transfers between devices with their start and end apart: 20 -> 20, of which waited for: 5 -> 5; matrix products, arithmetic and copies ran while one was open for 0% -> 0% of each run, Pallas kernels for 22% -> 23%
where the time goes in v3:
time: 82.4 us; the launch traced here: 81.3 us
  starting transfers between devices  37.9 us (46%)
  Pallas kernels  21.4 us (26%)
  waiting for transfers between devices  19.7 us (24%)
  local copies, waits for them, and re-layouts  1.15 us (1%)
  between operations  0.91 us (1%)
    ppermute x20, starting transfers between devices, swap(): return lax.ppermute(array, 'seq', [(i, i ^ k) for i in range(owners)])  37.9 us
    ppermute x20, waiting for transfers between devices, swap(): return lax.ppermute(array, 'seq', [(i, i ^ k) for i in range(owners)])  19.7 us
    pallas_call x8, Pallas kernels, owned(): call(lambda *refs: randoms(heads, counts, refs), shapes + [wide, wide], [...  8.29 us
    pallas_call x4, Pallas kernels, add_window(): call(functools.partial(window, heads, first, last), [wide] * 3, [VMEM] *...  5.81 us
    pallas_call x1, Pallas kernels, add_globals(): call(functools.partial(globals_, heads), [wide, jax.ShapeDtypeStruct(own....  2.54 us
    pallas_call x1, Pallas kernels, shards(): call(lambda *refs: pack(heads, plan, refs), [whole, jax.ShapeDtypeStruct(...  2.18 us
    pallas_call x1, Pallas kernels, shards(): call(lambda *refs: finish(ret_slots, refs), [whole] * 3, [HBM] * 3, [VMEM...  1.94 us
  transfers between devices with their start and end apart: 20, of which 5 were waited for; matrix products, arithmetic and copies ran while one was open for 0% of the time, Pallas kernels for 23%

profile of v3, /device:TPU:0, one launch (start us, length us, event | category | flops | bytes accessed | tf_op | source)
XLA Modules:
  0.0 81.3 jit_solution(10127683051276635702)
XLA Ops:
  0.6 0.0 copy-start.3
  0.6 0.6 copy-done.3
  1.3 0.6 pick_globals.1
  1.9 4.9 %collective-permute-start = (bf16[512,128]{1,0:T(8,128)(2,1)S(1)}, bf16[512,128]{1,0:T(8,128)(2,1)S(1)}, u32[]{:S(2)}, u32[]{:S(2)}) collective-permute-start(bf16[512,128]{1,0:T(8,128)(2,1)S(1)} %pick_globals.1), channel_id=1, source_target_pairs={{0,16},{4,20},{8,24},{12,28},{16,0},{20,4},{24,8},{28,12},{1,17},{... | collective-permute-start | bytes 393224 | tf_op jit(solution)/shard_map/ppermute | solution.py:390
  6.8 2.2 %pack.1 = (bf16[1024,128]{1,0:T(8,128)(2,1)S(1)}, f32[8,8,128]{2,1,0:T(8,128)S(1)}, bf16[1024,128]{1,0:T(8,128)(2,1)S(1)}, s32[27]{0:T(128)S(1)}, bf16[800,128]{...) custom-call(bf16[1024,128]{1,0:T(8,128)(2,1)} %refs_0_.1, ...), custom_call_target="tpu_custom_call" | custom-call | tf_op jit(solution)/shard_map/pack/pallas_call | solution.py:363
  9.0 0.0 copy-start
  9.0 0.5 copy-done.4
  9.5 0.0 collective-permute-start.5
  9.5 1.1 %collective-permute-start.9 = (bf16[1072,128]{1,0:T(8,128)(2,1)S(1)}, bf16[1072,128]{1,0:T(8,128)(2,1)S(1)}, u32[]{:S(2)}, u32[]{:S(2)}) collective-permute-start(bf16[1072,128]{1,0:T(8,128)(2,1)S(1)} %get-tuple-element.97), channel_id=1, source_target_pairs={{0,4},{4,0},{8,12},{12,8},{16,20},{20,16},{24,28},{28,24},{1,5},{5... | collective-permute-start | bytes 823304 | tf_op jit(solution)/shard_map/ppermute | solution.py:390
  10.6 7.3 %collective-permute-done = bf16[512,128]{1,0:T(8,128)(2,1)S(1)} collective-permute-done((bf16[512,128]{1,0:T(8,128)(2,1)S(1)}, bf16[512,128]{1,0:T(8,128)(2,1)S(1)}, u32[]{:S(2)}, u32[]{:S(2)}) %collective-permute-start) | collective-permute-done | bytes 131104 | tf_op jit(solution)/shard_map/ppermute | solution.py:390
  17.9 0.5 collective-permute-start.1
  18.4 3.6 %collective-permute-start.3 = (bf16[800,128]{1,0:T(8,128)(2,1)S(1)}, bf16[800,128]{1,0:T(8,128)(2,1)S(1)}, u32[]{:S(2)}, u32[]{:S(2)}) collective-permute-start(bf16[800,128]{1,0:T(8,128)(2,1)S(1)} %get-tuple-element.84), channel_id=1, source_target_pairs={{0,20},{4,16},{8,28},{12,24},{16,4},{20,0},{24,12},{28,8},{1,21},{... | collective-permute-start | bytes 614408 | tf_op jit(solution)/shard_map/ppermute | solution.py:390
  22.0 1.3 %window.4 = (f32[1024,128]{1,0:T(8,128)S(1)}, f32[1024,128]{1,0:T(8,128)S(1)}, f32[1024,128]{1,0:T(8,128)S(1)}) custom-call(bf16[1024,128]{1,0:T(8,128)(2,1)S(1)} %get-tuple-element.67.q_ref, bf16[1024,128]{1,0:T(8,128)(2,1)S(1)} %copy-done, f32[8,8,128]{2,1,0:T(8,128)S(1)} %get-tuple-element.69.stats_ref, bf16[1024,128]{1,0:T(8,128)(2,1)S(1)} %copy-done.1, ...), custom_call_target="tpu_custom_call" | custom-call | flops 3449999872 | tf_op jit(solution)/shard_map/window/pallas_call | solution.py:423
  23.3 1.6 %window.5 = (f32[1024,128]{1,0:T(8,128)S(1)}, f32[1024,128]{1,0:T(8,128)S(1)}, f32[1024,128]{1,0:T(8,128)S(1)}) custom-call(bf16[1024,128]{1,0:T(8,128)(2,1)S(1)} %get-tuple-element.67.q_ref, bf16[1024,128]{1,0:T(8,128)(2,1)S(1)} %copy-done, ...), custom_call_target="tpu_custom_call", output_to_operand_aliasing={{0}: (6, {}), {1}: (7, {}), {2}: (8, {})} | custom-call | flops 3449999872 | tf_op jit(solution)/shard_map/window/pallas_call | solution.py:423
  24.9 1.6 %window.6 = (f32[1024,128]{1,0:T(8,128)S(1)}, f32[1024,128]{1,0:T(8,128)S(1)}, f32[1024,128]{1,0:T(8,128)S(1)}) custom-call(bf16[1024,128]{1,0:T(8,128)(2,1)S(1)} %get-tuple-element.67.q_ref, bf16[1024,128]{1,0:T(8,128)(2,1)S(1)} %copy-done, ...), custom_call_target="tpu_custom_call", output_to_operand_aliasing={{0}: (6, {}), {1}: (7, {}), {2}: (8, {})} | custom-call | flops 3449999872 | tf_op jit(solution)/shard_map/window/pallas_call | solution.py:423
  26.5 1.3 %window.7 = (f32[1024,128]{1,0:T(8,128)S(1)}, f32[1024,128]{1,0:T(8,128)S(1)}, f32[1024,128]{1,0:T(8,128)S(1)}) custom-call(bf16[1024,128]{1,0:T(8,128)(2,1)S(1)} %get-tuple-element.67.q_ref, bf16[1024,128]{1,0:T(8,128)(2,1)S(1)} %copy-done, ...), custom_call_target="tpu_custom_call", output_to_operand_aliasing={{0}: (6, {}), {1}: (7, {}), {2}: (8, {})} | custom-call | flops 3449999872 | tf_op jit(solution)/shard_map/window/pallas_call | solution.py:423
  27.8 1.3 %collective-permute-start.6 = (bf16[1072,128]{1,0:T(8,128)(2,1)S(1)}, bf16[1072,128]{1,0:T(8,128)(2,1)S(1)}, u32[]{:S(2)}, u32[]{:S(2)}) collective-permute-start(bf16[1072,128]{1,0:T(8,128)(2,1)S(1)} %get-tuple-element.88), channel_id=1, source_target_pairs={{0,28},{4,24},{8,20},{12,16},{16,12},{20,8},{24,4},{28,0},{1,29},{... | collective-permute-start | bytes 823304 | tf_op jit(solution)/shard_map/ppermute | solution.py:390
  29.2 0.0 collective-permute-done.1
  29.2 0.1 collective-permute-start.2
  29.3 0.9 %randoms.8 = (bf16[384,128]{1,0:T(8,128)(2,1)S(1)}, f32[1024,128]{1,0:T(8,128)S(1)}, f32[1024,128]{1,0:T(8,128)S(1)}) custom-call(bf16[800,128]{1,0:T(8,128)(2,1)S(1)} %collective-permute-done.5.refs_0_, bf16[1024,128]{1,0:T(8,128)(2,1)S(1)} %copy-done.1, bf16[1024,128]{1,0:T(8,128)(2,1)S(1)} %copy-done.2, ...), custom_call_target="tpu_custom_call", output_to_operand_aliasing={{1}: (4, {}), {2}: (5, {})} | custom-call | flops 3449999872 | tf_op jit(solution)/shard_map/randoms/pallas_call | solution.py:408
  30.3 1.8 %collective-permute-start.11 = (bf16[384,128]{1,0:T(8,128)(2,1)S(1)}, bf16[384,128]{1,0:T(8,128)(2,1)S(1)}, u32[]{:S(2)}, u32[]{:S(2)}) collective-permute-start(bf16[384,128]{1,0:T(8,128)(2,1)S(1)} %get-tuple-element.93), channel_id=1, source_target_pairs={{0,16},{4,20},{8,24},{12,28},{16,0},{20,4},{24,8},{28,12},{1,17},{... | collective-permute-start | bytes 294920 | tf_op jit(solution)/shard_map/ppermute | solution.py:390
  32.0 0.9 %randoms.9 = (bf16[384,128]{1,0:T(8,128)(2,1)S(1)}, f32[1024,128]{1,0:T(8,128)S(1)}, f32[1024,128]{1,0:T(8,128)S(1)}) custom-call(bf16[800,128]{1,0:T(8,128)(2,1)S(1)} %get-tuple-element.98.refs_0_, bf16[1024,128]{1,0:T(8,128)(2,1)S(1)} %copy-done.1, bf16[1024,128]{1,0:T(8,128)(2,1)S(1)} %copy-done.2, ...), custom_call_target="tpu_custom_call", output_to_operand_aliasing={{1}: (4, {}), {2}: (5, {})} | custom-call | flops 3449999872 | tf_op jit(solution)/shard_map/randoms/pallas_call | solution.py:408
  33.0 0.0 collective-permute-done.3.refs_0_
  33.0 9.6 %collective-permute-start.7 = (bf16[800,128]{1,0:T(8,128)(2,1)S(1)}, bf16[800,128]{1,0:T(8,128)(2,1)S(1)}, u32[]{:S(2)}, u32[]{:S(2)}) collective-permute-start(bf16[800,128]{1,0:T(8,128)(2,1)S(1)} %get-tuple-element.94), channel_id=1, source_target_pairs={{0,24},{4,28},{8,16},{12,20},{16,8},{20,12},{24,0},{28,4},{1,25},{... | collective-permute-start | bytes 614408 | tf_op jit(solution)/shard_map/ppermute | solution.py:390
  42.6 0.9 %randoms.10 = (bf16[384,128]{1,0:T(8,128)(2,1)S(1)}, f32[1024,128]{1,0:T(8,128)S(1)}, f32[1024,128]{1,0:T(8,128)S(1)}) custom-call(bf16[800,128]{1,0:T(8,128)(2,1)S(1)} %collective-permute-done.3.refs_0_, bf16[1024,128]{1,0:T(8,128)(2,1)S(1)} %copy-done.1, bf16[1024,128]{1,0:T(8,128)(2,1)S(1)} %copy-done.2, ...), custom_call_target="tpu_custom_call", output_to_operand_aliasing={{1}: (4, {}), {2}: (5, {})} | custom-call | flops 3449999872 | tf_op jit(solution)/shard_map/randoms/pallas_call | solution.py:408
  43.6 0.1 collective-permute-start.8
  43.7 2.5 %globals.1 = (f32[1024,128]{1,0:T(8,128)S(1)}, bf16[512,128]{1,0:T(8,128)(2,1)S(1)}) custom-call(bf16[1024,128]{1,0:T(8,128)(2,1)S(1)} %get-tuple-element.67.q_ref, bf16[1024,128]{1,0:T(8,128)(2,1)S(1)} %copy-done, f32[8,8,128]{2,1,0:T(8,128)S(1)} %get-tuple-element.69.stats_ref, ...), custom_call_target="tpu_custom_call", output_to_operand_aliasing={{0}: (4, {})} | custom-call | tf_op jit(solution)/shard_map/globals/pallas_call | solution.py:393
  46.3 0.0 collective-permute-done.9.refs_0_
  46.3 1.6 %collective-permute-start.10 = (bf16[512,128]{1,0:T(8,128)(2,1)S(1)}, bf16[512,128]{1,0:T(8,128)(2,1)S(1)}, u32[]{:S(2)}, u32[]{:S(2)}) collective-permute-start(bf16[512,128]{1,0:T(8,128)(2,1)S(1)} %get-tuple-element.118), channel_id=1, source_target_pairs={{0,4},{4,0},{8,12},{12,8},{16,20},{20,16},{24,28},{28,24},{1,5},{5... | collective-permute-start | bytes 393224 | tf_op jit(solution)/shard_map/ppermute | solution.py:390
  47.9 1.2 %randoms.11 = (bf16[512,128]{1,0:T(8,128)(2,1)S(1)}, f32[1024,128]{1,0:T(8,128)S(1)}, f32[1024,128]{1,0:T(8,128)S(1)}) custom-call(bf16[1072,128]{1,0:T(8,128)(2,1)S(1)} %collective-permute-done.9.refs_0_, bf16[1024,128]{1,0:T(8,128)(2,1)S(1)} %copy-done.1, bf16[1024,128]{1,0:T(8,128)(2,1)S(1)} %copy-done.2, ...), custom_call_target="tpu_custom_call", output_to_operand_aliasing={{1}: (4, {}), {2}: (5, {})} | custom-call | flops 3449999872 | tf_op jit(solution)/shard_map/randoms/pallas_call | solution.py:408
  49.1 2.2 %collective-permute-done.10 = bf16[512,128]{1,0:T(8,128)(2,1)S(1)} collective-permute-done((bf16[512,128]{1,0:T(8,128)(2,1)S(1)}, bf16[512,128]{1,0:T(8,128)(2,1)S(1)}, u32[]{:S(2)}, u32[]{:S(2)}) %collective-permute-start.10) | collective-permute-done | bytes 131104 | tf_op jit(solution)/shard_map/ppermute | solution.py:390
  51.3 2.2 %collective-permute-start.13 = (bf16[384,128]{1,0:T(8,128)(2,1)S(1)}, bf16[384,128]{1,0:T(8,128)(2,1)S(1)}, u32[]{:S(2)}, u32[]{:S(2)}) collective-permute-start(bf16[384,128]{1,0:T(8,128)(2,1)S(1)} %get-tuple-element.120), channel_id=1, source_target_pairs={{0,20},{4,16},{8,28},{12,24},{16,4},{20,0},{24,12},{28,8},{1,21},{... | collective-permute-start | bytes 294920 | tf_op jit(solution)/shard_map/ppermute | solution.py:390
  53.6 0.0 collective-permute-done.11.refs_10_
  53.6 0.8 collective-permute-start.4
  54.4 4.2 %collective-permute-start.12 = (bf16[512,128]{1,0:T(8,128)(2,1)S(1)}, bf16[512,128]{1,0:T(8,128)(2,1)S(1)}, u32[]{:S(2)}, u32[]{:S(2)}) collective-permute-start(bf16[512,128]{1,0:T(8,128)(2,1)S(1)} %add_convert_fusion.2), channel_id=1, source_target_pairs={{0,8},{4,12},{8,0},{12,4},{16,24},{20,28},{24,16},{28,20},{1,9},{5... | collective-permute-start | bytes 393224 | tf_op jit(solution)/shard_map/ppermute | solution.py:390
  58.6 0.9 %randoms.12 = (bf16[384,128]{1,0:T(8,128)(2,1)S(1)}, f32[1024,128]{1,0:T(8,128)S(1)}, f32[1024,128]{1,0:T(8,128)S(1)}) custom-call(bf16[800,128]{1,0:T(8,128)(2,1)S(1)} %collective-permute-done.8.refs_0_, bf16[1024,128]{1,0:T(8,128)(2,1)S(1)} %copy-done.1, bf16[1024,128]{1,0:T(8,128)(2,1)S(1)} %copy-done.2, ...), custom_call_target="tpu_custom_call", output_to_operand_aliasing={{1}: (4, {}), {2}: (5, {})} | custom-call | flops 3449999872 | tf_op jit(solution)/shard_map/randoms/pallas_call | solution.py:408
  59.6 0.9 %randoms.13 = (bf16[384,128]{1,0:T(8,128)(2,1)S(1)}, f32[1024,128]{1,0:T(8,128)S(1)}, f32[1024,128]{1,0:T(8,128)S(1)}) custom-call(bf16[800,128]{1,0:T(8,128)(2,1)S(1)} %collective-permute-done.7.refs_0_, bf16[1024,128]{1,0:T(8,128)(2,1)S(1)} %copy-done.1, bf16[1024,128]{1,0:T(8,128)(2,1)S(1)} %copy-done.2, ...), custom_call_target="tpu_custom_call", output_to_operand_aliasing={{1}: (4, {}), {2}: (5, {})} | custom-call | flops 3449999872 | tf_op jit(solution)/shard_map/randoms/pallas_call | solution.py:408
  60.5 1.2 %randoms.14 = (bf16[512,128]{1,0:T(8,128)(2,1)S(1)}, f32[1024,128]{1,0:T(8,128)S(1)}, f32[1024,128]{1,0:T(8,128)S(1)}) custom-call(bf16[1072,128]{1,0:T(8,128)(2,1)S(1)} %collective-permute-done.6.refs_0_, bf16[1024,128]{1,0:T(8,128)(2,1)S(1)} %copy-done.1, bf16[1024,128]{1,0:T(8,128)(2,1)S(1)} %copy-done.2, ...), custom_call_target="tpu_custom_call", output_to_operand_aliasing={{1}: (4, {}), {2}: (5, {})} | custom-call | flops 3449999872 | tf_op jit(solution)/shard_map/randoms/pallas_call | solution.py:408
  61.7 3.5 %collective-permute-start.19 = (bf16[512,128]{1,0:T(8,128)(2,1)S(1)}, bf16[512,128]{1,0:T(8,128)(2,1)S(1)}, u32[]{:S(2)}, u32[]{:S(2)}) collective-permute-start(bf16[512,128]{1,0:T(8,128)(2,1)S(1)} %get-tuple-element.130), channel_id=1, source_target_pairs={{0,28},{4,24},{8,20},{12,16},{16,12},{20,8},{24,4},{28,0},{1,29},{... | collective-permute-start | bytes 393224 | tf_op jit(solution)/shard_map/ppermute | solution.py:390
  65.3 0.3 collective-permute-start.15
  65.6 4.4 %collective-permute-done.12 = bf16[512,128]{1,0:T(8,128)(2,1)S(1)} collective-permute-done((bf16[512,128]{1,0:T(8,128)(2,1)S(1)}, bf16[512,128]{1,0:T(8,128)(2,1)S(1)}, u32[]{:S(2)}, u32[]{:S(2)}) %collective-permute-start.12) | collective-permute-done | bytes 131104 | tf_op jit(solution)/shard_map/ppermute | solution.py:390
  70.0 0.1 collective-permute-start.14
  70.1 1.2 %randoms.15 = (bf16[512,128]{1,0:T(8,128)(2,1)S(1)}, f32[1024,128]{1,0:T(8,128)S(1)}, f32[1024,128]{1,0:T(8,128)S(1)}) custom-call(bf16[1072,128]{1,0:T(8,128)(2,1)S(1)} %collective-permute-done.4.refs_0_, bf16[1024,128]{1,0:T(8,128)(2,1)S(1)} %copy-done.1, bf16[1024,128]{1,0:T(8,128)(2,1)S(1)} %copy-done.2, ...), custom_call_target="tpu_custom_call", output_to_operand_aliasing={{1}: (4, {}), {2}: (5, {})} | custom-call | flops 3449999872 | tf_op jit(solution)/shard_map/randoms/pallas_call | solution.py:408
  71.3 0.7 collective-permute-start.18
  72.0 0.9 %collective-permute-done.15.refs_12_ = bf16[384,128]{1,0:T(8,128)(2,1)S(1)} collective-permute-done((bf16[384,128]{1,0:T(8,128)(2,1)S(1)}, bf16[384,128]{1,0:T(8,128)(2,1)S(1)}, u32[]{:S(2)}, u32[]{:S(2)}) %collective-permute-start.15) | collective-permute-done | bytes 98336 | tf_op jit(solution)/shard_map/ppermute | solution.py:390
  72.9 1.5 %collective-permute-start.16 = (bf16[512,128]{1,0:T(8,128)(2,1)S(1)}, bf16[512,128]{1,0:T(8,128)(2,1)S(1)}, u32[]{:S(2)}, u32[]{:S(2)}) collective-permute-start(bf16[512,128]{1,0:T(8,128)(2,1)S(1)} %get-tuple-element.126), channel_id=1, source_target_pairs={{0,4},{4,0},{8,12},{12,8},{16,20},{20,16},{24,28},{28,24},{1,5},{5... | collective-permute-start | bytes 393224 | tf_op jit(solution)/shard_map/ppermute | solution.py:390
  74.4 4.8 %collective-permute-done.14 = bf16[512,128]{1,0:T(8,128)(2,1)S(1)} collective-permute-done((bf16[512,128]{1,0:T(8,128)(2,1)S(1)}, bf16[512,128]{1,0:T(8,128)(2,1)S(1)}, u32[]{:S(2)}, u32[]{:S(2)}) %collective-permute-start.14) | collective-permute-done | bytes 131104 | tf_op jit(solution)/shard_map/ppermute | solution.py:390
  79.3 1.9 %finish.1 = (bf16[1024,128]{1,0:T(8,128)(2,1)}, bf16[1024,128]{1,0:T(8,128)(2,1)}, bf16[1024,128]{1,0:T(8,128)(2,1)}) custom-call(f32[1024,128]{1,0:T(8,128)S(1)} %get-tuple-element.81.refs_0_, f32[1024,128]{1,0:T(8,128)S(1)} %get-tuple-element.116.refs_1_, f32[1024,128]{1,0:T(8,128)S(1)} %get-tuple-element.117.refs_2_, ...), custom_call_target="tpu_custom_call" | custom-call | flops 3449999872 | tf_op jit(solution)/shard_map/finish/pallas_call | solution.py:510
  (24 shorter events, 0.3 us)
Async XLA Ops:
  0.6 0.7 copy-start.3
  1.9 15.9 %collective-permute-start = (bf16[512,128]{1,0:T(8,128)(2,1)S(1)}, bf16[512,128]{1,0:T(8,128)(2,1)S(1)}, u32[]{:S(2)}, u32[]{:S(2)}) collective-permute-start(bf16[512,128]{1,0:T(8,128)(2,1)S(1)} %pick_globals.1), channel_id=1, source_target_pairs={{0,16},{4,20},{8,24},{12,28},{16,0},{20,4},{24,8},{28,12},{1,17},{... | collective-permute-start | bytes 393224 | tf_op jit(solution)/shard_map/ppermute | solution.py:390
  6.8 15.2 %copy-start.1 = (bf16[1024,128]{1,0:T(8,128)(2,1)S(1)}, bf16[1024,128]{1,0:T(8,128)(2,1)}, u32[]{:S(2)}) copy-start(bf16[1024,128]{1,0:T(8,128)(2,1)} %refs_1_.17) | copy-start | bytes 786436
  6.8 15.2 %copy-start.2 = (bf16[1024,128]{1,0:T(8,128)(2,1)S(1)}, bf16[1024,128]{1,0:T(8,128)(2,1)}, u32[]{:S(2)}) copy-start(bf16[1024,128]{1,0:T(8,128)(2,1)} %refs_2_.17) | copy-start | bytes 786436
  9.0 0.5 copy-start.4
  9.0 13.0 %copy-start = (bf16[1024,128]{1,0:T(8,128)(2,1)S(1)}, bf16[1024,128]{1,0:T(8,128)(2,1)}, u32[]{:S(2)}) copy-start(bf16[1024,128]{1,0:T(8,128)(2,1)} %g_ref.9) | copy-start | bytes 786436
  9.5 18.4 %collective-permute-start.5 = (bf16[800,128]{1,0:T(8,128)(2,1)S(1)}, bf16[800,128]{1,0:T(8,128)(2,1)S(1)}, u32[]{:S(2)}, u32[]{:S(2)}) collective-permute-start(bf16[800,128]{1,0:T(8,128)(2,1)S(1)} %get-tuple-element.87), channel_id=1, source_target_pairs={{0,16},{4,20},{8,24},{12,28},{16,0},{20,4},{24,8},{28,12},{1,17},{... | collective-permute-start | bytes 614408 | tf_op jit(solution)/shard_map/ppermute | solution.py:390
  9.5 36.8 %collective-permute-start.9 = (bf16[1072,128]{1,0:T(8,128)(2,1)S(1)}, bf16[1072,128]{1,0:T(8,128)(2,1)S(1)}, u32[]{:S(2)}, u32[]{:S(2)}) collective-permute-start(bf16[1072,128]{1,0:T(8,128)(2,1)S(1)} %get-tuple-element.97), channel_id=1, source_target_pairs={{0,4},{4,0},{8,12},{12,8},{16,20},{20,16},{24,28},{28,24},{1,5},{5... | collective-permute-start | bytes 823304 | tf_op jit(solution)/shard_map/ppermute | solution.py:390
  17.9 11.3 %collective-permute-start.1 = (bf16[512,128]{1,0:T(8,128)(2,1)S(1)}, bf16[512,128]{1,0:T(8,128)(2,1)S(1)}, u32[]{:S(2)}, u32[]{:S(2)}) collective-permute-start(bf16[512,128]{1,0:T(8,128)(2,1)S(1)} %add.18), channel_id=1, source_target_pairs={{0,8},{4,12},{8,0},{12,4},{16,24},{20,28},{24,16},{28,20},{1,9},{5... | collective-permute-start | bytes 393224 | tf_op jit(solution)/shard_map/ppermute | solution.py:390
  18.4 14.6 %collective-permute-start.3 = (bf16[800,128]{1,0:T(8,128)(2,1)S(1)}, bf16[800,128]{1,0:T(8,128)(2,1)S(1)}, u32[]{:S(2)}, u32[]{:S(2)}) collective-permute-start(bf16[800,128]{1,0:T(8,128)(2,1)S(1)} %get-tuple-element.84), channel_id=1, source_target_pairs={{0,20},{4,16},{8,28},{12,24},{16,4},{20,0},{24,12},{28,8},{1,21},{... | collective-permute-start | bytes 614408 | tf_op jit(solution)/shard_map/ppermute | solution.py:390
  27.8 26.6 %collective-permute-start.6 = (bf16[1072,128]{1,0:T(8,128)(2,1)S(1)}, bf16[1072,128]{1,0:T(8,128)(2,1)S(1)}, u32[]{:S(2)}, u32[]{:S(2)}) collective-permute-start(bf16[1072,128]{1,0:T(8,128)(2,1)S(1)} %get-tuple-element.88), channel_id=1, source_target_pairs={{0,28},{4,24},{8,20},{12,16},{16,12},{20,8},{24,4},{28,0},{1,29},{... | collective-permute-start | bytes 823304 | tf_op jit(solution)/shard_map/ppermute | solution.py:390
  29.2 14.4 %collective-permute-start.2 = (bf16[512,128]{1,0:T(8,128)(2,1)S(1)}, bf16[512,128]{1,0:T(8,128)(2,1)S(1)}, u32[]{:S(2)}, u32[]{:S(2)}) collective-permute-start(bf16[512,128]{1,0:T(8,128)(2,1)S(1)} %add.19), channel_id=1, source_target_pairs={{0,4},{4,0},{8,12},{12,8},{16,20},{20,16},{24,28},{28,24},{1,5},{5... | collective-permute-start | bytes 393224 | tf_op jit(solution)/shard_map/ppermute | solution.py:390
  30.3 23.3 %collective-permute-start.11 = (bf16[384,128]{1,0:T(8,128)(2,1)S(1)}, bf16[384,128]{1,0:T(8,128)(2,1)S(1)}, u32[]{:S(2)}, u32[]{:S(2)}) collective-permute-start(bf16[384,128]{1,0:T(8,128)(2,1)S(1)} %get-tuple-element.93), channel_id=1, source_target_pairs={{0,16},{4,20},{8,24},{12,28},{16,0},{20,4},{24,8},{28,12},{1,17},{... | collective-permute-start | bytes 294920 | tf_op jit(solution)/shard_map/ppermute | solution.py:390
  33.0 21.4 %collective-permute-start.7 = (bf16[800,128]{1,0:T(8,128)(2,1)S(1)}, bf16[800,128]{1,0:T(8,128)(2,1)S(1)}, u32[]{:S(2)}, u32[]{:S(2)}) collective-permute-start(bf16[800,128]{1,0:T(8,128)(2,1)S(1)} %get-tuple-element.94), channel_id=1, source_target_pairs={{0,24},{4,28},{8,16},{12,20},{16,8},{20,12},{24,0},{28,4},{1,25},{... | collective-permute-start | bytes 614408 | tf_op jit(solution)/shard_map/ppermute | solution.py:390
  43.6 15.0 %collective-permute-start.8 = (bf16[800,128]{1,0:T(8,128)(2,1)S(1)}, bf16[800,128]{1,0:T(8,128)(2,1)S(1)}, u32[]{:S(2)}, u32[]{:S(2)}) collective-permute-start(bf16[800,128]{1,0:T(8,128)(2,1)S(1)} %get-tuple-element.96), channel_id=1, source_target_pairs={{0,8},{4,12},{8,0},{12,4},{16,24},{20,28},{24,16},{28,20},{1,9},{5... | collective-permute-start | bytes 614408 | tf_op jit(solution)/shard_map/ppermute | solution.py:390
  46.3 5.0 %collective-permute-start.10 = (bf16[512,128]{1,0:T(8,128)(2,1)S(1)}, bf16[512,128]{1,0:T(8,128)(2,1)S(1)}, u32[]{:S(2)}, u32[]{:S(2)}) collective-permute-start(bf16[512,128]{1,0:T(8,128)(2,1)S(1)} %get-tuple-element.118), channel_id=1, source_target_pairs={{0,4},{4,0},{8,12},{12,8},{16,20},{20,16},{24,28},{28,24},{1,5},{5... | collective-permute-start | bytes 393224 | tf_op jit(solution)/shard_map/ppermute | solution.py:390
  51.3 10.4 %collective-permute-start.13 = (bf16[384,128]{1,0:T(8,128)(2,1)S(1)}, bf16[384,128]{1,0:T(8,128)(2,1)S(1)}, u32[]{:S(2)}, u32[]{:S(2)}) collective-permute-start(bf16[384,128]{1,0:T(8,128)(2,1)S(1)} %get-tuple-element.120), channel_id=1, source_target_pairs={{0,20},{4,16},{8,28},{12,24},{16,4},{20,0},{24,12},{28,8},{1,21},{... | collective-permute-start | bytes 294920 | tf_op jit(solution)/shard_map/ppermute | solution.py:390
  53.6 16.5 %collective-permute-start.4 = (bf16[1072,128]{1,0:T(8,128)(2,1)S(1)}, bf16[1072,128]{1,0:T(8,128)(2,1)S(1)}, u32[]{:S(2)}, u32[]{:S(2)}) collective-permute-start(bf16[1072,128]{1,0:T(8,128)(2,1)S(1)} %get-tuple-element.85), channel_id=1, source_target_pairs={{0,12},{4,8},{8,4},{12,0},{16,28},{20,24},{24,20},{28,16},{1,13},{... | collective-permute-start | bytes 823304 | tf_op jit(solution)/shard_map/ppermute | solution.py:390
  54.4 15.5 %collective-permute-start.12 = (bf16[512,128]{1,0:T(8,128)(2,1)S(1)}, bf16[512,128]{1,0:T(8,128)(2,1)S(1)}, u32[]{:S(2)}, u32[]{:S(2)}) collective-permute-start(bf16[512,128]{1,0:T(8,128)(2,1)S(1)} %add_convert_fusion.2), channel_id=1, source_target_pairs={{0,8},{4,12},{8,0},{12,4},{16,24},{20,28},{24,16},{28,20},{1,9},{5... | collective-permute-start | bytes 393224 | tf_op jit(solution)/shard_map/ppermute | solution.py:390
  61.7 17.6 %collective-permute-start.19 = (bf16[512,128]{1,0:T(8,128)(2,1)S(1)}, bf16[512,128]{1,0:T(8,128)(2,1)S(1)}, u32[]{:S(2)}, u32[]{:S(2)}) collective-permute-start(bf16[512,128]{1,0:T(8,128)(2,1)S(1)} %get-tuple-element.130), channel_id=1, source_target_pairs={{0,28},{4,24},{8,20},{12,16},{16,12},{20,8},{24,4},{28,0},{1,29},{... | collective-permute-start | bytes 393224 | tf_op jit(solution)/shard_map/ppermute | solution.py:390
  65.3 7.6 %collective-permute-start.15 = (bf16[384,128]{1,0:T(8,128)(2,1)S(1)}, bf16[384,128]{1,0:T(8,128)(2,1)S(1)}, u32[]{:S(2)}, u32[]{:S(2)}) collective-permute-start(bf16[384,128]{1,0:T(8,128)(2,1)S(1)} %get-tuple-element.125), channel_id=1, source_target_pairs={{0,24},{4,28},{8,16},{12,20},{16,8},{20,12},{24,0},{28,4},{1,25},{... | collective-permute-start | bytes 294920 | tf_op jit(solution)/shard_map/ppermute | solution.py:390
  65.6 13.7 %collective-permute-start.17 = (bf16[384,128]{1,0:T(8,128)(2,1)S(1)}, bf16[384,128]{1,0:T(8,128)(2,1)S(1)}, u32[]{:S(2)}, u32[]{:S(2)}) collective-permute-start(bf16[384,128]{1,0:T(8,128)(2,1)S(1)} %get-tuple-element.127), channel_id=1, source_target_pairs={{0,8},{4,12},{8,0},{12,4},{16,24},{20,28},{24,16},{28,20},{1,9},{5... | collective-permute-start | bytes 294920 | tf_op jit(solution)/shard_map/ppermute | solution.py:390
  70.0 9.3 %collective-permute-start.14 = (bf16[512,128]{1,0:T(8,128)(2,1)S(1)}, bf16[512,128]{1,0:T(8,128)(2,1)S(1)}, u32[]{:S(2)}, u32[]{:S(2)}) collective-permute-start(bf16[512,128]{1,0:T(8,128)(2,1)S(1)} %add_convert_fusion.1), channel_id=1, source_target_pairs={{0,16},{4,20},{8,24},{12,28},{16,0},{20,4},{24,8},{28,12},{1,17},{... | collective-permute-start | bytes 393224 | tf_op jit(solution)/shard_map/ppermute | solution.py:390
  71.3 8.0 %collective-permute-start.18 = (bf16[512,128]{1,0:T(8,128)(2,1)S(1)}, bf16[512,128]{1,0:T(8,128)(2,1)S(1)}, u32[]{:S(2)}, u32[]{:S(2)}) collective-permute-start(bf16[512,128]{1,0:T(8,128)(2,1)S(1)} %get-tuple-element.128), channel_id=1, source_target_pairs={{0,12},{4,8},{8,4},{12,0},{16,28},{20,24},{24,20},{28,16},{1,13},{... | collective-permute-start | bytes 393224 | tf_op jit(solution)/shard_map/ppermute | solution.py:390
  72.9 6.4 %collective-permute-start.16 = (bf16[512,128]{1,0:T(8,128)(2,1)S(1)}, bf16[512,128]{1,0:T(8,128)(2,1)S(1)}, u32[]{:S(2)}, u32[]{:S(2)}) collective-permute-start(bf16[512,128]{1,0:T(8,128)(2,1)S(1)} %get-tuple-element.126), channel_id=1, source_target_pairs={{0,4},{4,0},{8,12},{12,8},{16,20},{20,16},{24,28},{28,24},{1,5},{5... | collective-permute-start | bytes 393224 | tf_op jit(solution)/shard_map/ppermute | solution.py:390

commit v4 on v3

--- a/solution.py
+++ b/solution.py
@@ -18,10 +18,10 @@
 F32 = jnp.float32
 BF16 = jnp.bfloat16
 LIMIT = 24
-PIECES = 4
+PIECES = 2
 COSTS = {'window': 3, 'randoms': 3, 'finish': 3}
-GATES = {'W': ['G1'], 'F5': ['G1'], 'F6': ['R0'], 'F7': ['F4'], 'F2': ['F5'], 'F3': ['F5'], 'R1': ['G2'], 'R3': ['R1'], 'r6': ['r4'], 'r7': ['r5', 'F1', 'F6'], 'P2': ['F6', 'F7', 'r4'], 'P3': ['r5', 'F5'], 'r1': ['r6'], 'R0': ['G2']}
-GROUPS = [[4], [0], [5], [1], [2], [6], [7], [3]]
+GATES = {'W': ['G1'], 'F5': ['G1'], 'F6': ['R0'], 'F7': ['F4'], 'F2': ['F5'], 'F3': ['F5'], 'R1': ['G2'], 'r6': ['r4'], 'r7': ['r5', 'F1', 'F6'], 'P2': ['F6', 'F7', 'r4'], 'P3': ['r5', 'F5'], 'r1': ['r6'], 'R0': ['G2'], 'G3': ['R1']}
+GROUPS = [[4], [0], [5], [1], [2, 6], [7], [3]]
 HOPS = {'G': [4, 2, 1], 'P': [1, 2, 4]}
 
 

time: 82.4 us -> 80.6 us (0.978)
  waiting for transfers between devices: 19.7 us -> 13.5 us
  starting transfers between devices: 37.9 us -> 43.6 us
    ppermute x20, waiting for transfers between devices: 19.7 us -> 13.5 us  [swap(): return lax.ppermute(array, 'seq', [(i, i ^ k) for i in range(owners)])]
    ppermute x20, starting transfers between devices: 37.9 us -> 43.6 us  [swap(): return lax.ppermute(array, 'seq', [(i, i ^ k) for i in range(owners)])]
    pallas_call x4 -> x2, Pallas kernels: 5.81 us -> 5.51 us  [add_window(): call(functools.partial(window, heads, first, last), [wide] * 3, [VMEM] *...]
    pallas_call x8 -> x7, Pallas kernels: 8.29 us -> 8.05 us  [owned(): call(lambda *refs: randoms(heads, counts, refs), shapes + [wide, wide], [...]
  transfers between devices with their start and end apart: 20 -> 20, of which waited for: 5 -> 6; matrix products, arithmetic and copies ran while one was open for 0% -> 0% of each run, Pallas kernels for 23% -> 23%
where the time goes in v4:
time: 80.6 us; the launch traced here: 80.2 us
  starting transfers between devices  43.6 us (54%)
  Pallas kernels  20.8 us (26%)
  waiting for transfers between devices  13.5 us (17%)
  local copies, waits for them, and re-layouts  1.15 us (1%)
  between operations  0.89 us (1%)
    ppermute x20, starting transfers between devices, swap(): return lax.ppermute(array, 'seq', [(i, i ^ k) for i in range(owners)])  43.6 us
    ppermute x20, waiting for transfers between devices, swap(): return lax.ppermute(array, 'seq', [(i, i ^ k) for i in range(owners)])  13.5 us
    pallas_call x7, Pallas kernels, owned(): call(lambda *refs: randoms(heads, counts, refs), shapes + [wide, wide], [...  8.05 us
    pallas_call x2, Pallas kernels, add_window(): call(functools.partial(window, heads, first, last), [wide] * 3, [VMEM] *...  5.51 us
    pallas_call x1, Pallas kernels, add_globals(): call(functools.partial(globals_, heads), [wide, jax.ShapeDtypeStruct(own....  2.54 us
    pallas_call x1, Pallas kernels, shards(): call(lambda *refs: pack(heads, plan, refs), [whole, jax.ShapeDtypeStruct(...  2.18 us
    pallas_call x1, Pallas kernels, shards(): call(lambda *refs: finish(ret_slots, refs), [whole] * 3, [HBM] * 3, [VMEM...  1.94 us
  transfers between devices with their start and end apart: 20, of which 6 were waited for; matrix products, arithmetic and copies ran while one was open for 0% of the time, Pallas kernels for 23%

profile of v4, /device:TPU:0, one launch (start us, length us, event | category | flops | bytes accessed | tf_op | source)
XLA Modules:
  0.0 80.2 jit_solution(2717932903967124446)
XLA Ops:
  0.6 0.0 copy-start.3
  0.6 0.6 copy-done.3
  1.3 0.6 pick_globals.1
  1.9 4.9 %collective-permute-start = (bf16[512,128]{1,0:T(8,128)(2,1)S(1)}, bf16[512,128]{1,0:T(8,128)(2,1)S(1)}, u32[]{:S(2)}, u32[]{:S(2)}) collective-permute-start(bf16[512,128]{1,0:T(8,128)(2,1)S(1)} %pick_globals.1), channel_id=1, source_target_pairs={{0,16},{4,20},{8,24},{12,28},{16,0},{20,4},{24,8},{28,12},{1,17},{... | collective-permute-start | bytes 393224 | tf_op jit(solution)/shard_map/ppermute | solution.py:390
  6.8 2.2 %pack.1 = (bf16[1024,128]{1,0:T(8,128)(2,1)S(1)}, f32[8,8,128]{2,1,0:T(8,128)S(1)}, bf16[1024,128]{1,0:T(8,128)(2,1)S(1)}, s32[27]{0:T(128)S(1)}, bf16[800,128]{...) custom-call(bf16[1024,128]{1,0:T(8,128)(2,1)} %refs_0_.1, ...), custom_call_target="tpu_custom_call" | custom-call | tf_op jit(solution)/shard_map/pack/pallas_call | solution.py:363
  9.0 0.0 copy-start
  9.0 0.5 copy-done.4
  9.5 0.0 collective-permute-start.2
  9.5 1.1 %collective-permute-start.9 = (bf16[1072,128]{1,0:T(8,128)(2,1)S(1)}, bf16[1072,128]{1,0:T(8,128)(2,1)S(1)}, u32[]{:S(2)}, u32[]{:S(2)}) collective-permute-start(bf16[1072,128]{1,0:T(8,128)(2,1)S(1)} %get-tuple-element.89), channel_id=1, source_target_pairs={{0,4},{4,0},{8,12},{12,8},{16,20},{20,16},{24,28},{28,24},{1,5},{5... | collective-permute-start | bytes 823304 | tf_op jit(solution)/shard_map/ppermute | solution.py:390
  10.6 3.0 %collective-permute-done = bf16[512,128]{1,0:T(8,128)(2,1)S(1)} collective-permute-done((bf16[512,128]{1,0:T(8,128)(2,1)S(1)}, bf16[512,128]{1,0:T(8,128)(2,1)S(1)}, u32[]{:S(2)}, u32[]{:S(2)}) %collective-permute-start) | collective-permute-done | bytes 131104 | tf_op jit(solution)/shard_map/ppermute | solution.py:390
  13.6 4.8 %collective-permute-start.1 = (bf16[512,128]{1,0:T(8,128)(2,1)S(1)}, bf16[512,128]{1,0:T(8,128)(2,1)S(1)}, u32[]{:S(2)}, u32[]{:S(2)}) collective-permute-start(bf16[512,128]{1,0:T(8,128)(2,1)S(1)} %add.18), channel_id=1, source_target_pairs={{0,8},{4,12},{8,0},{12,4},{16,24},{20,28},{24,16},{28,20},{1,9},{5... | collective-permute-start | bytes 393224 | tf_op jit(solution)/shard_map/ppermute | solution.py:390
  18.4 3.6 %collective-permute-start.4 = (bf16[800,128]{1,0:T(8,128)(2,1)S(1)}, bf16[800,128]{1,0:T(8,128)(2,1)S(1)}, u32[]{:S(2)}, u32[]{:S(2)}) collective-permute-start(bf16[800,128]{1,0:T(8,128)(2,1)S(1)} %get-tuple-element.80), channel_id=1, source_target_pairs={{0,20},{4,16},{8,28},{12,24},{16,4},{20,0},{24,12},{28,8},{1,21},{... | collective-permute-start | bytes 614408 | tf_op jit(solution)/shard_map/ppermute | solution.py:390
  22.0 2.8 %window.2 = (f32[1024,128]{1,0:T(8,128)S(1)}, f32[1024,128]{1,0:T(8,128)S(1)}, f32[1024,128]{1,0:T(8,128)S(1)}) custom-call(bf16[1024,128]{1,0:T(8,128)(2,1)S(1)} %get-tuple-element.59.q_ref, bf16[1024,128]{1,0:T(8,128)(2,1)S(1)} %copy-done, f32[8,8,128]{2,1,0:T(8,128)S(1)} %get-tuple-element.64.stats_ref, bf16[1024,128]{1,0:T(8,128)(2,1)S(1)} %copy-done.1, ...), custom_call_target="tpu_custom_call" | custom-call | flops 3449999872 | tf_op jit(solution)/shard_map/window/pallas_call | solution.py:423
  24.7 2.8 %window.3 = (f32[1024,128]{1,0:T(8,128)S(1)}, f32[1024,128]{1,0:T(8,128)S(1)}, f32[1024,128]{1,0:T(8,128)S(1)}) custom-call(bf16[1024,128]{1,0:T(8,128)(2,1)S(1)} %get-tuple-element.59.q_ref, bf16[1024,128]{1,0:T(8,128)(2,1)S(1)} %copy-done, ...), custom_call_target="tpu_custom_call", output_to_operand_aliasing={{0}: (6, {}), {1}: (7, {}), {2}: (8, {})} | custom-call | flops 3449999872 | tf_op jit(solution)/shard_map/window/pallas_call | solution.py:423
  27.5 0.1 collective-permute-start.6
  27.6 0.0 collective-permute-done.1
  27.6 0.9 %randoms.7 = (bf16[384,128]{1,0:T(8,128)(2,1)S(1)}, f32[1024,128]{1,0:T(8,128)S(1)}, f32[1024,128]{1,0:T(8,128)S(1)}) custom-call(bf16[800,128]{1,0:T(8,128)(2,1)S(1)} %collective-permute-done.2.refs_0_, bf16[1024,128]{1,0:T(8,128)(2,1)S(1)} %copy-done.1, bf16[1024,128]{1,0:T(8,128)(2,1)S(1)} %copy-done.2, ...), custom_call_target="tpu_custom_call", output_to_operand_aliasing={{1}: (4, {}), {2}: (5, {})} | custom-call | flops 3449999872 | tf_op jit(solution)/shard_map/randoms/pallas_call | solution.py:408
  28.6 1.0 %randoms.8 = (bf16[384,128]{1,0:T(8,128)(2,1)S(1)}, f32[1024,128]{1,0:T(8,128)S(1)}, f32[1024,128]{1,0:T(8,128)S(1)}) custom-call(bf16[800,128]{1,0:T(8,128)(2,1)S(1)} %get-tuple-element.61.refs_0_, bf16[1024,128]{1,0:T(8,128)(2,1)S(1)} %copy-done.1, bf16[1024,128]{1,0:T(8,128)(2,1)S(1)} %copy-done.2, ...), custom_call_target="tpu_custom_call", output_to_operand_aliasing={{1}: (4, {}), {2}: (5, {})} | custom-call | flops 3449999872 | tf_op jit(solution)/shard_map/randoms/pallas_call | solution.py:408
  29.6 2.3 %collective-permute-start.11 = (bf16[384,128]{1,0:T(8,128)(2,1)S(1)}, bf16[384,128]{1,0:T(8,128)(2,1)S(1)}, u32[]{:S(2)}, u32[]{:S(2)}) collective-permute-start(bf16[384,128]{1,0:T(8,128)(2,1)S(1)} %get-tuple-element.87), channel_id=1, source_target_pairs={{0,16},{4,20},{8,24},{12,28},{16,0},{20,4},{24,8},{28,12},{1,17},{... | collective-permute-start | bytes 294920 | tf_op jit(solution)/shard_map/ppermute | solution.py:390
  31.8 0.8 collective-permute-start.3
  32.6 0.0 collective-permute-done.4.refs_0_
  32.6 10.8 %collective-permute-start.8 = (bf16[800,128]{1,0:T(8,128)(2,1)S(1)}, bf16[800,128]{1,0:T(8,128)(2,1)S(1)}, u32[]{:S(2)}, u32[]{:S(2)}) collective-permute-start(bf16[800,128]{1,0:T(8,128)(2,1)S(1)} %get-tuple-element.88), channel_id=1, source_target_pairs={{0,24},{4,28},{8,16},{12,20},{16,8},{20,12},{24,0},{28,4},{1,25},{... | collective-permute-start | bytes 614408 | tf_op jit(solution)/shard_map/ppermute | solution.py:390
  43.4 0.9 %randoms.9 = (bf16[384,128]{1,0:T(8,128)(2,1)S(1)}, f32[1024,128]{1,0:T(8,128)S(1)}, f32[1024,128]{1,0:T(8,128)S(1)}) custom-call(bf16[800,128]{1,0:T(8,128)(2,1)S(1)} %collective-permute-done.4.refs_0_, bf16[1024,128]{1,0:T(8,128)(2,1)S(1)} %copy-done.1, bf16[1024,128]{1,0:T(8,128)(2,1)S(1)} %copy-done.2, ...), custom_call_target="tpu_custom_call", output_to_operand_aliasing={{1}: (4, {}), {2}: (5, {})} | custom-call | flops 3449999872 | tf_op jit(solution)/shard_map/randoms/pallas_call | solution.py:408
  44.4 0.0 collective-permute-done.3
  44.4 0.1 collective-permute-start.7
  44.5 2.5 %globals.1 = (f32[1024,128]{1,0:T(8,128)S(1)}, bf16[512,128]{1,0:T(8,128)(2,1)S(1)}) custom-call(bf16[1024,128]{1,0:T(8,128)(2,1)S(1)} %get-tuple-element.59.q_ref, bf16[1024,128]{1,0:T(8,128)(2,1)S(1)} %copy-done, f32[8,8,128]{2,1,0:T(8,128)S(1)} %get-tuple-element.64.stats_ref, ...), custom_call_target="tpu_custom_call", output_to_operand_aliasing={{0}: (4, {})} | custom-call | tf_op jit(solution)/shard_map/globals/pallas_call | solution.py:393
  47.0 0.0 collective-permute-done.9.refs_0_
  47.1 0.9 %collective-permute-start.10 = (bf16[512,128]{1,0:T(8,128)(2,1)S(1)}, bf16[512,128]{1,0:T(8,128)(2,1)S(1)}, u32[]{:S(2)}, u32[]{:S(2)}) collective-permute-start(bf16[512,128]{1,0:T(8,128)(2,1)S(1)} %get-tuple-element.102), channel_id=1, source_target_pairs={{0,4},{4,0},{8,12},{12,8},{16,20},{20,16},{24,28},{28,24},{1,5},{5... | collective-permute-start | bytes 393224 | tf_op jit(solution)/shard_map/ppermute | solution.py:390
  47.9 1.2 %randoms.10 = (bf16[512,128]{1,0:T(8,128)(2,1)S(1)}, f32[1024,128]{1,0:T(8,128)S(1)}, f32[1024,128]{1,0:T(8,128)S(1)}) custom-call(bf16[1072,128]{1,0:T(8,128)(2,1)S(1)} %collective-permute-done.9.refs_0_, bf16[1024,128]{1,0:T(8,128)(2,1)S(1)} %copy-done.1, bf16[1024,128]{1,0:T(8,128)(2,1)S(1)} %copy-done.2, ...), custom_call_target="tpu_custom_call", output_to_operand_aliasing={{1}: (4, {}), {2}: (5, {})} | custom-call | flops 3449999872 | tf_op jit(solution)/shard_map/randoms/pallas_call | solution.py:408
  49.1 3.0 %collective-permute-done.10 = bf16[512,128]{1,0:T(8,128)(2,1)S(1)} collective-permute-done((bf16[512,128]{1,0:T(8,128)(2,1)S(1)}, bf16[512,128]{1,0:T(8,128)(2,1)S(1)}, u32[]{:S(2)}, u32[]{:S(2)}) %collective-permute-start.10) | collective-permute-done | bytes 131104 | tf_op jit(solution)/shard_map/ppermute | solution.py:390
  52.1 2.3 %collective-permute-start.5 = (bf16[1072,128]{1,0:T(8,128)(2,1)S(1)}, bf16[1072,128]{1,0:T(8,128)(2,1)S(1)}, u32[]{:S(2)}, u32[]{:S(2)}) collective-permute-start(bf16[1072,128]{1,0:T(8,128)(2,1)S(1)} %get-tuple-element.81), channel_id=1, source_target_pairs={{0,12},{4,8},{8,4},{12,0},{16,28},{20,24},{24,20},{28,16},{1,13},{... | collective-permute-start | bytes 823304 | tf_op jit(solution)/shard_map/ppermute | solution.py:390
  54.4 0.1 collective-permute-start.13
  54.5 0.0 collective-permute-done.8.refs_1_
  54.5 2.2 %collective-permute-start.12 = (bf16[512,128]{1,0:T(8,128)(2,1)S(1)}, bf16[512,128]{1,0:T(8,128)(2,1)S(1)}, u32[]{:S(2)}, u32[]{:S(2)}) collective-permute-start(bf16[512,128]{1,0:T(8,128)(2,1)S(1)} %add_convert_fusion.2), channel_id=1, source_target_pairs={{0,8},{4,12},{8,0},{12,4},{16,24},{20,28},{24,16},{28,20},{1,9},{5... | collective-permute-start | bytes 393224 | tf_op jit(solution)/shard_map/ppermute | solution.py:390
  56.7 1.7 %randoms.11 = (bf16[384,128]{1,0:T(8,128)(2,1)S(1)}, bf16[384,128]{1,0:T(8,128)(2,1)S(1)}, f32[1024,128]{1,0:T(8,128)S(1)}, f32[1024,128]{1,0:T(8,128)S(1)}) custom-call(bf16[800,128]{1,0:T(8,128)(2,1)S(1)} %collective-permute-done.7.refs_0_, bf16[800,128]{1,0:T(8,128)(2,1)S(1)} %collective-permute-done.8.refs_1_, ...), custom_call_target="tpu_custom_call", output_to_operand_aliasing={{2}: (5, {}), {3}: (6, {})} | custom-call | flops 3449999872 | tf_op jit(solution)/shard_map/randoms/pallas_call | solution.py:408
  58.4 3.4 %collective-permute-start.15 = (bf16[384,128]{1,0:T(8,128)(2,1)S(1)}, bf16[384,128]{1,0:T(8,128)(2,1)S(1)}, u32[]{:S(2)}, u32[]{:S(2)}) collective-permute-start(bf16[384,128]{1,0:T(8,128)(2,1)S(1)} %get-tuple-element.109), channel_id=1, source_target_pairs={{0,24},{4,28},{8,16},{12,20},{16,8},{20,12},{24,0},{28,4},{1,25},{... | collective-permute-start | bytes 294920 | tf_op jit(solution)/shard_map/ppermute | solution.py:390
  61.8 0.0 collective-permute-start.17
  61.8 1.2 %randoms.12 = (bf16[512,128]{1,0:T(8,128)(2,1)S(1)}, f32[1024,128]{1,0:T(8,128)S(1)}, f32[1024,128]{1,0:T(8,128)S(1)}) custom-call(bf16[1072,128]{1,0:T(8,128)(2,1)S(1)} %collective-permute-done.6.refs_0_, bf16[1024,128]{1,0:T(8,128)(2,1)S(1)} %copy-done.1, bf16[1024,128]{1,0:T(8,128)(2,1)S(1)} %copy-done.2, ...), custom_call_target="tpu_custom_call", output_to_operand_aliasing={{1}: (4, {}), {2}: (5, {})} | custom-call | flops 3449999872 | tf_op jit(solution)/shard_map/randoms/pallas_call | solution.py:408
  63.0 0.4 collective-permute-done.13.refs_11_
  63.4 1.0 %collective-permute-start.19 = (bf16[512,128]{1,0:T(8,128)(2,1)S(1)}, bf16[512,128]{1,0:T(8,128)(2,1)S(1)}, u32[]{:S(2)}, u32[]{:S(2)}) collective-permute-start(bf16[512,128]{1,0:T(8,128)(2,1)S(1)} %get-tuple-element.114), channel_id=1, source_target_pairs={{0,28},{4,24},{8,20},{12,16},{16,12},{20,8},{24,4},{28,0},{1,29},{... | collective-permute-start | bytes 393224 | tf_op jit(solution)/shard_map/ppermute | solution.py:390
  64.4 2.0 %collective-permute-done.12 = bf16[512,128]{1,0:T(8,128)(2,1)S(1)} collective-permute-done((bf16[512,128]{1,0:T(8,128)(2,1)S(1)}, bf16[512,128]{1,0:T(8,128)(2,1)S(1)}, u32[]{:S(2)}, u32[]{:S(2)}) %collective-permute-start.12) | collective-permute-done | bytes 131104 | tf_op jit(solution)/shard_map/ppermute | solution.py:390
  66.5 0.9 %collective-permute-start.14 = (bf16[512,128]{1,0:T(8,128)(2,1)S(1)}, bf16[512,128]{1,0:T(8,128)(2,1)S(1)}, u32[]{:S(2)}, u32[]{:S(2)}) collective-permute-start(bf16[512,128]{1,0:T(8,128)(2,1)S(1)} %add_convert_fusion.1), channel_id=1, source_target_pairs={{0,16},{4,20},{8,24},{12,28},{16,0},{20,4},{24,8},{28,12},{1,17},{... | collective-permute-start | bytes 393224 | tf_op jit(solution)/shard_map/ppermute | solution.py:390
  67.3 0.0 collective-permute-done.5.refs_0_
  67.3 1.2 %randoms.13 = (bf16[512,128]{1,0:T(8,128)(2,1)S(1)}, f32[1024,128]{1,0:T(8,128)S(1)}, f32[1024,128]{1,0:T(8,128)S(1)}) custom-call(bf16[1072,128]{1,0:T(8,128)(2,1)S(1)} %collective-permute-done.5.refs_0_, bf16[1024,128]{1,0:T(8,128)(2,1)S(1)} %copy-done.1, bf16[1024,128]{1,0:T(8,128)(2,1)S(1)} %copy-done.2, ...), custom_call_target="tpu_custom_call", output_to_operand_aliasing={{1}: (4, {}), {2}: (5, {})} | custom-call | flops 3449999872 | tf_op jit(solution)/shard_map/randoms/pallas_call | solution.py:408
  68.5 4.5 %collective-permute-start.18 = (bf16[512,128]{1,0:T(8,128)(2,1)S(1)}, bf16[512,128]{1,0:T(8,128)(2,1)S(1)}, u32[]{:S(2)}, u32[]{:S(2)}) collective-permute-start(bf16[512,128]{1,0:T(8,128)(2,1)S(1)} %get-tuple-element.112), channel_id=1, source_target_pairs={{0,12},{4,8},{8,4},{12,0},{16,28},{20,24},{24,20},{28,16},{1,13},{... | collective-permute-start | bytes 393224 | tf_op jit(solution)/shard_map/ppermute | solution.py:390
  73.1 4.4 %collective-permute-done.14 = bf16[512,128]{1,0:T(8,128)(2,1)S(1)} collective-permute-done((bf16[512,128]{1,0:T(8,128)(2,1)S(1)}, bf16[512,128]{1,0:T(8,128)(2,1)S(1)}, u32[]{:S(2)}, u32[]{:S(2)}) %collective-permute-start.14) | collective-permute-done | bytes 131104 | tf_op jit(solution)/shard_map/ppermute | solution.py:390
  77.5 0.7 collective-permute-done.18.refs_9_
  78.2 1.9 %finish.1 = (bf16[1024,128]{1,0:T(8,128)(2,1)}, bf16[1024,128]{1,0:T(8,128)(2,1)}, bf16[1024,128]{1,0:T(8,128)(2,1)}) custom-call(f32[1024,128]{1,0:T(8,128)S(1)} %get-tuple-element.77.refs_0_, f32[1024,128]{1,0:T(8,128)S(1)} %get-tuple-element.100.refs_1_, f32[1024,128]{1,0:T(8,128)S(1)} %get-tuple-element.101.refs_2_, ...), custom_call_target="tpu_custom_call" | custom-call | flops 3449999872 | tf_op jit(solution)/shard_map/finish/pallas_call | solution.py:510
  (21 shorter events, 0.3 us)
Async XLA Ops:
  0.6 0.7 copy-start.3
  1.9 11.7 %collective-permute-start = (bf16[512,128]{1,0:T(8,128)(2,1)S(1)}, bf16[512,128]{1,0:T(8,128)(2,1)S(1)}, u32[]{:S(2)}, u32[]{:S(2)}) collective-permute-start(bf16[512,128]{1,0:T(8,128)(2,1)S(1)} %pick_globals.1), channel_id=1, source_target_pairs={{0,16},{4,20},{8,24},{12,28},{16,0},{20,4},{24,8},{28,12},{1,17},{... | collective-permute-start | bytes 393224 | tf_op jit(solution)/shard_map/ppermute | solution.py:390
  6.8 15.2 %copy-start.1 = (bf16[1024,128]{1,0:T(8,128)(2,1)S(1)}, bf16[1024,128]{1,0:T(8,128)(2,1)}, u32[]{:S(2)}) copy-start(bf16[1024,128]{1,0:T(8,128)(2,1)} %refs_1_.13) | copy-start | bytes 786436
  6.8 15.2 %copy-start.2 = (bf16[1024,128]{1,0:T(8,128)(2,1)S(1)}, bf16[1024,128]{1,0:T(8,128)(2,1)}, u32[]{:S(2)}) copy-start(bf16[1024,128]{1,0:T(8,128)(2,1)} %refs_2_.15) | copy-start | bytes 786436
  9.0 0.5 copy-start.4
  9.0 13.0 %copy-start = (bf16[1024,128]{1,0:T(8,128)(2,1)S(1)}, bf16[1024,128]{1,0:T(8,128)(2,1)}, u32[]{:S(2)}) copy-start(bf16[1024,128]{1,0:T(8,128)(2,1)} %g_ref.5) | copy-start | bytes 786436
  9.5 18.0 %collective-permute-start.2 = (bf16[800,128]{1,0:T(8,128)(2,1)S(1)}, bf16[800,128]{1,0:T(8,128)(2,1)S(1)}, u32[]{:S(2)}, u32[]{:S(2)}) collective-permute-start(bf16[800,128]{1,0:T(8,128)(2,1)S(1)} %get-tuple-element.63), channel_id=1, source_target_pairs={{0,16},{4,20},{8,24},{12,28},{16,0},{20,4},{24,8},{28,12},{1,17},{... | collective-permute-start | bytes 614408 | tf_op jit(solution)/shard_map/ppermute | solution.py:390
  9.5 37.5 %collective-permute-start.9 = (bf16[1072,128]{1,0:T(8,128)(2,1)S(1)}, bf16[1072,128]{1,0:T(8,128)(2,1)S(1)}, u32[]{:S(2)}, u32[]{:S(2)}) collective-permute-start(bf16[1072,128]{1,0:T(8,128)(2,1)S(1)} %get-tuple-element.89), channel_id=1, source_target_pairs={{0,4},{4,0},{8,12},{12,8},{16,20},{20,16},{24,28},{28,24},{1,5},{5... | collective-permute-start | bytes 823304 | tf_op jit(solution)/shard_map/ppermute | solution.py:390
  13.6 14.0 %collective-permute-start.1 = (bf16[512,128]{1,0:T(8,128)(2,1)S(1)}, bf16[512,128]{1,0:T(8,128)(2,1)S(1)}, u32[]{:S(2)}, u32[]{:S(2)}) collective-permute-start(bf16[512,128]{1,0:T(8,128)(2,1)S(1)} %add.18), channel_id=1, source_target_pairs={{0,8},{4,12},{8,0},{12,4},{16,24},{20,28},{24,16},{28,20},{1,9},{5... | collective-permute-start | bytes 393224 | tf_op jit(solution)/shard_map/ppermute | solution.py:390
  18.4 14.2 %collective-permute-start.4 = (bf16[800,128]{1,0:T(8,128)(2,1)S(1)}, bf16[800,128]{1,0:T(8,128)(2,1)S(1)}, u32[]{:S(2)}, u32[]{:S(2)}) collective-permute-start(bf16[800,128]{1,0:T(8,128)(2,1)S(1)} %get-tuple-element.80), channel_id=1, source_target_pairs={{0,20},{4,16},{8,28},{12,24},{16,4},{20,0},{24,12},{28,8},{1,21},{... | collective-permute-start | bytes 614408 | tf_op jit(solution)/shard_map/ppermute | solution.py:390
  27.5 27.0 %collective-permute-start.6 = (bf16[1072,128]{1,0:T(8,128)(2,1)S(1)}, bf16[1072,128]{1,0:T(8,128)(2,1)S(1)}, u32[]{:S(2)}, u32[]{:S(2)}) collective-permute-start(bf16[1072,128]{1,0:T(8,128)(2,1)S(1)} %get-tuple-element.83), channel_id=1, source_target_pairs={{0,28},{4,24},{8,20},{12,16},{16,12},{20,8},{24,4},{28,0},{1,29},{... | collective-permute-start | bytes 823304 | tf_op jit(solution)/shard_map/ppermute | solution.py:390
  29.6 24.8 %collective-permute-start.11 = (bf16[384,128]{1,0:T(8,128)(2,1)S(1)}, bf16[384,128]{1,0:T(8,128)(2,1)S(1)}, u32[]{:S(2)}, u32[]{:S(2)}) collective-permute-start(bf16[384,128]{1,0:T(8,128)(2,1)S(1)} %get-tuple-element.87), channel_id=1, source_target_pairs={{0,16},{4,20},{8,24},{12,28},{16,0},{20,4},{24,8},{28,12},{1,17},{... | collective-permute-start | bytes 294920 | tf_op jit(solution)/shard_map/ppermute | solution.py:390
  31.8 12.5 %collective-permute-start.3 = (bf16[512,128]{1,0:T(8,128)(2,1)S(1)}, bf16[512,128]{1,0:T(8,128)(2,1)S(1)}, u32[]{:S(2)}, u32[]{:S(2)}) collective-permute-start(bf16[512,128]{1,0:T(8,128)(2,1)S(1)} %add.19), channel_id=1, source_target_pairs={{0,4},{4,0},{8,12},{12,8},{16,20},{20,16},{24,28},{28,24},{1,5},{5... | collective-permute-start | bytes 393224 | tf_op jit(solution)/shard_map/ppermute | solution.py:390
  32.6 21.9 %collective-permute-start.8 = (bf16[800,128]{1,0:T(8,128)(2,1)S(1)}, bf16[800,128]{1,0:T(8,128)(2,1)S(1)}, u32[]{:S(2)}, u32[]{:S(2)}) collective-permute-start(bf16[800,128]{1,0:T(8,128)(2,1)S(1)} %get-tuple-element.88), channel_id=1, source_target_pairs={{0,24},{4,28},{8,16},{12,20},{16,8},{20,12},{24,0},{28,4},{1,25},{... | collective-permute-start | bytes 614408 | tf_op jit(solution)/shard_map/ppermute | solution.py:390
  44.4 12.4 %collective-permute-start.7 = (bf16[800,128]{1,0:T(8,128)(2,1)S(1)}, bf16[800,128]{1,0:T(8,128)(2,1)S(1)}, u32[]{:S(2)}, u32[]{:S(2)}) collective-permute-start(bf16[800,128]{1,0:T(8,128)(2,1)S(1)} %get-tuple-element.85), channel_id=1, source_target_pairs={{0,8},{4,12},{8,0},{12,4},{16,24},{20,28},{24,16},{28,20},{1,9},{5... | collective-permute-start | bytes 614408 | tf_op jit(solution)/shard_map/ppermute | solution.py:390
  47.1 5.0 %collective-permute-start.10 = (bf16[512,128]{1,0:T(8,128)(2,1)S(1)}, bf16[512,128]{1,0:T(8,128)(2,1)S(1)}, u32[]{:S(2)}, u32[]{:S(2)}) collective-permute-start(bf16[512,128]{1,0:T(8,128)(2,1)S(1)} %get-tuple-element.102), channel_id=1, source_target_pairs={{0,4},{4,0},{8,12},{12,8},{16,20},{20,16},{24,28},{28,24},{1,5},{5... | collective-permute-start | bytes 393224 | tf_op jit(solution)/shard_map/ppermute | solution.py:390
  52.1 15.2 %collective-permute-start.5 = (bf16[1072,128]{1,0:T(8,128)(2,1)S(1)}, bf16[1072,128]{1,0:T(8,128)(2,1)S(1)}, u32[]{:S(2)}, u32[]{:S(2)}) collective-permute-start(bf16[1072,128]{1,0:T(8,128)(2,1)S(1)} %get-tuple-element.81), channel_id=1, source_target_pairs={{0,12},{4,8},{8,4},{12,0},{16,28},{20,24},{24,20},{28,16},{1,13},{... | collective-permute-start | bytes 823304 | tf_op jit(solution)/shard_map/ppermute | solution.py:390
  54.4 9.0 %collective-permute-start.13 = (bf16[384,128]{1,0:T(8,128)(2,1)S(1)}, bf16[384,128]{1,0:T(8,128)(2,1)S(1)}, u32[]{:S(2)}, u32[]{:S(2)}) collective-permute-start(bf16[384,128]{1,0:T(8,128)(2,1)S(1)} %get-tuple-element.104), channel_id=1, source_target_pairs={{0,20},{4,16},{8,28},{12,24},{16,4},{20,0},{24,12},{28,8},{1,21},{... | collective-permute-start | bytes 294920 | tf_op jit(solution)/shard_map/ppermute | solution.py:390
  54.5 11.9 %collective-permute-start.12 = (bf16[512,128]{1,0:T(8,128)(2,1)S(1)}, bf16[512,128]{1,0:T(8,128)(2,1)S(1)}, u32[]{:S(2)}, u32[]{:S(2)}) collective-permute-start(bf16[512,128]{1,0:T(8,128)(2,1)S(1)} %add_convert_fusion.2), channel_id=1, source_target_pairs={{0,8},{4,12},{8,0},{12,4},{16,24},{20,28},{24,16},{28,20},{1,9},{5... | collective-permute-start | bytes 393224 | tf_op jit(solution)/shard_map/ppermute | solution.py:390
  58.4 14.7 %collective-permute-start.15 = (bf16[384,128]{1,0:T(8,128)(2,1)S(1)}, bf16[384,128]{1,0:T(8,128)(2,1)S(1)}, u32[]{:S(2)}, u32[]{:S(2)}) collective-permute-start(bf16[384,128]{1,0:T(8,128)(2,1)S(1)} %get-tuple-element.109), channel_id=1, source_target_pairs={{0,24},{4,28},{8,16},{12,20},{16,8},{20,12},{24,0},{28,4},{1,25},{... | collective-permute-start | bytes 294920 | tf_op jit(solution)/shard_map/ppermute | solution.py:390
  61.8 15.7 %collective-permute-start.17 = (bf16[384,128]{1,0:T(8,128)(2,1)S(1)}, bf16[384,128]{1,0:T(8,128)(2,1)S(1)}, u32[]{:S(2)}, u32[]{:S(2)}) collective-permute-start(bf16[384,128]{1,0:T(8,128)(2,1)S(1)} %get-tuple-element.111), channel_id=1, source_target_pairs={{0,8},{4,12},{8,0},{12,4},{16,24},{20,28},{24,16},{28,20},{1,9},{5... | collective-permute-start | bytes 294920 | tf_op jit(solution)/shard_map/ppermute | solution.py:390
  63.4 14.1 %collective-permute-start.19 = (bf16[512,128]{1,0:T(8,128)(2,1)S(1)}, bf16[512,128]{1,0:T(8,128)(2,1)S(1)}, u32[]{:S(2)}, u32[]{:S(2)}) collective-permute-start(bf16[512,128]{1,0:T(8,128)(2,1)S(1)} %get-tuple-element.114), channel_id=1, source_target_pairs={{0,28},{4,24},{8,20},{12,16},{16,12},{20,8},{24,4},{28,0},{1,29},{... | collective-permute-start | bytes 393224 | tf_op jit(solution)/shard_map/ppermute | solution.py:390
  66.5 11.0 %collective-permute-start.14 = (bf16[512,128]{1,0:T(8,128)(2,1)S(1)}, bf16[512,128]{1,0:T(8,128)(2,1)S(1)}, u32[]{:S(2)}, u32[]{:S(2)}) collective-permute-start(bf16[512,128]{1,0:T(8,128)(2,1)S(1)} %add_convert_fusion.1), channel_id=1, source_target_pairs={{0,16},{4,20},{8,24},{12,28},{16,0},{20,4},{24,8},{28,12},{1,17},{... | collective-permute-start | bytes 393224 | tf_op jit(solution)/shard_map/ppermute | solution.py:390
  68.5 9.7 %collective-permute-start.18 = (bf16[512,128]{1,0:T(8,128)(2,1)S(1)}, bf16[512,128]{1,0:T(8,128)(2,1)S(1)}, u32[]{:S(2)}, u32[]{:S(2)}) collective-permute-start(bf16[512,128]{1,0:T(8,128)(2,1)S(1)} %get-tuple-element.112), channel_id=1, source_target_pairs={{0,12},{4,8},{8,4},{12,0},{16,28},{20,24},{24,20},{28,16},{1,13},{... | collective-permute-start | bytes 393224 | tf_op jit(solution)/shard_map/ppermute | solution.py:390
  73.1 5.2 %collective-permute-start.16 = (bf16[512,128]{1,0:T(8,128)(2,1)S(1)}, bf16[512,128]{1,0:T(8,128)(2,1)S(1)}, u32[]{:S(2)}, u32[]{:S(2)}) collective-permute-start(bf16[512,128]{1,0:T(8,128)(2,1)S(1)} %get-tuple-element.110), channel_id=1, source_target_pairs={{0,4},{4,0},{8,12},{12,8},{16,20},{20,16},{24,28},{28,24},{1,5},{5... | collective-permute-start | bytes 393224 | tf_op jit(solution)/shard_map/ppermute | solution.py:390

commit v5 on v4

--- a/solution.py
+++ b/solution.py
@@ -85,10 +85,13 @@
     return -(-((2 * BLOCK + STAT + 1) * slots) // 16) * 16
 
 
-def pick_globals(blocks, k_hbm, v_hbm, glob_ref, own_ref, sems):
+def pick_globals(blocks, k_hbm, v_hbm, glob_hbm, own_ref, glob_ref, sems):
     many = glob_ref.shape[0]
     me = lax.axis_index("seq")
+    names = pltpu.make_async_copy(glob_hbm, glob_ref, sems.at[2 * many])
+    names.start()
     own_ref[...] = jnp.zeros_like(own_ref)
+    names.wait()
     for waiting in (False, True):
         for number in range(many):
             block = glob_ref[number]
@@ -356,10 +359,10 @@
         functools.partial(pick_globals, blocks),
         jax.ShapeDtypeStruct((2 * many * BLOCK, features), BF16),
         VMEM,
-        [HBM] * 2 + [SMEM],
-        [pltpu.SemaphoreType.DMA((2 * many,))],
+        [HBM] * 3,
+        [pltpu.SMEM(glob_blocks.shape, jnp.int32), pltpu.SemaphoreType.DMA((2 * many + 1,))],
         "pick_globals",
-    )(*in_hbm(keys, values), glob_blocks)
+    )(*in_hbm(keys, values, glob_blocks))
     packed = call(
         lambda *refs: pack(heads, plan, refs),
         [

time: 80.6 us -> 80.1 us (level)
  starting transfers between devices: 43.6 us -> 46 us
  waiting for transfers between devices: 13.5 us -> 11.3 us
    ppermute x20, starting transfers between devices: 43.6 us -> 46 us  [swap(): return lax.ppermute(array, 'seq', [(i, i ^ k) for i in range(owners)])]
    ppermute x20, waiting for transfers between devices: 13.5 us -> 11.3 us  [swap(): return lax.ppermute(array, 'seq', [(i, i ^ k) for i in range(owners)])]
  transfers between devices with their start and end apart: 20 -> 20, of which waited for: 6 -> 5; matrix products, arithmetic and copies ran while one was open for 0% -> 0% of each run, Pallas kernels for 23% -> 23%
where the time goes in v5:
time: 80.1 us; the launch traced here: 79.9 us
  starting transfers between devices  46 us (57%)
  Pallas kernels  21 us (26%)
  waiting for transfers between devices  11.3 us (14%)
  between operations  0.89 us (1%)
    ppermute x20, starting transfers between devices, swap(): return lax.ppermute(array, 'seq', [(i, i ^ k) for i in range(owners)])  46 us
    ppermute x20, waiting for transfers between devices, swap(): return lax.ppermute(array, 'seq', [(i, i ^ k) for i in range(owners)])  11.3 us
    pallas_call x7, Pallas kernels, owned(): call(lambda *refs: randoms(heads, counts, refs), shapes + [wide, wide], [...  8.07 us
    pallas_call x2, Pallas kernels, add_window(): call(functools.partial(window, heads, first, last), [wide] * 3, [VMEM] *...  5.51 us
    pallas_call x1, Pallas kernels, add_globals(): call(functools.partial(globals_, heads), [wide, jax.ShapeDtypeStruct(own....  2.54 us
    pallas_call x1, Pallas kernels, shards(): call(lambda *refs: pack(heads, plan, refs), [whole, jax.ShapeDtypeStruct(...  2.18 us
    pallas_call x1, Pallas kernels, shards(): call(lambda *refs: finish(ret_slots, refs), [whole] * 3, [HBM] * 3, [VMEM...  1.94 us
  transfers between devices with their start and end apart: 20, of which 5 were waited for; matrix products, arithmetic and copies ran while one was open for 0% of the time, Pallas kernels for 23%

profile of v5, /device:TPU:0, one launch (start us, length us, event | category | flops | bytes accessed | tf_op | source)
XLA Modules:
  0.0 79.9 jit_solution(4061086574023085866)
XLA Ops:
  0.6 0.7 pick_globals.1
  1.4 4.1 %collective-permute-start = (bf16[512,128]{1,0:T(8,128)(2,1)S(1)}, bf16[512,128]{1,0:T(8,128)(2,1)S(1)}, u32[]{:S(2)}, u32[]{:S(2)}) collective-permute-start(bf16[512,128]{1,0:T(8,128)(2,1)S(1)} %pick_globals.1), channel_id=1, source_target_pairs={{0,16},{4,20},{8,24},{12,28},{16,0},{20,4},{24,8},{28,12},{1,17},{... | collective-permute-start | bytes 393224 | tf_op jit(solution)/shard_map/ppermute | solution.py:393
  5.5 2.2 %pack.1 = (bf16[1024,128]{1,0:T(8,128)(2,1)S(1)}, f32[8,8,128]{2,1,0:T(8,128)S(1)}, bf16[1024,128]{1,0:T(8,128)(2,1)S(1)}, s32[27]{0:T(128)S(1)}, bf16[800,128]{...) custom-call(bf16[1024,128]{1,0:T(8,128)(2,1)} %refs_0_.1, ...), custom_call_target="tpu_custom_call" | custom-call | tf_op jit(solution)/shard_map/pack/pallas_call | solution.py:366
  7.7 0.0 copy-start
  7.7 0.5 copy-done.3
  8.2 0.0 collective-permute-start.2
  8.3 1.8 %collective-permute-start.9 = (bf16[1072,128]{1,0:T(8,128)(2,1)S(1)}, bf16[1072,128]{1,0:T(8,128)(2,1)S(1)}, u32[]{:S(2)}, u32[]{:S(2)}) collective-permute-start(bf16[1072,128]{1,0:T(8,128)(2,1)S(1)} %get-tuple-element.89), channel_id=1, source_target_pairs={{0,4},{4,0},{8,12},{12,8},{16,20},{20,16},{24,28},{28,24},{1,5},{5... | collective-permute-start | bytes 823304 | tf_op jit(solution)/shard_map/ppermute | solution.py:393
  10.1 2.2 %collective-permute-done = bf16[512,128]{1,0:T(8,128)(2,1)S(1)} collective-permute-done((bf16[512,128]{1,0:T(8,128)(2,1)S(1)}, bf16[512,128]{1,0:T(8,128)(2,1)S(1)}, u32[]{:S(2)}, u32[]{:S(2)}) %collective-permute-start) | collective-permute-done | bytes 131104 | tf_op jit(solution)/shard_map/ppermute | solution.py:393
  12.3 4.8 %collective-permute-start.1 = (bf16[512,128]{1,0:T(8,128)(2,1)S(1)}, bf16[512,128]{1,0:T(8,128)(2,1)S(1)}, u32[]{:S(2)}, u32[]{:S(2)}) collective-permute-start(bf16[512,128]{1,0:T(8,128)(2,1)S(1)} %add.18), channel_id=1, source_target_pairs={{0,8},{4,12},{8,0},{12,4},{16,24},{20,28},{24,16},{28,20},{1,9},{5... | collective-permute-start | bytes 393224 | tf_op jit(solution)/shard_map/ppermute | solution.py:393
  17.1 4.3 %collective-permute-start.4 = (bf16[800,128]{1,0:T(8,128)(2,1)S(1)}, bf16[800,128]{1,0:T(8,128)(2,1)S(1)}, u32[]{:S(2)}, u32[]{:S(2)}) collective-permute-start(bf16[800,128]{1,0:T(8,128)(2,1)S(1)} %get-tuple-element.80), channel_id=1, source_target_pairs={{0,20},{4,16},{8,28},{12,24},{16,4},{20,0},{24,12},{28,8},{1,21},{... | collective-permute-start | bytes 614408 | tf_op jit(solution)/shard_map/ppermute | solution.py:393
  21.4 2.8 %window.2 = (f32[1024,128]{1,0:T(8,128)S(1)}, f32[1024,128]{1,0:T(8,128)S(1)}, f32[1024,128]{1,0:T(8,128)S(1)}) custom-call(bf16[1024,128]{1,0:T(8,128)(2,1)S(1)} %get-tuple-element.59.q_ref, bf16[1024,128]{1,0:T(8,128)(2,1)S(1)} %copy-done, f32[8,8,128]{2,1,0:T(8,128)S(1)} %get-tuple-element.64.stats_ref, bf16[1024,128]{1,0:T(8,128)(2,1)S(1)} %copy-done.1, ...), custom_call_target="tpu_custom_call" | custom-call | flops 3449999872 | tf_op jit(solution)/shard_map/window/pallas_call | solution.py:426
  24.2 2.8 %window.3 = (f32[1024,128]{1,0:T(8,128)S(1)}, f32[1024,128]{1,0:T(8,128)S(1)}, f32[1024,128]{1,0:T(8,128)S(1)}) custom-call(bf16[1024,128]{1,0:T(8,128)(2,1)S(1)} %get-tuple-element.59.q_ref, bf16[1024,128]{1,0:T(8,128)(2,1)S(1)} %copy-done, ...), custom_call_target="tpu_custom_call", output_to_operand_aliasing={{0}: (6, {}), {1}: (7, {}), {2}: (8, {})} | custom-call | flops 3449999872 | tf_op jit(solution)/shard_map/window/pallas_call | solution.py:426
  27.0 0.1 collective-permute-start.6
  27.1 0.0 collective-permute-done.1
  27.1 0.9 %randoms.7 = (bf16[384,128]{1,0:T(8,128)(2,1)S(1)}, f32[1024,128]{1,0:T(8,128)S(1)}, f32[1024,128]{1,0:T(8,128)S(1)}) custom-call(bf16[800,128]{1,0:T(8,128)(2,1)S(1)} %collective-permute-done.2.refs_0_, bf16[1024,128]{1,0:T(8,128)(2,1)S(1)} %copy-done.1, bf16[1024,128]{1,0:T(8,128)(2,1)S(1)} %copy-done.2, ...), custom_call_target="tpu_custom_call", output_to_operand_aliasing={{1}: (4, {}), {2}: (5, {})} | custom-call | flops 3449999872 | tf_op jit(solution)/shard_map/randoms/pallas_call | solution.py:411
  28.1 1.0 %randoms.8 = (bf16[384,128]{1,0:T(8,128)(2,1)S(1)}, f32[1024,128]{1,0:T(8,128)S(1)}, f32[1024,128]{1,0:T(8,128)S(1)}) custom-call(bf16[800,128]{1,0:T(8,128)(2,1)S(1)} %get-tuple-element.61.refs_0_, bf16[1024,128]{1,0:T(8,128)(2,1)S(1)} %copy-done.1, bf16[1024,128]{1,0:T(8,128)(2,1)S(1)} %copy-done.2, ...), custom_call_target="tpu_custom_call", output_to_operand_aliasing={{1}: (4, {}), {2}: (5, {})} | custom-call | flops 3449999872 | tf_op jit(solution)/shard_map/randoms/pallas_call | solution.py:411
  29.0 1.5 %collective-permute-start.11 = (bf16[384,128]{1,0:T(8,128)(2,1)S(1)}, bf16[384,128]{1,0:T(8,128)(2,1)S(1)}, u32[]{:S(2)}, u32[]{:S(2)}) collective-permute-start(bf16[384,128]{1,0:T(8,128)(2,1)S(1)} %get-tuple-element.87), channel_id=1, source_target_pairs={{0,16},{4,20},{8,24},{12,28},{16,0},{20,4},{24,8},{28,12},{1,17},{... | collective-permute-start | bytes 294920 | tf_op jit(solution)/shard_map/ppermute | solution.py:393
  30.5 1.5 %collective-permute-start.3 = (bf16[512,128]{1,0:T(8,128)(2,1)S(1)}, bf16[512,128]{1,0:T(8,128)(2,1)S(1)}, u32[]{:S(2)}, u32[]{:S(2)}) collective-permute-start(bf16[512,128]{1,0:T(8,128)(2,1)S(1)} %add.19), channel_id=1, source_target_pairs={{0,4},{4,0},{8,12},{12,8},{16,20},{20,16},{24,28},{28,24},{1,5},{5... | collective-permute-start | bytes 393224 | tf_op jit(solution)/shard_map/ppermute | solution.py:393
  32.1 0.0 collective-permute-done.4.refs_0_
  32.1 10.1 %collective-permute-start.8 = (bf16[800,128]{1,0:T(8,128)(2,1)S(1)}, bf16[800,128]{1,0:T(8,128)(2,1)S(1)}, u32[]{:S(2)}, u32[]{:S(2)}) collective-permute-start(bf16[800,128]{1,0:T(8,128)(2,1)S(1)} %get-tuple-element.88), channel_id=1, source_target_pairs={{0,24},{4,28},{8,16},{12,20},{16,8},{20,12},{24,0},{28,4},{1,25},{... | collective-permute-start | bytes 614408 | tf_op jit(solution)/shard_map/ppermute | solution.py:393
  42.2 0.9 %randoms.9 = (bf16[384,128]{1,0:T(8,128)(2,1)S(1)}, f32[1024,128]{1,0:T(8,128)S(1)}, f32[1024,128]{1,0:T(8,128)S(1)}) custom-call(bf16[800,128]{1,0:T(8,128)(2,1)S(1)} %collective-permute-done.4.refs_0_, bf16[1024,128]{1,0:T(8,128)(2,1)S(1)} %copy-done.1, bf16[1024,128]{1,0:T(8,128)(2,1)S(1)} %copy-done.2, ...), custom_call_target="tpu_custom_call", output_to_operand_aliasing={{1}: (4, {}), {2}: (5, {})} | custom-call | flops 3449999872 | tf_op jit(solution)/shard_map/randoms/pallas_call | solution.py:411
  43.1 0.0 collective-permute-done.3
  43.1 0.1 collective-permute-start.7
  43.3 2.5 %globals.1 = (f32[1024,128]{1,0:T(8,128)S(1)}, bf16[512,128]{1,0:T(8,128)(2,1)S(1)}) custom-call(bf16[1024,128]{1,0:T(8,128)(2,1)S(1)} %get-tuple-element.59.q_ref, bf16[1024,128]{1,0:T(8,128)(2,1)S(1)} %copy-done, f32[8,8,128]{2,1,0:T(8,128)S(1)} %get-tuple-element.64.stats_ref, ...), custom_call_target="tpu_custom_call", output_to_operand_aliasing={{0}: (4, {})} | custom-call | tf_op jit(solution)/shard_map/globals/pallas_call | solution.py:396
  45.8 0.0 collective-permute-done.9.refs_0_
  45.8 1.5 %collective-permute-start.10 = (bf16[512,128]{1,0:T(8,128)(2,1)S(1)}, bf16[512,128]{1,0:T(8,128)(2,1)S(1)}, u32[]{:S(2)}, u32[]{:S(2)}) collective-permute-start(bf16[512,128]{1,0:T(8,128)(2,1)S(1)} %get-tuple-element.102), channel_id=1, source_target_pairs={{0,4},{4,0},{8,12},{12,8},{16,20},{20,16},{24,28},{28,24},{1,5},{5... | collective-permute-start | bytes 393224 | tf_op jit(solution)/shard_map/ppermute | solution.py:393
  47.4 1.2 %randoms.10 = (bf16[512,128]{1,0:T(8,128)(2,1)S(1)}, f32[1024,128]{1,0:T(8,128)S(1)}, f32[1024,128]{1,0:T(8,128)S(1)}) custom-call(bf16[1072,128]{1,0:T(8,128)(2,1)S(1)} %collective-permute-done.9.refs_0_, bf16[1024,128]{1,0:T(8,128)(2,1)S(1)} %copy-done.1, bf16[1024,128]{1,0:T(8,128)(2,1)S(1)} %copy-done.2, ...), custom_call_target="tpu_custom_call", output_to_operand_aliasing={{1}: (4, {}), {2}: (5, {})} | custom-call | flops 3449999872 | tf_op jit(solution)/shard_map/randoms/pallas_call | solution.py:411
  48.5 2.3 %collective-permute-done.10 = bf16[512,128]{1,0:T(8,128)(2,1)S(1)} collective-permute-done((bf16[512,128]{1,0:T(8,128)(2,1)S(1)}, bf16[512,128]{1,0:T(8,128)(2,1)S(1)}, u32[]{:S(2)}, u32[]{:S(2)}) %collective-permute-start.10) | collective-permute-done | bytes 131104 | tf_op jit(solution)/shard_map/ppermute | solution.py:393
  50.9 2.9 %collective-permute-start.5 = (bf16[1072,128]{1,0:T(8,128)(2,1)S(1)}, bf16[1072,128]{1,0:T(8,128)(2,1)S(1)}, u32[]{:S(2)}, u32[]{:S(2)}) collective-permute-start(bf16[1072,128]{1,0:T(8,128)(2,1)S(1)} %get-tuple-element.81), channel_id=1, source_target_pairs={{0,12},{4,8},{8,4},{12,0},{16,28},{20,24},{24,20},{28,16},{1,13},{... | collective-permute-start | bytes 823304 | tf_op jit(solution)/shard_map/ppermute | solution.py:393
  53.8 0.0 collective-permute-done.11.refs_10_
  53.8 2.7 %collective-permute-start.13 = (bf16[384,128]{1,0:T(8,128)(2,1)S(1)}, bf16[384,128]{1,0:T(8,128)(2,1)S(1)}, u32[]{:S(2)}, u32[]{:S(2)}) collective-permute-start(bf16[384,128]{1,0:T(8,128)(2,1)S(1)} %get-tuple-element.104), channel_id=1, source_target_pairs={{0,20},{4,16},{8,28},{12,24},{16,4},{20,0},{24,12},{28,8},{1,21},{... | collective-permute-start | bytes 294920 | tf_op jit(solution)/shard_map/ppermute | solution.py:393
  56.5 0.0 collective-permute-done.7.refs_0_
  56.5 1.7 %randoms.11 = (bf16[384,128]{1,0:T(8,128)(2,1)S(1)}, bf16[384,128]{1,0:T(8,128)(2,1)S(1)}, f32[1024,128]{1,0:T(8,128)S(1)}, f32[1024,128]{1,0:T(8,128)S(1)}) custom-call(bf16[800,128]{1,0:T(8,128)(2,1)S(1)} %collective-permute-done.7.refs_0_, bf16[800,128]{1,0:T(8,128)(2,1)S(1)} %collective-permute-done.8.refs_1_, ...), custom_call_target="tpu_custom_call", output_to_operand_aliasing={{2}: (5, {}), {3}: (6, {})} | custom-call | flops 3449999872 | tf_op jit(solution)/shard_map/randoms/pallas_call | solution.py:411
  58.2 2.3 %collective-permute-start.15 = (bf16[384,128]{1,0:T(8,128)(2,1)S(1)}, bf16[384,128]{1,0:T(8,128)(2,1)S(1)}, u32[]{:S(2)}, u32[]{:S(2)}) collective-permute-start(bf16[384,128]{1,0:T(8,128)(2,1)S(1)} %get-tuple-element.109), channel_id=1, source_target_pairs={{0,24},{4,28},{8,16},{12,20},{16,8},{20,12},{24,0},{28,4},{1,25},{... | collective-permute-start | bytes 294920 | tf_op jit(solution)/shard_map/ppermute | solution.py:393
  60.5 0.4 collective-permute-start.17
  60.9 1.2 %randoms.12 = (bf16[512,128]{1,0:T(8,128)(2,1)S(1)}, f32[1024,128]{1,0:T(8,128)S(1)}, f32[1024,128]{1,0:T(8,128)S(1)}) custom-call(bf16[1072,128]{1,0:T(8,128)(2,1)S(1)} %collective-permute-done.6.refs_0_, bf16[1024,128]{1,0:T(8,128)(2,1)S(1)} %copy-done.1, bf16[1024,128]{1,0:T(8,128)(2,1)S(1)} %copy-done.2, ...), custom_call_target="tpu_custom_call", output_to_operand_aliasing={{1}: (4, {}), {2}: (5, {})} | custom-call | flops 3449999872 | tf_op jit(solution)/shard_map/randoms/pallas_call | solution.py:411
  62.1 0.9 %collective-permute-done.13.refs_11_ = bf16[384,128]{1,0:T(8,128)(2,1)S(1)} collective-permute-done((bf16[384,128]{1,0:T(8,128)(2,1)S(1)}, bf16[384,128]{1,0:T(8,128)(2,1)S(1)}, u32[]{:S(2)}, u32[]{:S(2)}) %collective-permute-start.13) | collective-permute-done | bytes 98336 | tf_op jit(solution)/shard_map/ppermute | solution.py:393
  63.0 3.2 %collective-permute-start.19 = (bf16[512,128]{1,0:T(8,128)(2,1)S(1)}, bf16[512,128]{1,0:T(8,128)(2,1)S(1)}, u32[]{:S(2)}, u32[]{:S(2)}) collective-permute-start(bf16[512,128]{1,0:T(8,128)(2,1)S(1)} %get-tuple-element.114), channel_id=1, source_target_pairs={{0,28},{4,24},{8,20},{12,16},{16,12},{20,8},{24,4},{28,0},{1,29},{... | collective-permute-start | bytes 393224 | tf_op jit(solution)/shard_map/ppermute | solution.py:393
  66.3 0.6 collective-permute-done.12
  66.9 1.8 %collective-permute-start.14 = (bf16[512,128]{1,0:T(8,128)(2,1)S(1)}, bf16[512,128]{1,0:T(8,128)(2,1)S(1)}, u32[]{:S(2)}, u32[]{:S(2)}) collective-permute-start(bf16[512,128]{1,0:T(8,128)(2,1)S(1)} %add_convert_fusion.1), channel_id=1, source_target_pairs={{0,16},{4,20},{8,24},{12,28},{16,0},{20,4},{24,8},{28,12},{1,17},{... | collective-permute-start | bytes 393224 | tf_op jit(solution)/shard_map/ppermute | solution.py:393
  68.8 0.0 collective-permute-done.5.refs_0_
  68.8 1.2 %randoms.13 = (bf16[512,128]{1,0:T(8,128)(2,1)S(1)}, f32[1024,128]{1,0:T(8,128)S(1)}, f32[1024,128]{1,0:T(8,128)S(1)}) custom-call(bf16[1072,128]{1,0:T(8,128)(2,1)S(1)} %collective-permute-done.5.refs_0_, bf16[1024,128]{1,0:T(8,128)(2,1)S(1)} %copy-done.1, bf16[1024,128]{1,0:T(8,128)(2,1)S(1)} %copy-done.2, ...), custom_call_target="tpu_custom_call", output_to_operand_aliasing={{1}: (4, {}), {2}: (5, {})} | custom-call | flops 3449999872 | tf_op jit(solution)/shard_map/randoms/pallas_call | solution.py:411
  70.0 0.6 collective-permute-start.18
  70.5 2.2 %collective-permute-start.16 = (bf16[512,128]{1,0:T(8,128)(2,1)S(1)}, bf16[512,128]{1,0:T(8,128)(2,1)S(1)}, u32[]{:S(2)}, u32[]{:S(2)}) collective-permute-start(bf16[512,128]{1,0:T(8,128)(2,1)S(1)} %get-tuple-element.110), channel_id=1, source_target_pairs={{0,4},{4,0},{8,12},{12,8},{16,20},{20,16},{24,28},{28,24},{1,5},{5... | collective-permute-start | bytes 393224 | tf_op jit(solution)/shard_map/ppermute | solution.py:393
  72.7 5.2 %collective-permute-done.14 = bf16[512,128]{1,0:T(8,128)(2,1)S(1)} collective-permute-done((bf16[512,128]{1,0:T(8,128)(2,1)S(1)}, bf16[512,128]{1,0:T(8,128)(2,1)S(1)}, u32[]{:S(2)}, u32[]{:S(2)}) %collective-permute-start.14) | collective-permute-done | bytes 131104 | tf_op jit(solution)/shard_map/ppermute | solution.py:393
  77.9 0.0 collective-permute-done.17.refs_8_
  77.9 0.0 collective-permute-done.18.refs_9_
  78.0 1.9 %finish.1 = (bf16[1024,128]{1,0:T(8,128)(2,1)}, bf16[1024,128]{1,0:T(8,128)(2,1)}, bf16[1024,128]{1,0:T(8,128)(2,1)}) custom-call(f32[1024,128]{1,0:T(8,128)S(1)} %get-tuple-element.77.refs_0_, f32[1024,128]{1,0:T(8,128)S(1)} %get-tuple-element.100.refs_1_, f32[1024,128]{1,0:T(8,128)S(1)} %get-tuple-element.101.refs_2_, ...), custom_call_target="tpu_custom_call" | custom-call | flops 3449999872 | tf_op jit(solution)/shard_map/finish/pallas_call | solution.py:513
  (19 shorter events, 0.3 us)
Async XLA Ops:
  1.4 10.9 %collective-permute-start = (bf16[512,128]{1,0:T(8,128)(2,1)S(1)}, bf16[512,128]{1,0:T(8,128)(2,1)S(1)}, u32[]{:S(2)}, u32[]{:S(2)}) collective-permute-start(bf16[512,128]{1,0:T(8,128)(2,1)S(1)} %pick_globals.1), channel_id=1, source_target_pairs={{0,16},{4,20},{8,24},{12,28},{16,0},{20,4},{24,8},{28,12},{1,17},{... | collective-permute-start | bytes 393224 | tf_op jit(solution)/shard_map/ppermute | solution.py:393
  5.5 16.0 %copy-start.1 = (bf16[1024,128]{1,0:T(8,128)(2,1)S(1)}, bf16[1024,128]{1,0:T(8,128)(2,1)}, u32[]{:S(2)}) copy-start(bf16[1024,128]{1,0:T(8,128)(2,1)} %refs_1_.13) | copy-start | bytes 786436
  5.5 16.0 %copy-start.2 = (bf16[1024,128]{1,0:T(8,128)(2,1)S(1)}, bf16[1024,128]{1,0:T(8,128)(2,1)}, u32[]{:S(2)}) copy-start(bf16[1024,128]{1,0:T(8,128)(2,1)} %refs_2_.15) | copy-start | bytes 786436
  7.7 0.5 copy-start.3
  7.7 13.8 %copy-start = (bf16[1024,128]{1,0:T(8,128)(2,1)S(1)}, bf16[1024,128]{1,0:T(8,128)(2,1)}, u32[]{:S(2)}) copy-start(bf16[1024,128]{1,0:T(8,128)(2,1)} %g_ref.5) | copy-start | bytes 786436
  8.2 18.7 %collective-permute-start.2 = (bf16[800,128]{1,0:T(8,128)(2,1)S(1)}, bf16[800,128]{1,0:T(8,128)(2,1)S(1)}, u32[]{:S(2)}, u32[]{:S(2)}) collective-permute-start(bf16[800,128]{1,0:T(8,128)(2,1)S(1)} %get-tuple-element.63), channel_id=1, source_target_pairs={{0,16},{4,20},{8,24},{12,28},{16,0},{20,4},{24,8},{28,12},{1,17},{... | collective-permute-start | bytes 614408 | tf_op jit(solution)/shard_map/ppermute | solution.py:393
  8.3 37.6 %collective-permute-start.9 = (bf16[1072,128]{1,0:T(8,128)(2,1)S(1)}, bf16[1072,128]{1,0:T(8,128)(2,1)S(1)}, u32[]{:S(2)}, u32[]{:S(2)}) collective-permute-start(bf16[1072,128]{1,0:T(8,128)(2,1)S(1)} %get-tuple-element.89), channel_id=1, source_target_pairs={{0,4},{4,0},{8,12},{12,8},{16,20},{20,16},{24,28},{28,24},{1,5},{5... | collective-permute-start | bytes 823304 | tf_op jit(solution)/shard_map/ppermute | solution.py:393
  12.3 14.8 %collective-permute-start.1 = (bf16[512,128]{1,0:T(8,128)(2,1)S(1)}, bf16[512,128]{1,0:T(8,128)(2,1)S(1)}, u32[]{:S(2)}, u32[]{:S(2)}) collective-permute-start(bf16[512,128]{1,0:T(8,128)(2,1)S(1)} %add.18), channel_id=1, source_target_pairs={{0,8},{4,12},{8,0},{12,4},{16,24},{20,28},{24,16},{28,20},{1,9},{5... | collective-permute-start | bytes 393224 | tf_op jit(solution)/shard_map/ppermute | solution.py:393
  17.1 15.0 %collective-permute-start.4 = (bf16[800,128]{1,0:T(8,128)(2,1)S(1)}, bf16[800,128]{1,0:T(8,128)(2,1)S(1)}, u32[]{:S(2)}, u32[]{:S(2)}) collective-permute-start(bf16[800,128]{1,0:T(8,128)(2,1)S(1)} %get-tuple-element.80), channel_id=1, source_target_pairs={{0,20},{4,16},{8,28},{12,24},{16,4},{20,0},{24,12},{28,8},{1,21},{... | collective-permute-start | bytes 614408 | tf_op jit(solution)/shard_map/ppermute | solution.py:393
  27.0 29.5 %collective-permute-start.6 = (bf16[1072,128]{1,0:T(8,128)(2,1)S(1)}, bf16[1072,128]{1,0:T(8,128)(2,1)S(1)}, u32[]{:S(2)}, u32[]{:S(2)}) collective-permute-start(bf16[1072,128]{1,0:T(8,128)(2,1)S(1)} %get-tuple-element.83), channel_id=1, source_target_pairs={{0,28},{4,24},{8,20},{12,16},{16,12},{20,8},{24,4},{28,0},{1,29},{... | collective-permute-start | bytes 823304 | tf_op jit(solution)/shard_map/ppermute | solution.py:393
  29.0 24.8 %collective-permute-start.11 = (bf16[384,128]{1,0:T(8,128)(2,1)S(1)}, bf16[384,128]{1,0:T(8,128)(2,1)S(1)}, u32[]{:S(2)}, u32[]{:S(2)}) collective-permute-start(bf16[384,128]{1,0:T(8,128)(2,1)S(1)} %get-tuple-element.87), channel_id=1, source_target_pairs={{0,16},{4,20},{8,24},{12,28},{16,0},{20,4},{24,8},{28,12},{1,17},{... | collective-permute-start | bytes 294920 | tf_op jit(solution)/shard_map/ppermute | solution.py:393
  30.5 12.6 %collective-permute-start.3 = (bf16[512,128]{1,0:T(8,128)(2,1)S(1)}, bf16[512,128]{1,0:T(8,128)(2,1)S(1)}, u32[]{:S(2)}, u32[]{:S(2)}) collective-permute-start(bf16[512,128]{1,0:T(8,128)(2,1)S(1)} %add.19), channel_id=1, source_target_pairs={{0,4},{4,0},{8,12},{12,8},{16,20},{20,16},{24,28},{28,24},{1,5},{5... | collective-permute-start | bytes 393224 | tf_op jit(solution)/shard_map/ppermute | solution.py:393
  32.1 24.4 %collective-permute-start.8 = (bf16[800,128]{1,0:T(8,128)(2,1)S(1)}, bf16[800,128]{1,0:T(8,128)(2,1)S(1)}, u32[]{:S(2)}, u32[]{:S(2)}) collective-permute-start(bf16[800,128]{1,0:T(8,128)(2,1)S(1)} %get-tuple-element.88), channel_id=1, source_target_pairs={{0,24},{4,28},{8,16},{12,20},{16,8},{20,12},{24,0},{28,4},{1,25},{... | collective-permute-start | bytes 614408 | tf_op jit(solution)/shard_map/ppermute | solution.py:393
  43.1 13.4 %collective-permute-start.7 = (bf16[800,128]{1,0:T(8,128)(2,1)S(1)}, bf16[800,128]{1,0:T(8,128)(2,1)S(1)}, u32[]{:S(2)}, u32[]{:S(2)}) collective-permute-start(bf16[800,128]{1,0:T(8,128)(2,1)S(1)} %get-tuple-element.85), channel_id=1, source_target_pairs={{0,8},{4,12},{8,0},{12,4},{16,24},{20,28},{24,16},{28,20},{1,9},{5... | collective-permute-start | bytes 614408 | tf_op jit(solution)/shard_map/ppermute | solution.py:393
  45.8 5.0 %collective-permute-start.10 = (bf16[512,128]{1,0:T(8,128)(2,1)S(1)}, bf16[512,128]{1,0:T(8,128)(2,1)S(1)}, u32[]{:S(2)}, u32[]{:S(2)}) collective-permute-start(bf16[512,128]{1,0:T(8,128)(2,1)S(1)} %get-tuple-element.102), channel_id=1, source_target_pairs={{0,4},{4,0},{8,12},{12,8},{16,20},{20,16},{24,28},{28,24},{1,5},{5... | collective-permute-start | bytes 393224 | tf_op jit(solution)/shard_map/ppermute | solution.py:393
  50.9 17.9 %collective-permute-start.5 = (bf16[1072,128]{1,0:T(8,128)(2,1)S(1)}, bf16[1072,128]{1,0:T(8,128)(2,1)S(1)}, u32[]{:S(2)}, u32[]{:S(2)}) collective-permute-start(bf16[1072,128]{1,0:T(8,128)(2,1)S(1)} %get-tuple-element.81), channel_id=1, source_target_pairs={{0,12},{4,8},{8,4},{12,0},{16,28},{20,24},{24,20},{28,16},{1,13},{... | collective-permute-start | bytes 823304 | tf_op jit(solution)/shard_map/ppermute | solution.py:393
  53.8 9.2 %collective-permute-start.13 = (bf16[384,128]{1,0:T(8,128)(2,1)S(1)}, bf16[384,128]{1,0:T(8,128)(2,1)S(1)}, u32[]{:S(2)}, u32[]{:S(2)}) collective-permute-start(bf16[384,128]{1,0:T(8,128)(2,1)S(1)} %get-tuple-element.104), channel_id=1, source_target_pairs={{0,20},{4,16},{8,28},{12,24},{16,4},{20,0},{24,12},{28,8},{1,21},{... | collective-permute-start | bytes 294920 | tf_op jit(solution)/shard_map/ppermute | solution.py:393
  56.5 10.4 %collective-permute-start.12 = (bf16[512,128]{1,0:T(8,128)(2,1)S(1)}, bf16[512,128]{1,0:T(8,128)(2,1)S(1)}, u32[]{:S(2)}, u32[]{:S(2)}) collective-permute-start(bf16[512,128]{1,0:T(8,128)(2,1)S(1)} %add_convert_fusion.2), channel_id=1, source_target_pairs={{0,8},{4,12},{8,0},{12,4},{16,24},{20,28},{24,16},{28,20},{1,9},{5... | collective-permute-start | bytes 393224 | tf_op jit(solution)/shard_map/ppermute | solution.py:393
  58.2 12.3 %collective-permute-start.15 = (bf16[384,128]{1,0:T(8,128)(2,1)S(1)}, bf16[384,128]{1,0:T(8,128)(2,1)S(1)}, u32[]{:S(2)}, u32[]{:S(2)}) collective-permute-start(bf16[384,128]{1,0:T(8,128)(2,1)S(1)} %get-tuple-element.109), channel_id=1, source_target_pairs={{0,24},{4,28},{8,16},{12,20},{16,8},{20,12},{24,0},{28,4},{1,25},{... | collective-permute-start | bytes 294920 | tf_op jit(solution)/shard_map/ppermute | solution.py:393
  60.5 17.4 %collective-permute-start.17 = (bf16[384,128]{1,0:T(8,128)(2,1)S(1)}, bf16[384,128]{1,0:T(8,128)(2,1)S(1)}, u32[]{:S(2)}, u32[]{:S(2)}) collective-permute-start(bf16[384,128]{1,0:T(8,128)(2,1)S(1)} %get-tuple-element.111), channel_id=1, source_target_pairs={{0,8},{4,12},{8,0},{12,4},{16,24},{20,28},{24,16},{28,20},{1,9},{5... | collective-permute-start | bytes 294920 | tf_op jit(solution)/shard_map/ppermute | solution.py:393
  63.0 14.9 %collective-permute-start.19 = (bf16[512,128]{1,0:T(8,128)(2,1)S(1)}, bf16[512,128]{1,0:T(8,128)(2,1)S(1)}, u32[]{:S(2)}, u32[]{:S(2)}) collective-permute-start(bf16[512,128]{1,0:T(8,128)(2,1)S(1)} %get-tuple-element.114), channel_id=1, source_target_pairs={{0,28},{4,24},{8,20},{12,16},{16,12},{20,8},{24,4},{28,0},{1,29},{... | collective-permute-start | bytes 393224 | tf_op jit(solution)/shard_map/ppermute | solution.py:393
  66.9 10.9 %collective-permute-start.14 = (bf16[512,128]{1,0:T(8,128)(2,1)S(1)}, bf16[512,128]{1,0:T(8,128)(2,1)S(1)}, u32[]{:S(2)}, u32[]{:S(2)}) collective-permute-start(bf16[512,128]{1,0:T(8,128)(2,1)S(1)} %add_convert_fusion.1), channel_id=1, source_target_pairs={{0,16},{4,20},{8,24},{12,28},{16,0},{20,4},{24,8},{28,12},{1,17},{... | collective-permute-start | bytes 393224 | tf_op jit(solution)/shard_map/ppermute | solution.py:393
  70.0 8.0 %collective-permute-start.18 = (bf16[512,128]{1,0:T(8,128)(2,1)S(1)}, bf16[512,128]{1,0:T(8,128)(2,1)S(1)}, u32[]{:S(2)}, u32[]{:S(2)}) collective-permute-start(bf16[512,128]{1,0:T(8,128)(2,1)S(1)} %get-tuple-element.112), channel_id=1, source_target_pairs={{0,12},{4,8},{8,4},{12,0},{16,28},{20,24},{24,20},{28,16},{1,13},{... | collective-permute-start | bytes 393224 | tf_op jit(solution)/shard_map/ppermute | solution.py:393
  70.5 7.4 %collective-permute-start.16 = (bf16[512,128]{1,0:T(8,128)(2,1)S(1)}, bf16[512,128]{1,0:T(8,128)(2,1)S(1)}, u32[]{:S(2)}, u32[]{:S(2)}) collective-permute-start(bf16[512,128]{1,0:T(8,128)(2,1)S(1)} %get-tuple-element.110), channel_id=1, source_target_pairs={{0,4},{4,0},{8,12},{12,8},{16,20},{20,16},{24,28},{28,24},{1,5},{5... | collective-permute-start | bytes 393224 | tf_op jit(solution)/shard_map/ppermute | solution.py:393

commit v6 on v5

--- a/solution.py
+++ b/solution.py
@@ -109,9 +109,11 @@
 
 def pack(heads, plan, refs):
     q_hbm, g_hbm, o_hbm, k_hbm, norm_hbm, owner_hbm, local_hbm = refs[:7]
-    scaled_ref, stats_ref, kt_ref, src_ref = refs[7:11]
+    scaled_ref, stats_ref, kt_ref, src_hbm = refs[7:11]
     out_refs = refs[11 : 11 + len(plan)]
-    q_ref, g_ref, o_ref, k_ref, norm_ref, owner_ref, local_ref, sems, count, source, place = refs[11 + len(plan) :]
+    q_ref, g_ref, o_ref, k_ref, norm_ref, owner_ref, local_ref, sems, count, source, place, src_ref = refs[
+        11 + len(plan) :
+    ]
     copies = [
         pltpu.make_async_copy(a, b, sems.at[n])
         for n, (a, b) in enumerate(
@@ -194,10 +196,13 @@
         if extra:
             marks.append(jnp.zeros((extra, BLOCK), F32))
         out[2 * total * BLOCK :, :] = jnp.concatenate(tiles + marks, axis=0).astype(BF16)
+    table = pltpu.make_async_copy(src_ref, src_hbm, sems.at[7])
+    table.start()
     copies[6].wait()
     for b in range(blocks):
         rows = pl.ds(b * BLOCK, BLOCK)
         kt_ref[rows, :] = (k_ref[rows, :].astype(F32) * (1.0 / math.sqrt(width))).T.astype(BF16)
+    table.wait()
 
 
 def window(heads, first, last, q_ref, g_ref, stats_ref, k_ref, v_ref, kt_ref, *rest):
@@ -369,20 +374,21 @@
             whole,
             jax.ShapeDtypeStruct((blocks, STAT, BLOCK), F32),
             whole,
-            jax.ShapeDtypeStruct((sum(slots),), jnp.int32),
+            pltpu.HBM((sum(slots),), jnp.int32),
         ]
         + [jax.ShapeDtypeStruct((message_rows(n), features), BF16) for n in slots],
-        [VMEM] * 3 + [SMEM] + [VMEM] * len(plan),
+        [VMEM] * 3 + [HBM] + [VMEM] * len(plan),
         [HBM] * 7,
         [pltpu.VMEM((tokens, features), BF16)] * 4
         + [
             pltpu.VMEM(log_norm.shape, F32),
             pltpu.SMEM(rand_owner.shape[::-1], jnp.int32),
             pltpu.SMEM(rand_local.shape[::-1], jnp.int32),
-            pltpu.SemaphoreType.DMA((7,)),
+            pltpu.SemaphoreType.DMA((8,)),
             pltpu.SMEM((owners,), jnp.int32),
             pltpu.SMEM((owners * capacity,), jnp.int32),
             pltpu.SMEM((owners * capacity,), jnp.int32),
+            pltpu.SMEM((sum(slots),), jnp.int32),
         ],
         "pack",
     )(*in_hbm(queries, d_outputs, outputs, keys, log_norm, rand_owner.T, rand_local.T))

time: 80.1 us -> 80.2 us (level)
  waiting for transfers between devices: 11.3 us -> 20.7 us
  starting transfers between devices: 46 us -> 37.5 us
    ppermute x20, waiting for transfers between devices: 11.3 us -> 20.7 us  [swap(): return lax.ppermute(array, 'seq', [(i, i ^ k) for i in range(owners)])]
    ppermute x20, starting transfers between devices: 46 us -> 37.5 us  [swap(): return lax.ppermute(array, 'seq', [(i, i ^ k) for i in range(owners)])]
  transfers between devices with their start and end apart: 20 -> 20, of which waited for: 5 -> 7; matrix products, arithmetic and copies ran while one was open for 0% -> 0% of each run, Pallas kernels for 23% -> 23%
where the time goes in v6:
time: 80.2 us
  starting transfers between devices  37.5 us (47%)
  Pallas kernels  20.9 us (26%)
  waiting for transfers between devices  20.7 us (26%)
  between operations  0.89 us (1%)
    ppermute x20, starting transfers between devices, swap(): return lax.ppermute(array, 'seq', [(i, i ^ k) for i in range(owners)])  37.5 us
    ppermute x20, waiting for transfers between devices, swap(): return lax.ppermute(array, 'seq', [(i, i ^ k) for i in range(owners)])  20.7 us
    pallas_call x7, Pallas kernels, owned(): call(lambda *refs: randoms(heads, counts, refs), shapes + [wide, wide], [...  8.06 us
    pallas_call x2, Pallas kernels, add_window(): call(functools.partial(window, heads, first, last), [wide] * 3, [VMEM] *...  5.51 us
    pallas_call x1, Pallas kernels, add_globals(): call(functools.partial(globals_, heads), [wide, jax.ShapeDtypeStruct(own....  2.54 us
    pallas_call x1, Pallas kernels, shards(): call(lambda *refs: pack(heads, plan, refs), [whole, jax.ShapeDtypeStruct(...  2.1 us
    pallas_call x1, Pallas kernels, shards(): call(lambda *refs: finish(ret_slots, refs), [whole] * 3, [HBM] * 3, [VMEM...  1.94 us
  transfers between devices with their start and end apart: 20, of which 7 were waited for; matrix products, arithmetic and copies ran while one was open for 0% of the time, Pallas kernels for 23%

profile of v6, /device:TPU:0, one launch (start us, length us, event | category | flops | bytes accessed | tf_op | source)
XLA Modules:
  0.0 80.2 jit_solution(17421196725108828255)
XLA Ops:
  0.6 0.7 pick_globals.1
  1.4 4.9 %collective-permute-start = (bf16[512,128]{1,0:T(8,128)(2,1)S(1)}, bf16[512,128]{1,0:T(8,128)(2,1)S(1)}, u32[]{:S(2)}, u32[]{:S(2)}) collective-permute-start(bf16[512,128]{1,0:T(8,128)(2,1)S(1)} %pick_globals.1), channel_id=1, source_target_pairs={{0,16},{4,20},{8,24},{12,28},{16,0},{20,4},{24,8},{28,12},{1,17},{... | collective-permute-start | bytes 393224 | tf_op jit(solution)/shard_map/ppermute | solution.py:399
  6.2 2.1 %pack.1 = (bf16[1024,128]{1,0:T(8,128)(2,1)S(1)}, f32[8,8,128]{2,1,0:T(8,128)S(1)}, bf16[1024,128]{1,0:T(8,128)(2,1)S(1)}, s32[27]{0:T(128)}, bf16[800,128]{1,0:...) custom-call(bf16[1024,128]{1,0:T(8,128)(2,1)} %refs_0_.1, ...), custom_call_target="tpu_custom_call" | custom-call | tf_op jit(solution)/shard_map/pack/pallas_call | solution.py:371
  8.4 0.0 copy-start
  8.4 0.1 collective-permute-start.2
  8.5 1.1 %collective-permute-start.9 = (bf16[1072,128]{1,0:T(8,128)(2,1)S(1)}, bf16[1072,128]{1,0:T(8,128)(2,1)S(1)}, u32[]{:S(2)}, u32[]{:S(2)}) collective-permute-start(bf16[1072,128]{1,0:T(8,128)(2,1)S(1)} %get-tuple-element.89), channel_id=1, source_target_pairs={{0,4},{4,0},{8,12},{12,8},{16,20},{20,16},{24,28},{28,24},{1,5},{5... | collective-permute-start | bytes 823304 | tf_op jit(solution)/shard_map/ppermute | solution.py:399
  9.5 8.3 %collective-permute-done = bf16[512,128]{1,0:T(8,128)(2,1)S(1)} collective-permute-done((bf16[512,128]{1,0:T(8,128)(2,1)S(1)}, bf16[512,128]{1,0:T(8,128)(2,1)S(1)}, u32[]{:S(2)}, u32[]{:S(2)}) %collective-permute-start) | collective-permute-done | bytes 131104 | tf_op jit(solution)/shard_map/ppermute | solution.py:399
  17.8 0.1 collective-permute-start.1
  17.9 3.5 %collective-permute-start.4 = (bf16[800,128]{1,0:T(8,128)(2,1)S(1)}, bf16[800,128]{1,0:T(8,128)(2,1)S(1)}, u32[]{:S(2)}, u32[]{:S(2)}) collective-permute-start(bf16[800,128]{1,0:T(8,128)(2,1)S(1)} %get-tuple-element.80), channel_id=1, source_target_pairs={{0,20},{4,16},{8,28},{12,24},{16,4},{20,0},{24,12},{28,8},{1,21},{... | collective-permute-start | bytes 614408 | tf_op jit(solution)/shard_map/ppermute | solution.py:399
  21.4 2.8 %window.2 = (f32[1024,128]{1,0:T(8,128)S(1)}, f32[1024,128]{1,0:T(8,128)S(1)}, f32[1024,128]{1,0:T(8,128)S(1)}) custom-call(bf16[1024,128]{1,0:T(8,128)(2,1)S(1)} %get-tuple-element.59.q_ref, bf16[1024,128]{1,0:T(8,128)(2,1)S(1)} %copy-done, f32[8,8,128]{2,1,0:T(8,128)S(1)} %get-tuple-element.64.stats_ref, bf16[1024,128]{1,0:T(8,128)(2,1)S(1)} %copy-done.1, ...), custom_call_target="tpu_custom_call" | custom-call | flops 3449999872 | tf_op jit(solution)/shard_map/window/pallas_call | solution.py:432
  24.2 2.8 %window.3 = (f32[1024,128]{1,0:T(8,128)S(1)}, f32[1024,128]{1,0:T(8,128)S(1)}, f32[1024,128]{1,0:T(8,128)S(1)}) custom-call(bf16[1024,128]{1,0:T(8,128)(2,1)S(1)} %get-tuple-element.59.q_ref, bf16[1024,128]{1,0:T(8,128)(2,1)S(1)} %copy-done, ...), custom_call_target="tpu_custom_call", output_to_operand_aliasing={{0}: (6, {}), {1}: (7, {}), {2}: (8, {})} | custom-call | flops 3449999872 | tf_op jit(solution)/shard_map/window/pallas_call | solution.py:432
  27.0 1.8 %collective-permute-start.6 = (bf16[1072,128]{1,0:T(8,128)(2,1)S(1)}, bf16[1072,128]{1,0:T(8,128)(2,1)S(1)}, u32[]{:S(2)}, u32[]{:S(2)}) collective-permute-start(bf16[1072,128]{1,0:T(8,128)(2,1)S(1)} %get-tuple-element.83), channel_id=1, source_target_pairs={{0,28},{4,24},{8,20},{12,16},{16,12},{20,8},{24,4},{28,0},{1,29},{... | collective-permute-start | bytes 823304 | tf_op jit(solution)/shard_map/ppermute | solution.py:399
  28.8 0.0 collective-permute-done.1
  28.9 0.9 %randoms.7 = (bf16[384,128]{1,0:T(8,128)(2,1)S(1)}, f32[1024,128]{1,0:T(8,128)S(1)}, f32[1024,128]{1,0:T(8,128)S(1)}) custom-call(bf16[800,128]{1,0:T(8,128)(2,1)S(1)} %collective-permute-done.2.refs_0_, bf16[1024,128]{1,0:T(8,128)(2,1)S(1)} %copy-done.1, bf16[1024,128]{1,0:T(8,128)(2,1)S(1)} %copy-done.2, ...), custom_call_target="tpu_custom_call", output_to_operand_aliasing={{1}: (4, {}), {2}: (5, {})} | custom-call | flops 3449999872 | tf_op jit(solution)/shard_map/randoms/pallas_call | solution.py:417
  29.8 0.9 %randoms.8 = (bf16[384,128]{1,0:T(8,128)(2,1)S(1)}, f32[1024,128]{1,0:T(8,128)S(1)}, f32[1024,128]{1,0:T(8,128)S(1)}) custom-call(bf16[800,128]{1,0:T(8,128)(2,1)S(1)} %get-tuple-element.61.refs_0_, bf16[1024,128]{1,0:T(8,128)(2,1)S(1)} %copy-done.1, bf16[1024,128]{1,0:T(8,128)(2,1)S(1)} %copy-done.2, ...), custom_call_target="tpu_custom_call", output_to_operand_aliasing={{1}: (4, {}), {2}: (5, {})} | custom-call | flops 3449999872 | tf_op jit(solution)/shard_map/randoms/pallas_call | solution.py:417
  30.8 0.6 collective-permute-start.11
  31.3 0.7 collective-permute-start.3
  32.1 10.0 %collective-permute-start.8 = (bf16[800,128]{1,0:T(8,128)(2,1)S(1)}, bf16[800,128]{1,0:T(8,128)(2,1)S(1)}, u32[]{:S(2)}, u32[]{:S(2)}) collective-permute-start(bf16[800,128]{1,0:T(8,128)(2,1)S(1)} %get-tuple-element.88), channel_id=1, source_target_pairs={{0,24},{4,28},{8,16},{12,20},{16,8},{20,12},{24,0},{28,4},{1,25},{... | collective-permute-start | bytes 614408 | tf_op jit(solution)/shard_map/ppermute | solution.py:399
  42.1 0.9 %randoms.9 = (bf16[384,128]{1,0:T(8,128)(2,1)S(1)}, f32[1024,128]{1,0:T(8,128)S(1)}, f32[1024,128]{1,0:T(8,128)S(1)}) custom-call(bf16[800,128]{1,0:T(8,128)(2,1)S(1)} %collective-permute-done.4.refs_0_, bf16[1024,128]{1,0:T(8,128)(2,1)S(1)} %copy-done.1, bf16[1024,128]{1,0:T(8,128)(2,1)S(1)} %copy-done.2, ...), custom_call_target="tpu_custom_call", output_to_operand_aliasing={{1}: (4, {}), {2}: (5, {})} | custom-call | flops 3449999872 | tf_op jit(solution)/shard_map/randoms/pallas_call | solution.py:417
  43.1 0.0 collective-permute-done.3
  43.1 0.1 collective-permute-start.7
  43.2 2.5 %globals.1 = (f32[1024,128]{1,0:T(8,128)S(1)}, bf16[512,128]{1,0:T(8,128)(2,1)S(1)}) custom-call(bf16[1024,128]{1,0:T(8,128)(2,1)S(1)} %get-tuple-element.59.q_ref, bf16[1024,128]{1,0:T(8,128)(2,1)S(1)} %copy-done, f32[8,8,128]{2,1,0:T(8,128)S(1)} %get-tuple-element.64.stats_ref, ...), custom_call_target="tpu_custom_call", output_to_operand_aliasing={{0}: (4, {})} | custom-call | tf_op jit(solution)/shard_map/globals/pallas_call | solution.py:402
  45.7 0.0 collective-permute-done.9.refs_0_
  45.8 1.6 %collective-permute-start.10 = (bf16[512,128]{1,0:T(8,128)(2,1)S(1)}, bf16[512,128]{1,0:T(8,128)(2,1)S(1)}, u32[]{:S(2)}, u32[]{:S(2)}) collective-permute-start(bf16[512,128]{1,0:T(8,128)(2,1)S(1)} %get-tuple-element.102), channel_id=1, source_target_pairs={{0,4},{4,0},{8,12},{12,8},{16,20},{20,16},{24,28},{28,24},{1,5},{5... | collective-permute-start | bytes 393224 | tf_op jit(solution)/shard_map/ppermute | solution.py:399
  47.4 1.2 %randoms.10 = (bf16[512,128]{1,0:T(8,128)(2,1)S(1)}, f32[1024,128]{1,0:T(8,128)S(1)}, f32[1024,128]{1,0:T(8,128)S(1)}) custom-call(bf16[1072,128]{1,0:T(8,128)(2,1)S(1)} %collective-permute-done.9.refs_0_, bf16[1024,128]{1,0:T(8,128)(2,1)S(1)} %copy-done.1, bf16[1024,128]{1,0:T(8,128)(2,1)S(1)} %copy-done.2, ...), custom_call_target="tpu_custom_call", output_to_operand_aliasing={{1}: (4, {}), {2}: (5, {})} | custom-call | flops 3449999872 | tf_op jit(solution)/shard_map/randoms/pallas_call | solution.py:417
  48.5 2.2 %collective-permute-done.10 = bf16[512,128]{1,0:T(8,128)(2,1)S(1)} collective-permute-done((bf16[512,128]{1,0:T(8,128)(2,1)S(1)}, bf16[512,128]{1,0:T(8,128)(2,1)S(1)}, u32[]{:S(2)}, u32[]{:S(2)}) %collective-permute-start.10) | collective-permute-done | bytes 131104 | tf_op jit(solution)/shard_map/ppermute | solution.py:399
  50.8 3.0 %collective-permute-start.5 = (bf16[1072,128]{1,0:T(8,128)(2,1)S(1)}, bf16[1072,128]{1,0:T(8,128)(2,1)S(1)}, u32[]{:S(2)}, u32[]{:S(2)}) collective-permute-start(bf16[1072,128]{1,0:T(8,128)(2,1)S(1)} %get-tuple-element.81), channel_id=1, source_target_pairs={{0,12},{4,8},{8,4},{12,0},{16,28},{20,24},{24,20},{28,16},{1,13},{... | collective-permute-start | bytes 823304 | tf_op jit(solution)/shard_map/ppermute | solution.py:399
  53.8 0.0 collective-permute-done.11.refs_10_
  53.8 0.1 collective-permute-start.13
  53.9 0.0 collective-permute-done.6.refs_0_
  53.9 1.5 %collective-permute-start.12 = (bf16[512,128]{1,0:T(8,128)(2,1)S(1)}, bf16[512,128]{1,0:T(8,128)(2,1)S(1)}, u32[]{:S(2)}, u32[]{:S(2)}) collective-permute-start(bf16[512,128]{1,0:T(8,128)(2,1)S(1)} %add_convert_fusion.2), channel_id=1, source_target_pairs={{0,8},{4,12},{8,0},{12,4},{16,24},{20,28},{24,16},{28,20},{1,9},{5... | collective-permute-start | bytes 393224 | tf_op jit(solution)/shard_map/ppermute | solution.py:399
  55.5 1.7 %randoms.11 = (bf16[384,128]{1,0:T(8,128)(2,1)S(1)}, bf16[384,128]{1,0:T(8,128)(2,1)S(1)}, f32[1024,128]{1,0:T(8,128)S(1)}, f32[1024,128]{1,0:T(8,128)S(1)}) custom-call(bf16[800,128]{1,0:T(8,128)(2,1)S(1)} %collective-permute-done.7.refs_0_, bf16[800,128]{1,0:T(8,128)(2,1)S(1)} %collective-permute-done.8.refs_1_, ...), custom_call_target="tpu_custom_call", output_to_operand_aliasing={{2}: (5, {}), {3}: (6, {})} | custom-call | flops 3449999872 | tf_op jit(solution)/shard_map/randoms/pallas_call | solution.py:417
  57.1 3.4 %collective-permute-start.15 = (bf16[384,128]{1,0:T(8,128)(2,1)S(1)}, bf16[384,128]{1,0:T(8,128)(2,1)S(1)}, u32[]{:S(2)}, u32[]{:S(2)}) collective-permute-start(bf16[384,128]{1,0:T(8,128)(2,1)S(1)} %get-tuple-element.109), channel_id=1, source_target_pairs={{0,24},{4,28},{8,16},{12,20},{16,8},{20,12},{24,0},{28,4},{1,25},{... | collective-permute-start | bytes 294920 | tf_op jit(solution)/shard_map/ppermute | solution.py:399
  60.5 0.0 collective-permute-start.17
  60.5 1.2 %randoms.12 = (bf16[512,128]{1,0:T(8,128)(2,1)S(1)}, f32[1024,128]{1,0:T(8,128)S(1)}, f32[1024,128]{1,0:T(8,128)S(1)}) custom-call(bf16[1072,128]{1,0:T(8,128)(2,1)S(1)} %collective-permute-done.6.refs_0_, bf16[1024,128]{1,0:T(8,128)(2,1)S(1)} %copy-done.1, bf16[1024,128]{1,0:T(8,128)(2,1)S(1)} %copy-done.2, ...), custom_call_target="tpu_custom_call", output_to_operand_aliasing={{1}: (4, {}), {2}: (5, {})} | custom-call | flops 3449999872 | tf_op jit(solution)/shard_map/randoms/pallas_call | solution.py:417
  61.7 0.8 collective-permute-done.13.refs_11_
  62.5 1.2 %collective-permute-start.19 = (bf16[512,128]{1,0:T(8,128)(2,1)S(1)}, bf16[512,128]{1,0:T(8,128)(2,1)S(1)}, u32[]{:S(2)}, u32[]{:S(2)}) collective-permute-start(bf16[512,128]{1,0:T(8,128)(2,1)S(1)} %get-tuple-element.114), channel_id=1, source_target_pairs={{0,28},{4,24},{8,20},{12,16},{16,12},{20,8},{24,4},{28,0},{1,29},{... | collective-permute-start | bytes 393224 | tf_op jit(solution)/shard_map/ppermute | solution.py:399
  63.7 5.6 %collective-permute-done.12 = bf16[512,128]{1,0:T(8,128)(2,1)S(1)} collective-permute-done((bf16[512,128]{1,0:T(8,128)(2,1)S(1)}, bf16[512,128]{1,0:T(8,128)(2,1)S(1)}, u32[]{:S(2)}, u32[]{:S(2)}) %collective-permute-start.12) | collective-permute-done | bytes 131104 | tf_op jit(solution)/shard_map/ppermute | solution.py:399
  69.3 0.1 collective-permute-start.14
  69.4 1.2 %randoms.13 = (bf16[512,128]{1,0:T(8,128)(2,1)S(1)}, f32[1024,128]{1,0:T(8,128)S(1)}, f32[1024,128]{1,0:T(8,128)S(1)}) custom-call(bf16[1072,128]{1,0:T(8,128)(2,1)S(1)} %collective-permute-done.5.refs_0_, bf16[1024,128]{1,0:T(8,128)(2,1)S(1)} %copy-done.1, bf16[1024,128]{1,0:T(8,128)(2,1)S(1)} %copy-done.2, ...), custom_call_target="tpu_custom_call", output_to_operand_aliasing={{1}: (4, {}), {2}: (5, {})} | custom-call | flops 3449999872 | tf_op jit(solution)/shard_map/randoms/pallas_call | solution.py:417
  70.6 0.1 collective-permute-start.18
  70.7 3.8 %collective-permute-start.16 = (bf16[512,128]{1,0:T(8,128)(2,1)S(1)}, bf16[512,128]{1,0:T(8,128)(2,1)S(1)}, u32[]{:S(2)}, u32[]{:S(2)}) collective-permute-start(bf16[512,128]{1,0:T(8,128)(2,1)S(1)} %get-tuple-element.110), channel_id=1, source_target_pairs={{0,4},{4,0},{8,12},{12,8},{16,20},{20,16},{24,28},{28,24},{1,5},{5... | collective-permute-start | bytes 393224 | tf_op jit(solution)/shard_map/ppermute | solution.py:399
  74.4 3.0 %collective-permute-done.14 = bf16[512,128]{1,0:T(8,128)(2,1)S(1)} collective-permute-done((bf16[512,128]{1,0:T(8,128)(2,1)S(1)}, bf16[512,128]{1,0:T(8,128)(2,1)S(1)}, u32[]{:S(2)}, u32[]{:S(2)}) %collective-permute-start.14) | collective-permute-done | bytes 131104 | tf_op jit(solution)/shard_map/ppermute | solution.py:399
  77.5 0.0 collective-permute-done.17.refs_8_
  77.5 0.0 collective-permute-done.19.refs_13_
  77.5 0.5 collective-permute-done.18.refs_9_
  78.0 0.3 collective-permute-done.16.refs_7_
  78.2 1.9 %finish.1 = (bf16[1024,128]{1,0:T(8,128)(2,1)}, bf16[1024,128]{1,0:T(8,128)(2,1)}, bf16[1024,128]{1,0:T(8,128)(2,1)}) custom-call(f32[1024,128]{1,0:T(8,128)S(1)} %get-tuple-element.77.refs_0_, f32[1024,128]{1,0:T(8,128)S(1)} %get-tuple-element.100.refs_1_, f32[1024,128]{1,0:T(8,128)S(1)} %get-tuple-element.101.refs_2_, ...), custom_call_target="tpu_custom_call" | custom-call | flops 3449999872 | tf_op jit(solution)/shard_map/finish/pallas_call | solution.py:519
  (17 shorter events, 0.3 us)
Async XLA Ops:
  1.4 16.4 %collective-permute-start = (bf16[512,128]{1,0:T(8,128)(2,1)S(1)}, bf16[512,128]{1,0:T(8,128)(2,1)S(1)}, u32[]{:S(2)}, u32[]{:S(2)}) collective-permute-start(bf16[512,128]{1,0:T(8,128)(2,1)S(1)} %pick_globals.1), channel_id=1, source_target_pairs={{0,16},{4,20},{8,24},{12,28},{16,0},{20,4},{24,8},{28,12},{1,17},{... | collective-permute-start | bytes 393224 | tf_op jit(solution)/shard_map/ppermute | solution.py:399
  6.2 15.2 %copy-start.1 = (bf16[1024,128]{1,0:T(8,128)(2,1)S(1)}, bf16[1024,128]{1,0:T(8,128)(2,1)}, u32[]{:S(2)}) copy-start(bf16[1024,128]{1,0:T(8,128)(2,1)} %refs_1_.13) | copy-start | bytes 786436
  6.2 15.2 %copy-start.2 = (bf16[1024,128]{1,0:T(8,128)(2,1)S(1)}, bf16[1024,128]{1,0:T(8,128)(2,1)}, u32[]{:S(2)}) copy-start(bf16[1024,128]{1,0:T(8,128)(2,1)} %refs_2_.15) | copy-start | bytes 786436
  8.4 13.1 %copy-start = (bf16[1024,128]{1,0:T(8,128)(2,1)S(1)}, bf16[1024,128]{1,0:T(8,128)(2,1)}, u32[]{:S(2)}) copy-start(bf16[1024,128]{1,0:T(8,128)(2,1)} %g_ref.5) | copy-start | bytes 786436
  8.4 18.6 %collective-permute-start.2 = (bf16[800,128]{1,0:T(8,128)(2,1)S(1)}, bf16[800,128]{1,0:T(8,128)(2,1)S(1)}, u32[]{:S(2)}, u32[]{:S(2)}) collective-permute-start(bf16[800,128]{1,0:T(8,128)(2,1)S(1)} %get-tuple-element.63), channel_id=1, source_target_pairs={{0,16},{4,20},{8,24},{12,28},{16,0},{20,4},{24,8},{28,12},{1,17},{... | collective-permute-start | bytes 614408 | tf_op jit(solution)/shard_map/ppermute | solution.py:399
  8.5 37.3 %collective-permute-start.9 = (bf16[1072,128]{1,0:T(8,128)(2,1)S(1)}, bf16[1072,128]{1,0:T(8,128)(2,1)S(1)}, u32[]{:S(2)}, u32[]{:S(2)}) collective-permute-start(bf16[1072,128]{1,0:T(8,128)(2,1)S(1)} %get-tuple-element.89), channel_id=1, source_target_pairs={{0,4},{4,0},{8,12},{12,8},{16,20},{20,16},{24,28},{28,24},{1,5},{5... | collective-permute-start | bytes 823304 | tf_op jit(solution)/shard_map/ppermute | solution.py:399
  17.8 11.0 %collective-permute-start.1 = (bf16[512,128]{1,0:T(8,128)(2,1)S(1)}, bf16[512,128]{1,0:T(8,128)(2,1)S(1)}, u32[]{:S(2)}, u32[]{:S(2)}) collective-permute-start(bf16[512,128]{1,0:T(8,128)(2,1)S(1)} %add.18), channel_id=1, source_target_pairs={{0,8},{4,12},{8,0},{12,4},{16,24},{20,28},{24,16},{28,20},{1,9},{5... | collective-permute-start | bytes 393224 | tf_op jit(solution)/shard_map/ppermute | solution.py:399
  17.9 14.1 %collective-permute-start.4 = (bf16[800,128]{1,0:T(8,128)(2,1)S(1)}, bf16[800,128]{1,0:T(8,128)(2,1)S(1)}, u32[]{:S(2)}, u32[]{:S(2)}) collective-permute-start(bf16[800,128]{1,0:T(8,128)(2,1)S(1)} %get-tuple-element.80), channel_id=1, source_target_pairs={{0,20},{4,16},{8,28},{12,24},{16,4},{20,0},{24,12},{28,8},{1,21},{... | collective-permute-start | bytes 614408 | tf_op jit(solution)/shard_map/ppermute | solution.py:399
  27.0 26.9 %collective-permute-start.6 = (bf16[1072,128]{1,0:T(8,128)(2,1)S(1)}, bf16[1072,128]{1,0:T(8,128)(2,1)S(1)}, u32[]{:S(2)}, u32[]{:S(2)}) collective-permute-start(bf16[1072,128]{1,0:T(8,128)(2,1)S(1)} %get-tuple-element.83), channel_id=1, source_target_pairs={{0,28},{4,24},{8,20},{12,16},{16,12},{20,8},{24,4},{28,0},{1,29},{... | collective-permute-start | bytes 823304 | tf_op jit(solution)/shard_map/ppermute | solution.py:399
  30.8 23.0 %collective-permute-start.11 = (bf16[384,128]{1,0:T(8,128)(2,1)S(1)}, bf16[384,128]{1,0:T(8,128)(2,1)S(1)}, u32[]{:S(2)}, u32[]{:S(2)}) collective-permute-start(bf16[384,128]{1,0:T(8,128)(2,1)S(1)} %get-tuple-element.87), channel_id=1, source_target_pairs={{0,16},{4,20},{8,24},{12,28},{16,0},{20,4},{24,8},{28,12},{1,17},{... | collective-permute-start | bytes 294920 | tf_op jit(solution)/shard_map/ppermute | solution.py:399
  31.3 11.7 %collective-permute-start.3 = (bf16[512,128]{1,0:T(8,128)(2,1)S(1)}, bf16[512,128]{1,0:T(8,128)(2,1)S(1)}, u32[]{:S(2)}, u32[]{:S(2)}) collective-permute-start(bf16[512,128]{1,0:T(8,128)(2,1)S(1)} %add.19), channel_id=1, source_target_pairs={{0,4},{4,0},{8,12},{12,8},{16,20},{20,16},{24,28},{28,24},{1,5},{5... | collective-permute-start | bytes 393224 | tf_op jit(solution)/shard_map/ppermute | solution.py:399
  32.1 21.8 %collective-permute-start.8 = (bf16[800,128]{1,0:T(8,128)(2,1)S(1)}, bf16[800,128]{1,0:T(8,128)(2,1)S(1)}, u32[]{:S(2)}, u32[]{:S(2)}) collective-permute-start(bf16[800,128]{1,0:T(8,128)(2,1)S(1)} %get-tuple-element.88), channel_id=1, source_target_pairs={{0,24},{4,28},{8,16},{12,20},{16,8},{20,12},{24,0},{28,4},{1,25},{... | collective-permute-start | bytes 614408 | tf_op jit(solution)/shard_map/ppermute | solution.py:399
  43.1 12.4 %collective-permute-start.7 = (bf16[800,128]{1,0:T(8,128)(2,1)S(1)}, bf16[800,128]{1,0:T(8,128)(2,1)S(1)}, u32[]{:S(2)}, u32[]{:S(2)}) collective-permute-start(bf16[800,128]{1,0:T(8,128)(2,1)S(1)} %get-tuple-element.85), channel_id=1, source_target_pairs={{0,8},{4,12},{8,0},{12,4},{16,24},{20,28},{24,16},{28,20},{1,9},{5... | collective-permute-start | bytes 614408 | tf_op jit(solution)/shard_map/ppermute | solution.py:399
  45.8 5.0 %collective-permute-start.10 = (bf16[512,128]{1,0:T(8,128)(2,1)S(1)}, bf16[512,128]{1,0:T(8,128)(2,1)S(1)}, u32[]{:S(2)}, u32[]{:S(2)}) collective-permute-start(bf16[512,128]{1,0:T(8,128)(2,1)S(1)} %get-tuple-element.102), channel_id=1, source_target_pairs={{0,4},{4,0},{8,12},{12,8},{16,20},{20,16},{24,28},{28,24},{1,5},{5... | collective-permute-start | bytes 393224 | tf_op jit(solution)/shard_map/ppermute | solution.py:399
  50.8 18.6 %collective-permute-start.5 = (bf16[1072,128]{1,0:T(8,128)(2,1)S(1)}, bf16[1072,128]{1,0:T(8,128)(2,1)S(1)}, u32[]{:S(2)}, u32[]{:S(2)}) collective-permute-start(bf16[1072,128]{1,0:T(8,128)(2,1)S(1)} %get-tuple-element.81), channel_id=1, source_target_pairs={{0,12},{4,8},{8,4},{12,0},{16,28},{20,24},{24,20},{28,16},{1,13},{... | collective-permute-start | bytes 823304 | tf_op jit(solution)/shard_map/ppermute | solution.py:399
  53.8 8.7 %collective-permute-start.13 = (bf16[384,128]{1,0:T(8,128)(2,1)S(1)}, bf16[384,128]{1,0:T(8,128)(2,1)S(1)}, u32[]{:S(2)}, u32[]{:S(2)}) collective-permute-start(bf16[384,128]{1,0:T(8,128)(2,1)S(1)} %get-tuple-element.104), channel_id=1, source_target_pairs={{0,20},{4,16},{8,28},{12,24},{16,4},{20,0},{24,12},{28,8},{1,21},{... | collective-permute-start | bytes 294920 | tf_op jit(solution)/shard_map/ppermute | solution.py:399
  53.9 15.3 %collective-permute-start.12 = (bf16[512,128]{1,0:T(8,128)(2,1)S(1)}, bf16[512,128]{1,0:T(8,128)(2,1)S(1)}, u32[]{:S(2)}, u32[]{:S(2)}) collective-permute-start(bf16[512,128]{1,0:T(8,128)(2,1)S(1)} %add_convert_fusion.2), channel_id=1, source_target_pairs={{0,8},{4,12},{8,0},{12,4},{16,24},{20,28},{24,16},{28,20},{1,9},{5... | collective-permute-start | bytes 393224 | tf_op jit(solution)/shard_map/ppermute | solution.py:399
  57.1 13.5 %collective-permute-start.15 = (bf16[384,128]{1,0:T(8,128)(2,1)S(1)}, bf16[384,128]{1,0:T(8,128)(2,1)S(1)}, u32[]{:S(2)}, u32[]{:S(2)}) collective-permute-start(bf16[384,128]{1,0:T(8,128)(2,1)S(1)} %get-tuple-element.109), channel_id=1, source_target_pairs={{0,24},{4,28},{8,16},{12,20},{16,8},{20,12},{24,0},{28,4},{1,25},{... | collective-permute-start | bytes 294920 | tf_op jit(solution)/shard_map/ppermute | solution.py:399
  60.5 17.0 %collective-permute-start.17 = (bf16[384,128]{1,0:T(8,128)(2,1)S(1)}, bf16[384,128]{1,0:T(8,128)(2,1)S(1)}, u32[]{:S(2)}, u32[]{:S(2)}) collective-permute-start(bf16[384,128]{1,0:T(8,128)(2,1)S(1)} %get-tuple-element.111), channel_id=1, source_target_pairs={{0,8},{4,12},{8,0},{12,4},{16,24},{20,28},{24,16},{28,20},{1,9},{5... | collective-permute-start | bytes 294920 | tf_op jit(solution)/shard_map/ppermute | solution.py:399
  62.5 15.0 %collective-permute-start.19 = (bf16[512,128]{1,0:T(8,128)(2,1)S(1)}, bf16[512,128]{1,0:T(8,128)(2,1)S(1)}, u32[]{:S(2)}, u32[]{:S(2)}) collective-permute-start(bf16[512,128]{1,0:T(8,128)(2,1)S(1)} %get-tuple-element.114), channel_id=1, source_target_pairs={{0,28},{4,24},{8,20},{12,16},{16,12},{20,8},{24,4},{28,0},{1,29},{... | collective-permute-start | bytes 393224 | tf_op jit(solution)/shard_map/ppermute | solution.py:399
  69.3 8.1 %collective-permute-start.14 = (bf16[512,128]{1,0:T(8,128)(2,1)S(1)}, bf16[512,128]{1,0:T(8,128)(2,1)S(1)}, u32[]{:S(2)}, u32[]{:S(2)}) collective-permute-start(bf16[512,128]{1,0:T(8,128)(2,1)S(1)} %add_convert_fusion.1), channel_id=1, source_target_pairs={{0,16},{4,20},{8,24},{12,28},{16,0},{20,4},{24,8},{28,12},{1,17},{... | collective-permute-start | bytes 393224 | tf_op jit(solution)/shard_map/ppermute | solution.py:399
  70.6 7.4 %collective-permute-start.18 = (bf16[512,128]{1,0:T(8,128)(2,1)S(1)}, bf16[512,128]{1,0:T(8,128)(2,1)S(1)}, u32[]{:S(2)}, u32[]{:S(2)}) collective-permute-start(bf16[512,128]{1,0:T(8,128)(2,1)S(1)} %get-tuple-element.112), channel_id=1, source_target_pairs={{0,12},{4,8},{8,4},{12,0},{16,28},{20,24},{24,20},{28,16},{1,13},{... | collective-permute-start | bytes 393224 | tf_op jit(solution)/shard_map/ppermute | solution.py:399
  70.7 7.6 %collective-permute-start.16 = (bf16[512,128]{1,0:T(8,128)(2,1)S(1)}, bf16[512,128]{1,0:T(8,128)(2,1)S(1)}, u32[]{:S(2)}, u32[]{:S(2)}) collective-permute-start(bf16[512,128]{1,0:T(8,128)(2,1)S(1)} %get-tuple-element.110), channel_id=1, source_target_pairs={{0,4},{4,0},{8,12},{12,8},{16,20},{20,16},{24,28},{28,24},{1,5},{5... | collective-permute-start | bytes 393224 | tf_op jit(solution)/shard_map/ppermute | solution.py:399
